TPU v7x, 32 devices: a whole 2x2x4 slice. The times are simulated.
32 devices in a mesh: dp: 2 (over core), seq: 16 (over z, y, x).
Axes of the slice: x: 2, y: 2, z: 4, core: 2. Of those that a mesh axis runs over, the one named last changes fastest.
Arguments:
- self_query: bfloat16 [2, 2048, 4096], P('dp', 'seq'), may hold values from -120 to 120
- self_key: bfloat16 [2, 2048, 4096], P('dp', 'seq'), may hold values from -6 to 6
- self_value: bfloat16 [2, 2048, 4096], P('dp', 'seq'), may hold values from -6 to 6
- cross_query: bfloat16 [2, 2048, 4096], P('dp', 'seq'), may hold values from -250 to 250
- text_embed: bfloat16 [2, 16, 512, 4096], P('dp', 'seq'), may hold values from -6 to 6
- cross_key_weight: bfloat16 [4096, 4096], P('dp', 'seq'), may hold values from -0.09375 to 0.09375
- cross_value_weight: bfloat16 [4096, 4096], P('dp', 'seq'), may hold values from -0.09375 to 0.09375
- text_lengths: int32 [2], P('dp'), may hold values from 64 to 512, as said below
- encoder_index: int32 [2], P('dp'), may hold values from 0 to 15
Outputs:
- attended: bfloat16 [2, 2048, 4096], P('dp', 'seq')
Inputs may be any that keep to these rules, and one draw needn't show every extreme that they name: `text_lengths`: one clip's prompt fills all 512 positions and another clip's holds 64.
All inputs are finite; a program needn't handle non-finite values.
Results may differ from a plain program's by a relative error of at most 0.011.
Values may be sent and summed in bfloat16 or wider, within the bound.
No kernel may reach another device: no remote copies, remote signals or barrier semaphores. Data moves between devices by JAX's collectives and lax.ppermute only.
A program may use at most 128 MiB of HBM per device.

v0:
```python
import jax
import jax.numpy as jnp
from jax import lax
from jax.sharding import PartitionSpec as P

HEAD = 128


def broadcast(value, axis, source):
    kept = jnp.where(lax.axis_index(axis) == source, value, 0).astype(value.dtype)
    return lax.psum(kept, axis)


def attend_all(queries, keys, values, bias):
    rows = queries.shape[0]
    block = min(512, rows)
    scale = 1.0 / queries.shape[2] ** 0.5

    def one_block(query_rows):
        scores = (
            jnp.einsum("qhe,khe->hqk", query_rows, keys, preferred_element_type=jnp.float32) * scale
            + bias
        )
        top = jnp.max(scores, axis=2, keepdims=True)
        probs = jnp.exp(scores - top)
        total = jnp.sum(probs, axis=2, keepdims=True)
        weights = (probs / total).astype(jnp.bfloat16)
        return jnp.einsum("hqk,khe->qhe", weights, values, preferred_element_type=jnp.float32)

    blocks = queries.reshape(rows // block, block, queries.shape[1], queries.shape[2])
    outputs = lax.map(one_block, blocks)
    return outputs.reshape(rows, queries.shape[1], queries.shape[2]).astype(jnp.bfloat16)


def split_heads(matrix):
    return matrix.reshape(matrix.shape[0], matrix.shape[1] // HEAD, HEAD)


def shards(
    self_query,
    self_key,
    self_value,
    cross_query,
    text_embed,
    cross_key_weight,
    cross_value_weight,
    text_lengths,
    encoder_index,
):
    prompt = broadcast(text_embed[0, 0], "seq", encoder_index[0])
    width_dev = cross_key_weight.shape[1]
    key_sum = jnp.dot(
        prompt,
        lax.all_gather(cross_key_weight, "dp", axis=0, tiled=True),
        preferred_element_type=jnp.float32,
    )
    value_sum = jnp.dot(
        prompt,
        lax.all_gather(cross_value_weight, "dp", axis=0, tiled=True),
        preferred_element_type=jnp.float32,
    )
    cross_key = key_sum.astype(jnp.bfloat16)
    cross_value = value_sum.astype(jnp.bfloat16)
    valid = jnp.arange(prompt.shape[0], dtype=jnp.int32) < text_lengths[0]
    bias = jnp.where(valid, jnp.float32(0.0), jnp.float32(-1e30))[None, None, :]
    head_query, head_key, head_value = (
        lax.all_to_all(self_query, "seq", split_axis=2, concat_axis=1, tiled=True),
        lax.all_to_all(self_key, "seq", split_axis=2, concat_axis=1, tiled=True),
        lax.all_to_all(self_value, "seq", split_axis=2, concat_axis=1, tiled=True),
    )
    self_out = attend_all(
        split_heads(head_query[0]),
        split_heads(head_key[0]),
        split_heads(head_value[0]),
        jnp.float32(0.0),
    )
    self_out = self_out.reshape(1, self_out.shape[0], width_dev)
    self_tokens = lax.all_to_all(self_out, "seq", split_axis=1, concat_axis=2, tiled=True)
    every_key, every_value = (
        lax.all_gather(cross_key, "seq", axis=1, tiled=True),
        lax.all_gather(cross_value, "seq", axis=1, tiled=True),
    )
    cross_out = attend_all(
        split_heads(cross_query[0]), split_heads(every_key), split_heads(every_value), bias
    )
    cross_out = cross_out.reshape(1, cross_out.shape[0], every_key.shape[1])
    return (self_tokens.astype(jnp.float32) + cross_out.astype(jnp.float32)).astype(jnp.bfloat16)


def solution(mesh):
    placed = (
        P("dp", "seq", None),
        P("dp", "seq", None),
        P("dp", "seq", None),
        P("dp", "seq", None),
        P("dp", "seq", None, None),
        P("dp", "seq"),
        P("dp", "seq"),
        P("dp"),
        P("dp"),
    )
    return jax.shard_map(
        shards, mesh=mesh, in_specs=placed, out_specs=P("dp", "seq", None), check_vma=False
    )
```

profile of v0, /device:TPU:0, one launch (start us, length us, event | category | flops | bytes accessed | tf_op | source)
XLA Modules:
  0.0 482.7 jit_solution(17623432804891382178)
XLA Ops:
  7.4 0.7 all-gather.9.cloned.1.call-update
  8.8 4.4 select_bitcast_fusion
  13.3 0.7 all-gather.5.cloned.1.call-update
  14.1 9.0 %all-gather.9.cloned.1.call-done = bf16[4096,256]{1,0:T(8,128)(2,1)} async-done(((bf16[2048,256]{1,0:T(8,128)(2,1)}), bf16[4096,256]{1,0:T(8,128)(2,1)}) %all-gather.9.cloned.1.call-update) | async-done | bytes 2097168 | tf_op jit(solution)/shard_map/all_gather | solution.py:54
  23.0 161.3 %all-reduce.2.cloned.1.call-done = bf16[512,4096]{1,0:T(8,128)(2,1)} async-done(((bf16[512,4096]{1,0:T(8,128)(2,1)}), bf16[512,4096]{1,0:T(8,128)(2,1)}) %all-reduce.2.cloned.1.call-update) | async-done | bytes 4194320 | tf_op jit(solution)/shard_map/psum | solution.py:11
  184.3 4.8 convolution_convert_fusion
  189.2 2.8 copy.58
  192.0 0.5 broadcast.45
  192.5 22.3 %reduce = bf16[4096,128]{1,0:T(8,128)(2,1)S(1)} reduce(bf16[4096,1,128]{2,1,0:T(2,128)(2,1)S(1)} %bitcast.105, bf16[]{:T(256)} %broadcast.45), dimensions={1}, to_apply=%bitcast.66.reduce_sub_computation | reduce | bytes 2097154
  214.8 1.1 reshape.86
  215.9 4.7 all-to-all-start
  220.6 5.0 %copy.60 = bf16[1,128,4096]{1,0,2:T(2,128)(2,1)S(1)} copy(bf16[1,128,4096]{2,1,0:T(8,128)(2,1)} %param.12) | data formatting | bytes 2097152 | tf_op args[1]
  225.6 23.3 %reduce.1 = bf16[4096,128]{1,0:T(8,128)(2,1)} reduce(bf16[4096,1,128]{2,1,0:T(2,128)(2,1)S(1)} %bitcast.107, bf16[]{:T(256)} %broadcast.45), dimensions={1}, to_apply=%bitcast.68.reduce_sub_computation | reduce | bytes 2097154
  248.9 2.2 reshape.88
  251.1 21.1 %all-to-all-start.1 = ((bf16[16,2,16384]{2,1,0:T(2,128)(2,1)}), bf16[16,2,16384]{2,1,0:T(2,128)(2,1)}, u32[]{:S(2)}, u32[]{:S(2)}) async-start(bf16[16,2,16384]{2,1,0:T(2,128)(2,1)} %reshape.88), calls=%async_computation.1 | async-start | bytes 2097152 | tf_op jit(solution)/shard_map/all_to_all | solution.py:68
  272.2 5.0 %copy.62 = bf16[1,128,4096]{1,0,2:T(2,128)(2,1)S(1)} copy(bf16[1,128,4096]{2,1,0:T(8,128)(2,1)} %param.13) | data formatting | bytes 2097152 | tf_op args[2]
  277.2 23.3 %reduce.2 = bf16[4096,128]{1,0:T(8,128)(2,1)} reduce(bf16[4096,1,128]{2,1,0:T(2,128)(2,1)S(1)} %bitcast.108, bf16[]{:T(256)} %broadcast.45), dimensions={1}, to_apply=%bitcast.70.reduce_sub_computation | reduce | bytes 2097154
  300.5 2.2 reshape.90
  302.7 1.1 all-to-all-done.1
  303.8 9.2 %all-to-all-start.2 = ((bf16[16,2,16384]{2,1,0:T(2,128)(2,1)}), bf16[16,2,16384]{2,1,0:T(2,128)(2,1)}, u32[]{:S(2)}, u32[]{:S(2)}) async-start(bf16[16,2,16384]{2,1,0:T(2,128)(2,1)} %reshape.90), calls=%async_computation.2 | async-start | bytes 2097152 | tf_op jit(solution)/shard_map/all_to_all | solution.py:69
  313.0 0.3 all-gather.7.cloned.1.call-start
  313.3 1.1 reshape.87
  314.5 0.5 copy.59
  315.0 0.3 reshape_reshape_squeeze.4
  315.3 4.3 reshape.89
  319.8 0.7 copy.61
  320.5 0.5 reshape_squeeze.6
  321.0 1.3 copy.65
  322.3 12.6 %all-to-all-done.2 = bf16[16,2,16384]{2,1,0:T(2,128)(2,1)} async-done(((bf16[16,2,16384]{2,1,0:T(2,128)(2,1)}), bf16[16,2,16384]{2,1,0:T(2,128)(2,1)}, u32[]{:S(2)}, u32[]{:S(2)}) %all-to-all-start.2) | async-done | bytes 1048608 | tf_op jit(solution)/shard_map/all_to_all | solution.py:69
  334.9 4.3 reshape.91
  339.3 0.7 copy.63
  340.0 0.5 reshape_squeeze.7
  340.5 1.3 copy.66
  341.8 4.9 %convolution_convert_fusion.1 = bf16[512,256]{1,0:T(8,128)(2,1)} fusion(bf16[512,4096]{1,0:T(8,128)(2,1)} %all-reduce.2.cloned.1.call-done, bf16[4096,256]{1,0:T(8,128)(2,1)} %all-gather.5.cloned.1.call-done), kind=kOutput, calls=%fused_computation.34 | convolution fusion | flops 1073872896 | bytes 6553600 | tf_op jit(solution)/shard_map/dot_general | solution.py:57
  346.8 42.6 %while.2 = (s32[]{:T(128)}, bf16[4,512,2,128]{3,1,2,0:T(8,128)(2,1)}, bf16[4,512,2,128]{3,2,1,0:T(2,128)(2,1)S(1)}, bf16[2048,2,128]{2,0,1:T(8,128)(2,1)S(1)}, bf16[2048,2,128]{2,0,1:T(8,128)(2,1)S(1)}, /*index=5*/s32[]{:T(128)}) while((s32[]{:T(128)}, bf16[4,512,2,128]{3,1,2,0:T(8,128)(2,1)}, bf16[4,512,2,128]{3,2,1,0:T(2,128)(2,1)S(1)}, ...), condition=%wide.region_3.4_spmd, body=%wide.region_0.3_spmd.sunk | while | flops 1084229632 | bytes 20193364 | solution.py:31
  346.9 0.2 constant_dynamic-slice_fusion.2
  347.0 5.0 %fusion.46 = (f32[2,512]{1,0:T(2,128)S(1)}, f32[2,512,2048]{2,1,0:T(8,128)}) fusion(bf16[2048,2,128]{2,0,1:T(8,128)(2,1)S(1)} %get-tuple-element.135, bf16[1,512,2,128]{3,2,1,0:T(2,128)(2,1)S(1)} %constant_dynamic-slice_fusion.2), kind=kOutput, calls=%fused_computation.39.clone.1 | convolution fusion | flops 543164416 | bytes 9703424 | tf_op jit(solution)/shard_map/while/body/eval_jaxpr/sub | solution.py:25
  352.1 5.6 %fusion.47 = bf16[4,512,2,128]{3,1,2,0:T(8,128)(2,1)} fusion(bf16[4,512,2,128]{3,1,2,0:T(8,128)(2,1)} %get-tuple-element.127, s32[]{:T(128)S(6)} %copy.107, bf16[2048,2,128]{2,0,1:T(8,128)(2,1)S(1)} %get-tuple-element.136, f32[2,512,2048]{2,1,0:T(8,128)} %get-tuple-element.118, f32[2,512]{1,0:T(2,128)S(1)} %get-tuple-element.119), kind=kOutput, calls=%fused_computation.8.clone.1 | convolution fusion | flops 541065216 | bytes 9965572 | tf_op jit(solution)/shard_map/while/body/eval_jaxpr/hqk,khe->qhe/dot_general | solution.py:28
  357.7 0.2 constant_dynamic-slice_fusion.2
  357.8 5.0 %fusion.46 = (f32[2,512]{1,0:T(2,128)S(1)}, f32[2,512,2048]{2,1,0:T(8,128)}) fusion(bf16[2048,2,128]{2,0,1:T(8,128)(2,1)S(1)} %get-tuple-element.135, bf16[1,512,2,128]{3,2,1,0:T(2,128)(2,1)S(1)} %constant_dynamic-slice_fusion.2), kind=kOutput, calls=%fused_computation.39.clone.1 | convolution fusion | flops 543164416 | bytes 9703424 | tf_op jit(solution)/shard_map/while/body/eval_jaxpr/sub | solution.py:25
  362.9 5.4 %fusion.47 = bf16[4,512,2,128]{3,1,2,0:T(8,128)(2,1)} fusion(bf16[4,512,2,128]{3,1,2,0:T(8,128)(2,1)} %get-tuple-element.127, s32[]{:T(128)S(6)} %copy.107, bf16[2048,2,128]{2,0,1:T(8,128)(2,1)S(1)} %get-tuple-element.136, f32[2,512,2048]{2,1,0:T(8,128)} %get-tuple-element.118, f32[2,512]{1,0:T(2,128)S(1)} %get-tuple-element.119), kind=kOutput, calls=%fused_computation.8.clone.1 | convolution fusion | flops 541065216 | bytes 9965572 | tf_op jit(solution)/shard_map/while/body/eval_jaxpr/hqk,khe->qhe/dot_general | solution.py:28
  368.2 0.2 constant_dynamic-slice_fusion.2
  368.4 5.0 %fusion.46 = (f32[2,512]{1,0:T(2,128)S(1)}, f32[2,512,2048]{2,1,0:T(8,128)}) fusion(bf16[2048,2,128]{2,0,1:T(8,128)(2,1)S(1)} %get-tuple-element.135, bf16[1,512,2,128]{3,2,1,0:T(2,128)(2,1)S(1)} %constant_dynamic-slice_fusion.2), kind=kOutput, calls=%fused_computation.39.clone.1 | convolution fusion | flops 543164416 | bytes 9703424 | tf_op jit(solution)/shard_map/while/body/eval_jaxpr/sub | solution.py:25
  373.5 5.4 %fusion.47 = bf16[4,512,2,128]{3,1,2,0:T(8,128)(2,1)} fusion(bf16[4,512,2,128]{3,1,2,0:T(8,128)(2,1)} %get-tuple-element.127, s32[]{:T(128)S(6)} %copy.107, bf16[2048,2,128]{2,0,1:T(8,128)(2,1)S(1)} %get-tuple-element.136, f32[2,512,2048]{2,1,0:T(8,128)} %get-tuple-element.118, f32[2,512]{1,0:T(2,128)S(1)} %get-tuple-element.119), kind=kOutput, calls=%fused_computation.8.clone.1 | convolution fusion | flops 541065216 | bytes 9965572 | tf_op jit(solution)/shard_map/while/body/eval_jaxpr/hqk,khe->qhe/dot_general | solution.py:28
  378.9 0.2 constant_dynamic-slice_fusion.2
  379.1 5.0 %fusion.46 = (f32[2,512]{1,0:T(2,128)S(1)}, f32[2,512,2048]{2,1,0:T(8,128)}) fusion(bf16[2048,2,128]{2,0,1:T(8,128)(2,1)S(1)} %get-tuple-element.135, bf16[1,512,2,128]{3,2,1,0:T(2,128)(2,1)S(1)} %constant_dynamic-slice_fusion.2), kind=kOutput, calls=%fused_computation.39.clone.1 | convolution fusion | flops 543164416 | bytes 9703424 | tf_op jit(solution)/shard_map/while/body/eval_jaxpr/sub | solution.py:25
  384.1 5.4 %fusion.47 = bf16[4,512,2,128]{3,1,2,0:T(8,128)(2,1)} fusion(bf16[4,512,2,128]{3,1,2,0:T(8,128)(2,1)} %get-tuple-element.127, s32[]{:T(128)S(6)} %copy.107, bf16[2048,2,128]{2,0,1:T(8,128)(2,1)S(1)} %get-tuple-element.136, f32[2,512,2048]{2,1,0:T(8,128)} %get-tuple-element.118, f32[2,512]{1,0:T(2,128)S(1)} %get-tuple-element.119), kind=kOutput, calls=%fused_computation.8.clone.1 | convolution fusion | flops 541065216 | bytes 9965572 | tf_op jit(solution)/shard_map/while/body/eval_jaxpr/hqk,khe->qhe/dot_general | solution.py:28
  389.5 2.3 copy.67
  391.8 0.5 convert_element_type.108
  392.3 10.5 %reduce.3 = bf16[2048,256]{1,0:T(8,128)(2,1)S(1)} reduce(bf16[2048,1,256]{2,1,0:T(2,128)(2,1)S(1)} %bitcast.106, bf16[]{:T(256)} %broadcast.45), dimensions={1}, to_apply=%bitcast.72.reduce_sub_computation | reduce | bytes 2097154
  402.8 1.1 reshape.92
  403.9 4.9 %all-to-all-start.3 = ((bf16[16,2,16384]{2,1,0:T(2,128)(2,1)}), bf16[16,2,16384]{2,1,0:T(2,128)(2,1)S(1)}, u32[]{:S(2)}, u32[]{:S(2)}) async-start(bf16[16,2,16384]{2,1,0:T(2,128)(2,1)} %reshape.92), calls=%async_computation.3 | async-start | bytes 2097152 | tf_op jit(solution)/shard_map/all_to_all | solution.py:78
  408.9 1.2 copy.83
  410.7 38.1 %all-to-all-done.3 = bf16[16,2,16384]{2,1,0:T(2,128)(2,1)S(1)} async-done(((bf16[16,2,16384]{2,1,0:T(2,128)(2,1)}), bf16[16,2,16384]{2,1,0:T(2,128)(2,1)S(1)}, u32[]{:S(2)}, u32[]{:S(2)}) %all-to-all-start.3) | async-done | bytes 1048608 | tf_op jit(solution)/shard_map/all_to_all | solution.py:78
  448.8 1.0 reshape.93
  449.8 0.2 copy.69
  450.0 1.5 convert_bitcast_fusion
  451.6 1.9 copy.70
  453.5 3.5 fusion.17
  457.0 4.6 fusion.30
  461.6 6.5 %copy.77 = bf16[512,4096]{0,1:T(8,128)(2,1)} copy(bf16[512,4096]{1,0:T(8,128)(2,1)} %all-gather.7.cloned.1.call-done) | data formatting | bytes 8388608 | tf_op jit(solution)/shard_map/reshape | solution.py:36
  468.1 5.9 %fusion.25 = f32[32,128,128]{2,1,0:T(8,128)S(1)} fusion(bf16[512,32,128]{0,2,1:T(8,128)(2,1)} %bitcast.113, f32[32,128,512]{1,2,0:T(8,128)} %get-tuple-element.84, f32[32,128]{1,0:T(8,128)S(1)} %get-tuple-element.83), kind=kOutput, calls=%fused_computation.32 | convolution fusion | flops 542113792 | bytes 14696448 | tf_op jit(solution)/shard_map/while/body/eval_jaxpr/hqk,khe->qhe/dot_general | solution.py:28
  474.0 0.3 fusion.23
  474.3 1.3 copy.75
  (26 shorter events, 0.6 us)
Async XLA Ops:
  7.4 15.7 %all-gather.9.cloned.1.call-start = ((), (), s32[]{:S(2)}) async-start(), calls=%async_computation.7 | async-start | bytes 3145728 | tf_op jit(solution)/shard_map/all_gather | solution.py:54
  8.1 176.2 %all-reduce.2.cloned.1.call-start = ((), (), s32[]{:S(2)}) async-start(), calls=%async_computation.4 | async-start | bytes 8388608 | tf_op jit(solution)/shard_map/psum | solution.py:11
  13.2 328.6 %all-gather.5.cloned.1.call-start = ((), (), s32[]{:S(2)}) async-start(), calls=%async_computation.5 | async-start | bytes 3145728 | tf_op jit(solution)/shard_map/all_gather | solution.py:59
  14.0 175.2 %copy-start.1 = (bf16[1,128,4096]{2,1,0:T(8,128)(2,1)S(1)}, bf16[1,128,4096]{2,1,0:T(8,128)(2,1)}, u32[]{:S(2)}) copy-start(bf16[1,128,4096]{2,1,0:T(8,128)(2,1)} %param.11) | copy-start | bytes 3145732
  14.0 439.5 %all-gather.11.cloned.1.call-start = ((), (), s32[]{:S(2)}) async-start(), calls=%async_computation.8 | async-start | bytes 4456448 | tf_op jit(solution)/shard_map/all_gather | solution.py:80
  215.9 35.2 %all-to-all-start = ((bf16[16,2,16384]{2,1,0:T(2,128)(2,1)}), bf16[16,2,16384]{2,1,0:T(2,128)(2,1)S(1)}, u32[]{:S(2)}, u32[]{:S(2)}) async-start(bf16[16,2,16384]{2,1,0:T(2,128)(2,1)} %reshape.86), calls=%async_computation | async-start | bytes 2097152 | tf_op jit(solution)/shard_map/all_to_all | solution.py:67
  251.1 52.7 %all-to-all-start.1 = ((bf16[16,2,16384]{2,1,0:T(2,128)(2,1)}), bf16[16,2,16384]{2,1,0:T(2,128)(2,1)}, u32[]{:S(2)}, u32[]{:S(2)}) async-start(bf16[16,2,16384]{2,1,0:T(2,128)(2,1)} %reshape.88), calls=%async_computation.1 | async-start | bytes 2097152 | tf_op jit(solution)/shard_map/all_to_all | solution.py:68
  303.8 31.1 %all-to-all-start.2 = ((bf16[16,2,16384]{2,1,0:T(2,128)(2,1)}), bf16[16,2,16384]{2,1,0:T(2,128)(2,1)}, u32[]{:S(2)}, u32[]{:S(2)}) async-start(bf16[16,2,16384]{2,1,0:T(2,128)(2,1)} %reshape.90), calls=%async_computation.2 | async-start | bytes 2097152 | tf_op jit(solution)/shard_map/all_to_all | solution.py:69
  313.0 148.7 %all-gather.7.cloned.1.call-start = ((), (), s32[]{:S(2)}) async-start(), calls=%async_computation.6 | async-start | bytes 4456448 | tf_op jit(solution)/shard_map/all_gather | solution.py:81
  341.8 5.0 %copy-start.3 = (bf16[2048,2,128]{2,0,1:T(8,128)(2,1)S(1)}, bf16[2048,2,128]{2,0,1:T(8,128)(2,1)}, u32[]{:S(2)}) copy-start(bf16[2048,2,128]{2,0,1:T(8,128)(2,1)} %copy.65) | copy-start | bytes 3145732
  341.8 5.0 %copy-start.4 = (bf16[2048,2,128]{2,0,1:T(8,128)(2,1)S(1)}, bf16[2048,2,128]{2,0,1:T(8,128)(2,1)}, u32[]{:S(2)}) copy-start(bf16[2048,2,128]{2,0,1:T(8,128)(2,1)} %copy.66) | copy-start | bytes 3145732
  402.8 6.0 %copy-start.2 = (bf16[1,128,4096]{2,1,0:T(8,128)(2,1)S(1)}, bf16[1,128,4096]{2,1,0:T(8,128)(2,1)}, u32[]{:S(2)}) copy-start(bf16[1,128,4096]{2,1,0:T(8,128)(2,1)} %param.14) | copy-start | bytes 3145732
  403.9 44.9 %all-to-all-start.3 = ((bf16[16,2,16384]{2,1,0:T(2,128)(2,1)}), bf16[16,2,16384]{2,1,0:T(2,128)(2,1)S(1)}, u32[]{:S(2)}, u32[]{:S(2)}) async-start(bf16[16,2,16384]{2,1,0:T(2,128)(2,1)} %reshape.92), calls=%async_computation.3 | async-start | bytes 2097152 | tf_op jit(solution)/shard_map/all_to_all | solution.py:78
  450.0 3.5 copy-start
Sparse Core Ops, SparseCore 0:
  9.7 13.2 all-gather.8
  24.6 11.7 all-gather.4
  189.3 118.8 all-gather.10
  346.9 107.8 all-gather.6
Sparse Core Ops, SparseCore 1:
  14.2 170.1 all-reduce.1
where the time goes:
time: 488 us; the launch traced here: 483 us
  waiting for transfers between devices  224 us (46%)
  other arithmetic  90.3 us (19%)
  matrix products  61 us (12%)
  local copies, waits for them, and re-layouts  51.5 us (11%)
  starting transfers between devices  40.2 us (8%)
  between operations  16.2 us (3%)
    psum x1, waiting for transfers between devices, broadcast(): return lax.psum(kept, axis)  161 us
    unnamed x4, other arithmetic  79.4 us
    all_to_all x1, waiting for transfers between devices, shards(): lax.all_to_all(self_out, 'seq', split_axis=1, concat_axis=2, tiled=True)  38.1 us
    unnamed x26, local copies, waits for them, and re-layouts  32.3 us
    dot_general x5, matrix products, one_block(): jnp.einsum('hqk,khe->qhe', weights, values, preferred_element_type=jnp.fl...  27.7 us
    all_to_all x1, starting transfers between devices, shards(): lax.all_to_all(self_key, 'seq', split_axis=2, concat_axis=1, tiled=True)  21.1 us
    sub x4, matrix products, one_block(): probs = jnp.exp(scores - top)  20.1 us
    all_to_all x1, waiting for transfers between devices, shards(): lax.all_to_all(self_value, 'seq', split_axis=2, concat_axis=1, tiled=True)  12.6 us
  transfers between devices with their start and end apart: 9, of which 5 were waited for; matrix products, arithmetic and copies ran while one was open for 39% of the time, Pallas kernels for 0%

commit v1 on v0

v1 whole, which is shorter than its diff:
```python
import functools
import math

import jax
import jax.numpy as jnp
from jax import lax
from jax.experimental import pallas as pl
from jax.experimental.pallas import tpu as pltpu
from jax.sharding import PartitionSpec as P

HEAD = 128
VMEM_BYTES = 48 * 1024 * 1024
LOG2E = math.log2(math.e)


def params():
    return pltpu.CompilerParams(vmem_limit_bytes=VMEM_BYTES)


def pack(arrays, n):
    rows, columns = arrays[0].shape
    width = columns // n
    per = max(1, n // 4)
    count = len(arrays)

    def body(*refs):
        out_ref = refs[-1]
        for a in range(count):
            for j in range(per):
                out_ref[j, a] = refs[a][:, j * width : (j + 1) * width]

    return pl.pallas_call(
        body,
        grid=(n // per,),
        in_specs=[pl.BlockSpec((rows, per * width), lambda i: (0, i))] * count,
        out_specs=pl.BlockSpec((per, count, rows, width), lambda i: (i, 0, 0, 0)),
        out_shape=jax.ShapeDtypeStruct((n, count, rows, width), arrays[0].dtype),
        compiler_params=params(),
        name="pack",
    )(*arrays)


def unpack(blocks):
    n, rows, width = blocks.shape
    per = max(1, n // 4)

    def body(in_ref, out_ref):
        for j in range(per):
            out_ref[:, j * width : (j + 1) * width] = in_ref[j]

    return pl.pallas_call(
        body,
        grid=(n // per,),
        in_specs=[pl.BlockSpec((per, rows, width), lambda i: (i, 0, 0))],
        out_specs=pl.BlockSpec((rows, per * width), lambda i: (0, i)),
        out_shape=jax.ShapeDtypeStruct((rows, n * width), blocks.dtype),
        compiler_params=params(),
        name="unpack",
    )(blocks)


def self_attention(blocks):
    n, _, rows, width = blocks.shape
    heads = width // HEAD
    tokens = n * rows
    per = max(1, min(n, 256 // rows))
    step = 2 * per if n % (2 * per) == 0 else per
    factor = LOG2E / HEAD**0.5

    def body(q_ref, k_ref, v_ref, out_ref, values):
        @pl.when(pl.program_id(1) == 0)
        def _():
            values[:, :HEAD] = v_ref[:, 0].reshape(tokens, HEAD)
            values[:, HEAD:] = jnp.ones((tokens, HEAD), jnp.bfloat16)

        keys = k_ref[:, 0].reshape(tokens, HEAD)
        for part in range(step // per):
            q = q_ref[part * per : (part + 1) * per, 0].reshape(per * rows, HEAD)
            scores = lax.dot_general(
                q, keys, (((1,), (1,)), ((), ())), preferred_element_type=jnp.float32
            )
            top = jnp.max(scores, axis=1, keepdims=True)
            probs = jnp.exp2((scores - top) * factor).astype(jnp.bfloat16)
            total = jnp.dot(probs, values[...], preferred_element_type=jnp.float32)
            out = (total[:, :HEAD] / total[:, HEAD:]).astype(jnp.bfloat16)
            out_ref[part * per : (part + 1) * per] = out.reshape(per, rows, HEAD)

    return pl.pallas_call(
        body,
        grid=(heads, n // step),
        in_specs=[
            pl.BlockSpec((step, 1, rows, HEAD), lambda h, i: (i, 0, 0, h)),
            pl.BlockSpec((n, 1, rows, HEAD), lambda h, i: (0, 1, 0, h)),
            pl.BlockSpec((n, 1, rows, HEAD), lambda h, i: (0, 2, 0, h)),
        ],
        out_specs=pl.BlockSpec((step, rows, HEAD), lambda h, i: (i, 0, h)),
        out_shape=jax.ShapeDtypeStruct((n, rows, width), jnp.bfloat16),
        scratch_shapes=[pltpu.VMEM((tokens, 2 * HEAD), jnp.bfloat16)],
        compiler_params=params(),
        cost_estimate=pl.CostEstimate(
            flops=4 * heads * tokens * tokens * HEAD,
            bytes_accessed=2 * 4 * tokens * width,
            transcendentals=heads * tokens * tokens,
        ),
        name="self_attention",
    )(blocks, blocks, blocks)


def cross_attention(queries, text, length, self_out):
    n, rows, width = queries.shape
    heads = width // HEAD
    positions = text.shape[0]
    step = max(1, min(n, 512 // rows))
    factor = LOG2E / HEAD**0.5

    def body(length_ref, q_ref, k_ref, v_ref, self_ref, out_ref, values):
        @pl.when(pl.program_id(1) == 0)
        def _():
            values[:, :HEAD] = v_ref[...]
            values[:, HEAD:] = jnp.ones((positions, HEAD), jnp.bfloat16)

        q = q_ref[...].reshape(step * rows, HEAD)
        scores = lax.dot_general(
            q, k_ref[...], (((1,), (1,)), ((), ())), preferred_element_type=jnp.float32
        )
        place = lax.broadcasted_iota(jnp.int32, (1, positions), 1)
        scores = jnp.where(place < length_ref[0], scores, -1e30)
        top = jnp.max(scores, axis=1, keepdims=True)
        probs = jnp.exp2((scores - top) * factor).astype(jnp.bfloat16)
        total = jnp.dot(probs, values[...], preferred_element_type=jnp.float32)
        out = (total[:, :HEAD] / total[:, HEAD:]).astype(jnp.bfloat16).astype(jnp.float32)
        out = out.reshape(step, rows, HEAD) + self_ref[...].astype(jnp.float32)
        out_ref[...] = out.astype(jnp.bfloat16)

    return pl.pallas_call(
        body,
        grid_spec=pltpu.PrefetchScalarGridSpec(
            num_scalar_prefetch=1,
            grid=(heads, n // step),
            in_specs=[
                pl.BlockSpec((step, rows, HEAD), lambda h, i, _: (i, 0, h)),
                pl.BlockSpec((positions, HEAD), lambda h, i, _: (0, h)),
                pl.BlockSpec((positions, HEAD), lambda h, i, _: (0, heads + h)),
                pl.BlockSpec((step, rows, HEAD), lambda h, i, _: (i, 0, h)),
            ],
            out_specs=pl.BlockSpec((step, rows, HEAD), lambda h, i, _: (i, 0, h)),
            scratch_shapes=[pltpu.VMEM((positions, 2 * HEAD), jnp.bfloat16)],
        ),
        out_shape=jax.ShapeDtypeStruct((n, rows, width), jnp.bfloat16),
        compiler_params=params(),
        cost_estimate=pl.CostEstimate(
            flops=4 * heads * n * rows * positions * HEAD,
            bytes_accessed=2 * 3 * n * rows * width,
            transcendentals=heads * n * rows * positions,
        ),
        name="cross_attention",
    )(length, queries, text, text, self_out)


def exchange(value, bit, n):
    return lax.ppermute(value, "seq", [(i, i ^ (1 << bit)) for i in range(n)])


def swap(value):
    return lax.ppermute(value, "dp", [(0, 1), (1, 0)])


def bit_of(index, bit):
    return (index >> bit) & 1


def pick(value, index):
    return lax.dynamic_index_in_dim(value, index, 0, keepdims=False)


def in_order(mine, other, position):
    first = jnp.where(position == 0, mine, other)
    second = jnp.where(position == 0, other, mine)
    return jnp.stack([first, second])


def text_of_pair(embed, key_weight, value_weight, length, encoder, n):
    positions, columns = embed.shape
    few = positions // 8
    core = lax.axis_index("dp")
    me = lax.axis_index("seq")
    half = columns // 2
    facts = jnp.stack([length, encoder])
    other_facts = swap(facts)
    own_half = lax.dynamic_slice_in_dim(embed, core * half, half, 1)
    sent_half = lax.dynamic_slice_in_dim(embed, (1 - core) * half, half, 1)
    other_half = swap(sent_half)
    mine_long = length > other_facts[0]
    encoder_long = jnp.where(mine_long, encoder, other_facts[1])
    encoder_short = jnp.where(mine_long, other_facts[1], encoder)
    long = jnp.where(mine_long, own_half, other_half)
    short = jnp.where(mine_long, other_half[:few], own_half[:few])
    rows_long, rows_short = positions // 4, few // 4
    rows = rows_long + rows_short
    packed = jnp.concatenate(
        [long.reshape(4, rows_long, half), short.reshape(4, rows_short, half)], axis=1
    ).reshape(2, 2, rows, half)

    def choose(own, got, bit):
        keep_long = bit_of(encoder_long, bit) == bit_of(me, bit)
        keep_short = bit_of(encoder_short, bit) == bit_of(me, bit)
        place = lax.broadcasted_iota(jnp.int32, (rows, 1), 0)
        keep = jnp.where(place < rows_long, keep_long, keep_short)
        return jnp.where(keep, own, got)

    x, y = bit_of(me, 0), bit_of(me, 1)
    part_a, part_b = packed[..., : half // 2], packed[..., half // 2 :]
    part_a, part_b = part_a.transpose(1, 0, 2, 3), part_b
    got_a = exchange(pick(part_a, 1 - x), 0, n)
    got_b = exchange(pick(part_b, 1 - y), 1, n)
    part_a = choose(pick(part_a, x), got_a, 0)
    part_b = choose(pick(part_b, y), got_b, 1)
    got_a = exchange(pick(part_a, 1 - y), 1, n)
    got_b = exchange(pick(part_b, 1 - x), 0, n)
    piece = jnp.concatenate(
        [choose(pick(part_a, y), got_a, 1), choose(pick(part_b, x), got_b, 0)], axis=1
    )
    bits = n.bit_length() - 1
    last = bits - 1
    for bit in range(2, last):
        piece = choose(piece, exchange(piece, bit, n), bit)
    near = bit_of(me, 2)
    halves = jnp.stack([piece[:, : half // 2], piece[:, half // 2 :]])
    own = pick(halves, near)
    own = choose(own, exchange(own, last, n), last)
    got = exchange(own, 2, n)
    part_a, part_b = jnp.where(near == 0, own, got), jnp.where(near == 0, got, own)
    two_a = in_order(part_a, exchange(part_a, 1, n), y)
    two_b = in_order(part_b, exchange(part_b, 0, n), x)
    four_a = in_order(two_a, exchange(two_a, 0, n), x).transpose(1, 0, 2, 3)
    four_b = in_order(two_b, exchange(two_b, 1, n), y)
    weight = jnp.concatenate([key_weight, value_weight], axis=1)
    width = weight.shape[1]
    sums = jnp.dot(
        four_a.reshape(4 * rows, half // 2), weight[: half // 2], preferred_element_type=jnp.float32
    ) + jnp.dot(
        four_b.reshape(4 * rows, half // 2), weight[half // 2 :], preferred_element_type=jnp.float32
    )
    sums = sums.reshape(4, rows, width)
    sums_long = sums[:, :rows_long].reshape(positions, width)
    sums_short = jnp.pad(sums[:, rows_long:].reshape(few, width), ((0, positions - few), (0, 0)))
    mine = jnp.where(mine_long, sums_long, sums_short)
    sent = jnp.where(mine_long, sums_short, sums_long)
    return (mine + swap(sent)).astype(jnp.bfloat16)


def text_of_clip(embed, key_weight, value_weight, encoder):
    kept = jnp.where(lax.axis_index("seq") == encoder, embed, 0).astype(embed.dtype)
    prompt = lax.psum(kept, "seq")
    weight = lax.all_gather(
        jnp.concatenate([key_weight, value_weight], axis=1), "dp", axis=0, tiled=True
    )
    return jnp.dot(prompt, weight, preferred_element_type=jnp.float32).astype(jnp.bfloat16)


def shards(
    n_dp,
    n,
    self_query,
    self_key,
    self_value,
    cross_query,
    text_embed,
    cross_key_weight,
    cross_value_weight,
    text_lengths,
    encoder_index,
):
    packed = pack([self_query[0], self_key[0], self_value[0]], n)
    count, rows, width = packed.shape[1:]
    packed_cross = pack([cross_query[0]], n).reshape(n, rows, width)
    blocks = lax.all_to_all(
        packed.reshape(n, count * rows, width), "seq", split_axis=0, concat_axis=0, tiled=True
    ).reshape(packed.shape)
    packed_cross, blocks = lax.optimization_barrier((packed_cross, blocks))
    cross = lax.all_to_all(packed_cross, "seq", split_axis=0, concat_axis=0, tiled=True)
    if n_dp == 2 and n >= 16 and n & (n - 1) == 0:
        text = text_of_pair(
            text_embed[0, 0],
            cross_key_weight,
            cross_value_weight,
            text_lengths[0],
            encoder_index[0],
            n,
        )
    else:
        text = text_of_clip(
            text_embed[0, 0], cross_key_weight, cross_value_weight, encoder_index[0]
        )
    self_out = self_attention(blocks)
    out = cross_attention(cross, text, text_lengths, self_out)
    tokens = lax.all_to_all(out, "seq", split_axis=0, concat_axis=0, tiled=True)
    return unpack(tokens)[None]


def solution(mesh):
    placed = (
        P("dp", "seq", None),
        P("dp", "seq", None),
        P("dp", "seq", None),
        P("dp", "seq", None),
        P("dp", "seq", None, None),
        P("dp", "seq"),
        P("dp", "seq"),
        P("dp"),
        P("dp"),
    )
    return jax.shard_map(
        functools.partial(shards, mesh.shape["dp"], mesh.shape["seq"]),
        mesh=mesh,
        in_specs=placed,
        out_specs=P("dp", "seq", None),
        check_vma=False,
    )
```

time: 488 us -> 238 us (0.49)
  waiting for transfers between devices: 224 us -> 100 us
  other arithmetic: 90.3 us -> 18.3 us
  matrix products: 61 us -> 3.85 us
  local copies, waits for them, and re-layouts: 51.5 us -> 10.3 us
  blocking collectives: 0 us -> 32.2 us
  Pallas kernels: 0 us -> 29.7 us
  between operations: 16.2 us -> 3.61 us
    psum x1 -> x0, waiting for transfers between devices: 161 us -> none  [broadcast(): return lax.psum(kept, axis)]
    ppermute x0 -> x14, waiting for transfers between devices: none -> 100 us  [the longest x11 97.8 us: exchange(): return lax.ppermute(value, 'seq', [(i, i ^ 1 << bit) for i in range(n)])]
    unnamed x4 -> x0, other arithmetic: 79.4 us -> none
    all_to_all x4 -> x2, waiting for transfers between devices: 51.8 us -> 0.01 us  [the longest x1 0.01 us: shards(): lax.all_to_all(packed_cross, 'seq', split_axis=0, concat_axis=0, tiled=True)]
    dot_general x8 -> x2, matrix products: 40.9 us -> 3.85 us  [the longest x1 2.05 us: text_of_pair(): jnp.dot(four_b.reshape(4 * rows, half // 2), weight[half // 2:], preferre...]
    all_to_all x0 -> x1, blocking collectives: none -> 32.2 us  [shards(): tokens = lax.all_to_all(out, 'seq', split_axis=0, concat_axis=0, tiled=True)]
    pallas_call x0 -> x5, Pallas kernels: none -> 29.7 us  [the longest x1 17 us: self_attention(): pl.pallas_call(body, grid=(heads, n // step), in_specs=[pl.BlockSpec((ste...]
    all_to_all x4 -> x2, starting transfers between devices: 39.8 us -> 10.8 us  [the longest x1 6.49 us: shards(): lax.all_to_all(packed.reshape(n, count * rows, width), 'seq', split_axis=...]
  transfers between devices with their start and end apart: 9 -> 16, of which waited for: 5 -> 12; matrix products, arithmetic and copies ran while one was open for 39% -> 8% of each run, Pallas kernels for 0% -> 9%
where the time goes in v1:
time: 238 us; the launch traced here: 237 us
  waiting for transfers between devices  100 us (42%)
  starting transfers between devices  39.2 us (16%)
  blocking collectives  32.2 us (14%)
  Pallas kernels  29.7 us (12%)
  other arithmetic  18.3 us (8%)
  local copies, waits for them, and re-layouts  10.3 us (4%)
  matrix products  3.85 us (2%)
  between operations  3.61 us (2%)
    ppermute x11, waiting for transfers between devices, exchange(): return lax.ppermute(value, 'seq', [(i, i ^ 1 << bit) for i in range(n)])  97.8 us
    all_to_all x1, blocking collectives, shards(): tokens = lax.all_to_all(out, 'seq', split_axis=0, concat_axis=0, tiled=True)  32.2 us
    ppermute x11, starting transfers between devices, exchange(): return lax.ppermute(value, 'seq', [(i, i ^ 1 << bit) for i in range(n)])  27.8 us
    pallas_call x1, Pallas kernels, self_attention(): pl.pallas_call(body, grid=(heads, n // step), in_specs=[pl.BlockSpec((ste...  17 us
    pallas_call x1, Pallas kernels, cross_attention(): pl.pallas_call(body, grid_spec=pltpu.PrefetchScalarGridSpec(num_scalar_pr...  7.25 us
    all_to_all x1, starting transfers between devices, shards(): lax.all_to_all(packed.reshape(n, count * rows, width), 'seq', split_axis=...  6.49 us
    select_n x6, other arithmetic, choose(): return jnp.where(keep, own, got)  5.41 us
    unnamed x31, local copies, waits for them, and re-layouts  5.37 us
  transfers between devices with their start and end apart: 16, of which 12 were waited for; matrix products, arithmetic and copies ran while one was open for 8% of the time, Pallas kernels for 9%

profile of v1, /device:TPU:0, one launch (start us, length us, event | category | flops | bytes accessed | tf_op | source)
XLA Modules:
  0.0 237.3 jit_solution(10449064703332602715)
XLA Ops:
  0.0 3.2 %dynamic-slice_bitcast_fusion = bf16[512,2048]{1,0:T(8,128)(2,1)} fusion(bf16[1,1,512,4096]{3,2,1,0:T(8,128)(2,1)} %param.13, s32[]{:T(128)S(6)} %select_n.186), kind=kLoop, calls=%fused_computation.3 | loop fusion | bytes 4194308 | tf_op jit(solution)/shard_map/dynamic_slice | solution.py:191
  3.2 0.5 collective-permute-start.1
  5.0 0.1 pad_add_fusion
  5.1 2.3 collective-permute-done
  7.4 0.6 fusion.18
  8.7 2.4 %bitcast_select_fusion = bf16[512,2048]{1,0:T(8,128)(2,1)S(1)} fusion(bf16[512,2048]{1,0:T(8,128)(2,1)S(1)} %collective-permute-done.1, bf16[1,1,512,4096]{3,2,1,0:T(8,128)(2,1)} %param.13, s32[]{:T(128)S(6)} %select_n.185, pred[]{:T(512)} %bitcast.7), kind=kLoop, calls=%fused_computation.2 | loop fusion | flops 1048576 | bytes 6291461 | tf_op jit(solution)/shard_map/jit(_where)/select_n | solution.py:196
  11.1 1.2 fusion.13
  12.4 0.1 fusion
  12.5 0.9 dynamic-slice_bitcast_fusion.1
  13.4 0.3 copy-done.8
  13.7 2.8 %collective-permute-start.2 = (bf16[2,144,1024]{2,1,0:T(8,128)(2,1)}, bf16[2,144,1024]{2,1,0:T(8,128)(2,1)}, u32[]{:S(2)}, u32[]{:S(2)}) collective-permute-start(bf16[2,144,1024]{2,1,0:T(8,128)(2,1)} %dynamic-slice_bitcast_fusion.1), channel_id=1, source_target_pairs={{0,1},{1,0},{2,3},{3,2},{4,5},{5,4},{6,7},{7,6},{8,9},{9,8},{10,11... | collective-permute-start | bytes 1769480 | tf_op jit(solution)/shard_map/ppermute | solution.py:161
  16.5 2.3 pack.3
  18.9 6.5 %all-to-all-start = ((bf16[16,384,256]{2,1,0:T(8,128)(2,1)}), bf16[16,384,256]{2,1,0:T(8,128)(2,1)S(1)}, u32[]{:S(2)}, u32[]{:S(2)}) async-start(bf16[16,384,256]{2,1,0:T(8,128)(2,1)} %bitcast.86), calls=%async_computation | async-start | bytes 6291456 | tf_op jit(solution)/shard_map/all_to_all | solution.py:277
  26.7 1.2 fusion.7
  27.8 2.0 collective-permute-start.4
  29.9 1.1 collective-permute-done.2
  30.9 1.2 bitcast_select_fusion.1
  32.2 2.2 collective-permute-start.3
  34.3 32.5 %collective-permute-done.4 = bf16[2,144,1024]{2,1,0:T(8,128)(2,1)S(1)} collective-permute-done((bf16[2,144,1024]{2,1,0:T(8,128)(2,1)S(1)}, bf16[2,144,1024]{2,1,0:T(8,128)(2,1)S(1)}, u32[]{:S(2)}, u32[]{:S(2)}) %collective-permute-start.4) | collective-permute-done | bytes 589856 | tf_op jit(solution)/shard_map/ppermute | solution.py:161
  66.9 0.2 fusion.10
  67.1 1.5 collective-permute-start.5
  68.7 5.6 %collective-permute-done.3 = bf16[144,1024]{1,0:T(8,128)(2,1)S(1)} collective-permute-done((bf16[144,1024]{1,0:T(8,128)(2,1)S(1)}, bf16[144,1024]{1,0:T(8,128)(2,1)S(1)}, u32[]{:S(2)}, u32[]{:S(2)}) %collective-permute-start.3) | collective-permute-done | bytes 294944 | tf_op jit(solution)/shard_map/ppermute | solution.py:161
  74.3 0.1 bitcast_select_fusion.3
  74.4 3.5 %collective-permute-done.5 = bf16[144,1024]{1,0:T(8,128)(2,1)S(1)} collective-permute-done((bf16[144,1024]{1,0:T(8,128)(2,1)S(1)}, bf16[144,1024]{1,0:T(8,128)(2,1)S(1)}, u32[]{:S(2)}, u32[]{:S(2)}) %collective-permute-start.5) | collective-permute-done | bytes 294944 | tf_op jit(solution)/shard_map/ppermute | solution.py:161
  77.9 0.8 bitcast_select_fusion.2
  78.7 1.8 pad_maximum_fusion.2
  80.6 0.7 collective-permute-start.6
  81.3 19.9 %collective-permute-done.6 = bf16[144,2048]{1,0:T(8,128)(2,1)} collective-permute-done((bf16[144,2048]{1,0:T(8,128)(2,1)}, bf16[144,2048]{1,0:T(8,128)(2,1)}, u32[]{:S(2)}, u32[]{:S(2)}) %collective-permute-start.6) | collective-permute-done | bytes 589856 | tf_op jit(solution)/shard_map/ppermute | solution.py:161
  101.2 1.3 broadcast_select_fusion
  102.6 0.1 fusion.12
  102.7 11.6 %collective-permute-start.7 = (bf16[144,1024]{1,0:T(8,128)(2,1)S(1)}, bf16[144,1024]{1,0:T(8,128)(2,1)}, u32[]{:S(2)}, u32[]{:S(2)}) collective-permute-start(bf16[144,1024]{1,0:T(8,128)(2,1)S(1)} %fusion.12), channel_id=1, source_target_pairs={{0,8},{1,9},{2,10},{3,11},{4,12},{5,13},{6,14},{7,15},{8,0},{9,1},... | collective-permute-start | bytes 884744 | tf_op jit(solution)/shard_map/ppermute | solution.py:161
  114.4 12.4 %collective-permute-done.7 = bf16[144,1024]{1,0:T(8,128)(2,1)} collective-permute-done((bf16[144,1024]{1,0:T(8,128)(2,1)S(1)}, bf16[144,1024]{1,0:T(8,128)(2,1)}, u32[]{:S(2)}, u32[]{:S(2)}) %collective-permute-start.7) | collective-permute-done | bytes 294944 | tf_op jit(solution)/shard_map/ppermute | solution.py:161
  126.8 1.8 broadcast_select_fusion.1
  128.5 9.2 %collective-permute-done.8 = bf16[144,1024]{1,0:T(8,128)(2,1)} collective-permute-done((bf16[144,1024]{1,0:T(8,128)(2,1)}, bf16[144,1024]{1,0:T(8,128)(2,1)}, u32[]{:S(2)}, u32[]{:S(2)}) %collective-permute-start.8) | collective-permute-done | bytes 294944 | tf_op jit(solution)/shard_map/ppermute | solution.py:161
  137.7 1.8 broadcast_select_fusion.2
  139.6 1.2 copy-done.2
  140.8 1.6 pack.2
  142.4 0.1 constant_dynamic-update-slice_fusion.1
  142.5 2.0 collective-permute-start.11
  144.5 3.5 %collective-permute-done.9 = bf16[144,1024]{1,0:T(8,128)(2,1)} collective-permute-done((bf16[144,1024]{1,0:T(8,128)(2,1)}, bf16[144,1024]{1,0:T(8,128)(2,1)}, u32[]{:S(2)}, u32[]{:S(2)}) %collective-permute-start.9) | collective-permute-done | bytes 294944 | tf_op jit(solution)/shard_map/ppermute | solution.py:161
  147.9 1.1 select_bitcast_fusion.7
  149.1 2.0 collective-permute-start.10
  151.1 0.2 collective-permute-done.11
  151.4 3.0 %collective-permute-start.12 = (bf16[2,144,1024]{2,1,0:T(8,128)(2,1)S(1)}, bf16[2,144,1024]{2,1,0:T(8,128)(2,1)S(1)}, u32[]{:S(2)}, u32[]{:S(2)}) collective-permute-start(bf16[2,144,1024]{2,1,0:T(8,128)(2,1)S(1)} %pad_maximum_fusion.4), channel_id=1, source_target_pairs={{0,2},{1,3},{2,0},{3,1},{4,6},{5,7},{6,4},{7,5},{8,10},{9,11},{10,... | collective-permute-start | bytes 1769480 | tf_op jit(solution)/shard_map/ppermute | solution.py:161
  154.4 0.1 constant_dynamic-update-slice_fusion
  154.5 8.9 %collective-permute-done.10 = bf16[2,144,1024]{2,1,0:T(8,128)(2,1)S(1)} collective-permute-done((bf16[2,144,1024]{2,1,0:T(8,128)(2,1)S(1)}, bf16[2,144,1024]{2,1,0:T(8,128)(2,1)S(1)}, u32[]{:S(2)}, u32[]{:S(2)}) %collective-permute-start.10) | collective-permute-done | bytes 589856 | tf_op jit(solution)/shard_map/ppermute | solution.py:161
  163.4 0.1 select_bitcast_fusion.3
  163.5 0.1 pad_maximum_fusion
  163.6 0.9 collective-permute-done.12
  164.5 1.1 select_bitcast_fusion.1
  165.6 1.8 fusion.4
  167.4 1.6 copy-done
  169.1 4.3 %all-to-all-start.1 = ((bf16[16,128,256]{2,1,0:T(8,128)(2,1)}), bf16[16,128,256]{2,1,0:T(8,128)(2,1)S(1)}, u32[]{:S(2)}, u32[]{:S(2)}) async-start(bf16[16,128,256]{2,1,0:T(8,128)(2,1)} %bitcast.1), calls=%async_computation.1 | async-start | bytes 2097152 | tf_op jit(solution)/shard_map/all_to_all | solution.py:281
  173.4 1.3 pad_maximum_fusion.1
  174.7 0.4 copy-done.12
  175.2 2.0 convolution_add_fusion
  177.3 0.1 pad_select_fusion
  177.4 0.1 collective-permute-start.13
  177.5 1.6 copy-done.1
  179.1 17.0 %self_attention.1.self_ref = bf16[16,128,256]{2,1,0:T(8,128)(2,1)S(1)} custom-call(bf16[16,3,128,256]{3,2,1,0:T(8,128)(2,1)S(1)} %bitcast.76, bf16[16,3,128,256]{3,2,1,0:T(8,128)(2,1)S(1)} %bitcast.77, bf16[16,3,128,256]{3,2,1,0:T(8,128)(2,1)S(1)} %bitcast.78), custom_call_target="tpu_custom_call" | custom-call | flops 4294967296 | bytes 4194304 | tf_op jit(solution)/shard_map/self_attention/pallas_call | solution.py:88
  196.1 0.2 fusion.2.k_ref.v_ref
  196.4 7.3 %cross_attention.1 = bf16[16,128,256]{2,1,0:T(8,128)(2,1)S(1)} custom-call(s32[1]{0:T(128)S(6)} %copy.12.length_ref, bf16[16,128,256]{2,1,0:T(8,128)(2,1)S(1)} %all-to-all-done.1.q_ref, bf16[512,512]{1,0:T(8,128)(2,1)S(1)} %fusion.2.k_ref.v_ref, bf16[512,512]{1,0:T(8,128)(2,1)S(1)} %fusion.2.k_ref.v_ref, bf16[16,128,256]{2,1,0:T(8,128)(2,1)S(1)} %self_attention.1.self_ref), custom_call_target="tpu_custom_call" | custom-call | flops 1073741824 | bytes 3145728 | tf_op jit(solution)/shard_map/cross_attention/pallas_call | solution.py:135
  203.6 32.2 %all_to_all.15.in_ref = bf16[16,128,256]{2,1,0:T(8,128)(2,1)S(1)} all-to-all(bf16[16,128,256]{2,1,0:T(8,128)(2,1)S(1)} %cross_attention.1), channel_id=1, replica_groups=mesh['dp'=2,'seq'=16] {'seq'}, dimensions={0} | all-to-all | bytes 2097152 | tf_op jit(solution)/shard_map/all_to_all | solution.py:297
  235.8 1.5 unpack.1
  (44 shorter events, 0.5 us)
Async XLA Ops:
  3.2 5.5 %collective-permute-start.1 = (bf16[512,2048]{1,0:T(8,128)(2,1)}, bf16[512,2048]{1,0:T(8,128)(2,1)S(1)}, u32[]{:S(2)}, u32[]{:S(2)}) collective-permute-start(bf16[512,2048]{1,0:T(8,128)(2,1)} %dynamic-slice_bitcast_fusion), channel_id=1, source_target_pairs={{0,16},{16,0},{1,17},{17,1},{2,18},{18,2},{3,19},{19,3},{4,20},{20... | collective-permute-start | bytes 6291464 | tf_op jit(solution)/shard_map/ppermute | solution.py:165
  5.0 2.4 %collective-permute-start = (s32[2]{0:T(128)S(1)}, s32[2]{0:T(128)S(1)}, u32[]{:S(2)}, u32[]{:S(2)}) collective-permute-start(s32[2]{0:T(128)S(1)} %pad_add_fusion), channel_id=1, source_target_pairs={{0,16},{16,0},{1,17},{17,1},{2,18},{18,2},{3,19},{19,3},{4,20},{20... | collective-permute-start | bytes 32 | tf_op jit(solution)/shard_map/ppermute | solution.py:165
  11.1 1.4 copy-start.6
  12.3 4.2 %copy-start.4 = (bf16[1,128,4096]{2,1,0:T(8,128)(2,1)S(1)}, bf16[1,128,4096]{2,1,0:T(8,128)(2,1)}, u32[]{:S(2)}) copy-start(bf16[1,128,4096]{2,1,0:T(8,128)(2,1)} %param.10) | copy-start | bytes 3145732
  12.3 4.2 %copy-start.5 = (bf16[1,128,4096]{2,1,0:T(8,128)(2,1)S(1)}, bf16[1,128,4096]{2,1,0:T(8,128)(2,1)}, u32[]{:S(2)}) copy-start(bf16[1,128,4096]{2,1,0:T(8,128)(2,1)} %param.11) | copy-start | bytes 3145732
  12.5 1.2 copy-start.8
  12.5 4.0 %copy-start.3 = (bf16[1,128,4096]{2,1,0:T(8,128)(2,1)S(1)}, bf16[1,128,4096]{2,1,0:T(8,128)(2,1)}, u32[]{:S(2)}) copy-start(bf16[1,128,4096]{2,1,0:T(8,128)(2,1)} %param.9) | copy-start | bytes 3145732
  13.7 17.2 %collective-permute-start.2 = (bf16[2,144,1024]{2,1,0:T(8,128)(2,1)}, bf16[2,144,1024]{2,1,0:T(8,128)(2,1)}, u32[]{:S(2)}, u32[]{:S(2)}) collective-permute-start(bf16[2,144,1024]{2,1,0:T(8,128)(2,1)} %dynamic-slice_bitcast_fusion.1), channel_id=1, source_target_pairs={{0,1},{1,0},{2,3},{3,2},{4,5},{5,4},{6,7},{7,6},{8,9},{9,8},{10,11... | collective-permute-start | bytes 1769480 | tf_op jit(solution)/shard_map/ppermute | solution.py:161
  18.9 148.6 %all-to-all-start = ((bf16[16,384,256]{2,1,0:T(8,128)(2,1)}), bf16[16,384,256]{2,1,0:T(8,128)(2,1)S(1)}, u32[]{:S(2)}, u32[]{:S(2)}) async-start(bf16[16,384,256]{2,1,0:T(8,128)(2,1)} %bitcast.86), calls=%async_computation | async-start | bytes 6291456 | tf_op jit(solution)/shard_map/all_to_all | solution.py:277
  26.6 4.3 %copy-start.9 = (bf16[2,2,144,1024]{3,2,1,0:T(8,128)(2,1)S(1)}, bf16[2,2,144,1024]{3,2,1,0:T(8,128)(2,1)}, u32[]{:S(2)}) copy-start(bf16[2,2,144,1024]{3,2,1,0:T(8,128)(2,1)} %copy-done.8) | copy-start | bytes 3538948
  27.8 39.0 %collective-permute-start.4 = (bf16[2,144,1024]{2,1,0:T(8,128)(2,1)S(1)}, bf16[2,144,1024]{2,1,0:T(8,128)(2,1)S(1)}, u32[]{:S(2)}, u32[]{:S(2)}) collective-permute-start(bf16[2,144,1024]{2,1,0:T(8,128)(2,1)S(1)} %fusion.7), channel_id=1, source_target_pairs={{0,2},{1,3},{2,0},{3,1},{4,6},{5,7},{6,4},{7,5},{8,10},{9,11},{10,... | collective-permute-start | bytes 1769480 | tf_op jit(solution)/shard_map/ppermute | solution.py:161
  29.9 37.0 %copy-start.7 = (bf16[512,2048]{1,0:T(8,128)(2,1)S(1)}, bf16[512,2048]{1,0:T(8,128)(2,1)}, u32[]{:S(2)}) copy-start(bf16[512,2048]{1,0:T(8,128)(2,1)} %copy-done.6) | copy-start | bytes 6291460
  32.2 42.1 %collective-permute-start.3 = (bf16[144,1024]{1,0:T(8,128)(2,1)S(1)}, bf16[144,1024]{1,0:T(8,128)(2,1)S(1)}, u32[]{:S(2)}, u32[]{:S(2)}) collective-permute-start(bf16[144,1024]{1,0:T(8,128)(2,1)S(1)} %dynamic-slice_bitcast_fusion.3), channel_id=1, source_target_pairs={{0,2},{1,3},{2,0},{3,1},{4,6},{5,7},{6,4},{7,5},{8,10},{9,11},{10,... | collective-permute-start | bytes 884744 | tf_op jit(solution)/shard_map/ppermute | solution.py:161
  67.1 10.8 %collective-permute-start.5 = (bf16[144,1024]{1,0:T(8,128)(2,1)S(1)}, bf16[144,1024]{1,0:T(8,128)(2,1)S(1)}, u32[]{:S(2)}, u32[]{:S(2)}) collective-permute-start(bf16[144,1024]{1,0:T(8,128)(2,1)S(1)} %dynamic-slice_bitcast_fusion.2), channel_id=1, source_target_pairs={{0,1},{1,0},{2,3},{3,2},{4,5},{5,4},{6,7},{7,6},{8,9},{9,8},{10,11... | collective-permute-start | bytes 884744 | tf_op jit(solution)/shard_map/ppermute | solution.py:161
  80.6 20.7 %collective-permute-start.6 = (bf16[144,2048]{1,0:T(8,128)(2,1)}, bf16[144,2048]{1,0:T(8,128)(2,1)}, u32[]{:S(2)}, u32[]{:S(2)}) collective-permute-start(bf16[144,2048]{1,0:T(8,128)(2,1)} %pad_maximum_fusion.2), channel_id=1, source_target_pairs={{0,4},{1,5},{2,6},{3,7},{4,0},{5,1},{6,2},{7,3},{8,12},{9,13},{10,... | collective-permute-start | bytes 1769480 | tf_op jit(solution)/shard_map/ppermute | solution.py:161
  102.7 24.0 %collective-permute-start.7 = (bf16[144,1024]{1,0:T(8,128)(2,1)S(1)}, bf16[144,1024]{1,0:T(8,128)(2,1)}, u32[]{:S(2)}, u32[]{:S(2)}) collective-permute-start(bf16[144,1024]{1,0:T(8,128)(2,1)S(1)} %fusion.12), channel_id=1, source_target_pairs={{0,8},{1,9},{2,10},{3,11},{4,12},{5,13},{6,14},{7,15},{8,0},{9,1},... | collective-permute-start | bytes 884744 | tf_op jit(solution)/shard_map/ppermute | solution.py:161
  128.5 9.2 %collective-permute-start.8 = (bf16[144,1024]{1,0:T(8,128)(2,1)}, bf16[144,1024]{1,0:T(8,128)(2,1)}, u32[]{:S(2)}, u32[]{:S(2)}) collective-permute-start(bf16[144,1024]{1,0:T(8,128)(2,1)} %broadcast_select_fusion.1), channel_id=1, source_target_pairs={{0,4},{1,5},{2,6},{3,7},{4,0},{5,1},{6,2},{7,3},{8,12},{9,13},{10,... | collective-permute-start | bytes 884744 | tf_op jit(solution)/shard_map/ppermute | solution.py:161
  139.5 8.4 %collective-permute-start.9 = (bf16[144,1024]{1,0:T(8,128)(2,1)}, bf16[144,1024]{1,0:T(8,128)(2,1)}, u32[]{:S(2)}, u32[]{:S(2)}) collective-permute-start(bf16[144,1024]{1,0:T(8,128)(2,1)} %get-tuple-element.16), channel_id=1, source_target_pairs={{0,2},{1,3},{2,0},{3,1},{4,6},{5,7},{6,4},{7,5},{8,10},{9,11},{10,... | collective-permute-start | bytes 884744 | tf_op jit(solution)/shard_map/ppermute | solution.py:161
  139.6 1.2 copy-start.2
  140.8 1.6 copy-start.13
  142.5 8.8 %collective-permute-start.11 = (bf16[144,1024]{1,0:T(8,128)(2,1)S(1)}, bf16[144,1024]{1,0:T(8,128)(2,1)S(1)}, u32[]{:S(2)}, u32[]{:S(2)}) collective-permute-start(bf16[144,1024]{1,0:T(8,128)(2,1)S(1)} %get-tuple-element.15), channel_id=1, source_target_pairs={{0,1},{1,0},{2,3},{3,2},{4,5},{5,4},{6,7},{7,6},{8,9},{9,8},{10,11... | collective-permute-start | bytes 884744 | tf_op jit(solution)/shard_map/ppermute | solution.py:161
  149.1 5.3 %copy-start.14 = (bf16[2048,256]{1,0:T(8,128)(2,1)S(1)}, bf16[2048,256]{1,0:T(8,128)(2,1)}, u32[]{:S(2)}) copy-start(bf16[2048,256]{1,0:T(8,128)(2,1)} %param.15) | copy-start | bytes 3145732
  149.1 14.3 %collective-permute-start.10 = (bf16[2,144,1024]{2,1,0:T(8,128)(2,1)S(1)}, bf16[2,144,1024]{2,1,0:T(8,128)(2,1)S(1)}, u32[]{:S(2)}, u32[]{:S(2)}) collective-permute-start(bf16[2,144,1024]{2,1,0:T(8,128)(2,1)S(1)} %pad_maximum_fusion.3), channel_id=1, source_target_pairs={{0,1},{1,0},{2,3},{3,2},{4,5},{5,4},{6,7},{7,6},{8,9},{9,8},{10,11... | collective-permute-start | bytes 1769480 | tf_op jit(solution)/shard_map/ppermute | solution.py:161
  151.4 13.1 %collective-permute-start.12 = (bf16[2,144,1024]{2,1,0:T(8,128)(2,1)S(1)}, bf16[2,144,1024]{2,1,0:T(8,128)(2,1)S(1)}, u32[]{:S(2)}, u32[]{:S(2)}) collective-permute-start(bf16[2,144,1024]{2,1,0:T(8,128)(2,1)S(1)} %pad_maximum_fusion.4), channel_id=1, source_target_pairs={{0,2},{1,3},{2,0},{3,1},{4,6},{5,7},{6,4},{7,5},{8,10},{9,11},{10,... | collective-permute-start | bytes 1769480 | tf_op jit(solution)/shard_map/ppermute | solution.py:161
  154.5 11.1 %copy-start.11 = (bf16[2048,512]{1,0:T(8,128)(2,1)}, bf16[2048,512]{1,0:T(8,128)(2,1)S(1)}, u32[]{:S(2)}) copy-start(bf16[2048,512]{1,0:T(8,128)(2,1)S(1)} %constant_dynamic-update-slice_fusion) | copy-start | bytes 6291460
  167.4 1.6 copy-start
  169.1 4.3 %copy-start.10 = (bf16[1,2,144,1024]{3,2,1,0:T(8,128)(2,1)S(1)}, bf16[1,2,144,1024]{3,2,1,0:T(8,128)(2,1)}, u32[]{:S(2)}) copy-start(bf16[1,2,144,1024]{3,2,1,0:T(8,128)(2,1)} %get-tuple-element.9) | copy-start | bytes 1769476
  169.1 27.3 %all-to-all-start.1 = ((bf16[16,128,256]{2,1,0:T(8,128)(2,1)}), bf16[16,128,256]{2,1,0:T(8,128)(2,1)S(1)}, u32[]{:S(2)}, u32[]{:S(2)}) async-start(bf16[16,128,256]{2,1,0:T(8,128)(2,1)} %bitcast.1), calls=%async_computation.1 | async-start | bytes 2097152 | tf_op jit(solution)/shard_map/all_to_all | solution.py:281
  173.4 1.8 copy-start.12
  177.2 1.9 copy-start.1
  177.4 18.7 %collective-permute-start.13 = (f32[512,512]{1,0:T(8,128)S(1)}, f32[512,512]{1,0:T(8,128)S(1)}, u32[]{:S(2)}, u32[]{:S(2)}) collective-permute-start(f32[512,512]{1,0:T(8,128)S(1)} %pad_select_fusion), channel_id=1, source_target_pairs={{0,16},{16,0},{1,17},{17,1},{2,18},{18,2},{3,19},{19,3},{4,20},{20... | collective-permute-start | bytes 3145736 | tf_op jit(solution)/shard_map/ppermute | solution.py:165

commit v2 on v1

--- a/solution.py
+++ b/solution.py
@@ -17,46 +17,52 @@
     return pltpu.CompilerParams(vmem_limit_bytes=VMEM_BYTES)
 
 
-def pack(arrays, n):
+def pack(arrays, n, groups):
     rows, columns = arrays[0].shape
     width = columns // n
+    part = width // groups
     per = max(1, n // 4)
     count = len(arrays)
 
     def body(*refs):
-        out_ref = refs[-1]
-        for a in range(count):
-            for j in range(per):
-                out_ref[j, a] = refs[a][:, j * width : (j + 1) * width]
+        for g in range(groups):
+            for a in range(count):
+                for j in range(per):
+                    start = j * width + g * part
+                    refs[count + g][j, a] = refs[a][:, start : start + part]
 
     return pl.pallas_call(
         body,
         grid=(n // per,),
         in_specs=[pl.BlockSpec((rows, per * width), lambda i: (0, i))] * count,
-        out_specs=pl.BlockSpec((per, count, rows, width), lambda i: (i, 0, 0, 0)),
-        out_shape=jax.ShapeDtypeStruct((n, count, rows, width), arrays[0].dtype),
+        out_specs=[pl.BlockSpec((per, count, rows, part), lambda i: (i, 0, 0, 0))] * groups,
+        out_shape=[jax.ShapeDtypeStruct((n, count, rows, part), arrays[0].dtype)] * groups,
         compiler_params=params(),
         name="pack",
     )(*arrays)
 
 
-def unpack(blocks):
-    n, rows, width = blocks.shape
+def unpack(parts):
+    groups = len(parts)
+    n, rows, part = parts[0].shape
+    width = part * groups
     per = max(1, n // 4)
 
-    def body(in_ref, out_ref):
-        for j in range(per):
-            out_ref[:, j * width : (j + 1) * width] = in_ref[j]
+    def body(*refs):
+        for g in range(groups):
+            for j in range(per):
+                start = j * width + g * part
+                refs[groups][:, start : start + part] = refs[g][j]
 
     return pl.pallas_call(
         body,
         grid=(n // per,),
-        in_specs=[pl.BlockSpec((per, rows, width), lambda i: (i, 0, 0))],
+        in_specs=[pl.BlockSpec((per, rows, part), lambda i: (i, 0, 0))] * groups,
         out_specs=pl.BlockSpec((rows, per * width), lambda i: (0, i)),
-        out_shape=jax.ShapeDtypeStruct((rows, n * width), blocks.dtype),
+        out_shape=jax.ShapeDtypeStruct((rows, n * width), parts[0].dtype),
         compiler_params=params(),
         name="unpack",
-    )(blocks)
+    )(*parts)
 
 
 def self_attention(blocks):
@@ -106,10 +112,11 @@
     )(blocks, blocks, blocks)
 
 
-def cross_attention(queries, text, length, self_out):
-    n, rows, width = queries.shape
+def cross_attention(blocks, text, length, self_out, first):
+    n, _, rows, width = blocks.shape
     heads = width // HEAD
     positions = text.shape[0]
+    values_at = text.shape[1] // HEAD // 2 + first
     step = max(1, min(n, 512 // rows))
     factor = LOG2E / HEAD**0.5
 
@@ -119,7 +126,7 @@
             values[:, :HEAD] = v_ref[...]
             values[:, HEAD:] = jnp.ones((positions, HEAD), jnp.bfloat16)
 
-        q = q_ref[...].reshape(step * rows, HEAD)
+        q = q_ref[:, 0].reshape(step * rows, HEAD)
         scores = lax.dot_general(
             q, k_ref[...], (((1,), (1,)), ((), ())), preferred_element_type=jnp.float32
         )
@@ -138,9 +145,9 @@
             num_scalar_prefetch=1,
             grid=(heads, n // step),
             in_specs=[
-                pl.BlockSpec((step, rows, HEAD), lambda h, i, _: (i, 0, h)),
-                pl.BlockSpec((positions, HEAD), lambda h, i, _: (0, h)),
-                pl.BlockSpec((positions, HEAD), lambda h, i, _: (0, heads + h)),
+                pl.BlockSpec((step, 1, rows, HEAD), lambda h, i, _: (i, 3, 0, h)),
+                pl.BlockSpec((positions, HEAD), lambda h, i, _: (0, first + h)),
+                pl.BlockSpec((positions, HEAD), lambda h, i, _: (0, values_at + h)),
                 pl.BlockSpec((step, rows, HEAD), lambda h, i, _: (i, 0, h)),
             ],
             out_specs=pl.BlockSpec((step, rows, HEAD), lambda h, i, _: (i, 0, h)),
@@ -154,7 +161,12 @@
             transcendentals=heads * n * rows * positions,
         ),
         name="cross_attention",
-    )(length, queries, text, text, self_out)
+    )(length, blocks, text, text, self_out)
+
+
+def spread(blocks):
+    flat = blocks.reshape(blocks.shape[0], -1, blocks.shape[-1])
+    return lax.all_to_all(flat, "seq", split_axis=0, concat_axis=0, tiled=True).reshape(blocks.shape)
 
 
 def exchange(value, bit, n):
@@ -179,7 +191,7 @@
     return jnp.stack([first, second])
 
 
-def text_of_pair(embed, key_weight, value_weight, length, encoder, n):
+def text_of_pair(embed, key_weight, value_weight, length, encoder, n, before, between):
     positions, columns = embed.shape
     few = positions // 8
     core = lax.axis_index("dp")
@@ -220,6 +232,7 @@
     piece = jnp.concatenate(
         [choose(pick(part_a, y), got_a, 1), choose(pick(part_b, x), got_b, 0)], axis=1
     )
+    piece = before(piece)
     bits = n.bit_length() - 1
     last = bits - 1
     for bit in range(2, last):
@@ -230,6 +243,7 @@
     own = choose(own, exchange(own, last, n), last)
     got = exchange(own, 2, n)
     part_a, part_b = jnp.where(near == 0, own, got), jnp.where(near == 0, got, own)
+    part_a, part_b = between((part_a, part_b))
     two_a = in_order(part_a, exchange(part_a, 1, n), y)
     two_b = in_order(part_b, exchange(part_b, 0, n), x)
     four_a = in_order(two_a, exchange(two_a, 0, n), x).transpose(1, 0, 2, 3)
@@ -271,15 +285,25 @@
     text_lengths,
     encoder_index,
 ):
-    packed = pack([self_query[0], self_key[0], self_value[0]], n)
-    count, rows, width = packed.shape[1:]
-    packed_cross = pack([cross_query[0]], n).reshape(n, rows, width)
-    blocks = lax.all_to_all(
-        packed.reshape(n, count * rows, width), "seq", split_axis=0, concat_axis=0, tiled=True
-    ).reshape(packed.shape)
-    packed_cross, blocks = lax.optimization_barrier((packed_cross, blocks))
-    cross = lax.all_to_all(packed_cross, "seq", split_axis=0, concat_axis=0, tiled=True)
-    if n_dp == 2 and n >= 16 and n & (n - 1) == 0:
+    width = cross_key_weight.shape[1]
+    groups = 2 if width // HEAD % 2 == 0 else 1
+    packed = pack([self_query[0], self_key[0], self_value[0], cross_query[0]], n, groups)
+    blocks = [spread(packed[0])]
+    self_out = []
+    pair = n_dp == 2 and n >= 16 and n & (n - 1) == 0
+
+    def before(piece):
+        blocks[0], piece = lax.optimization_barrier((blocks[0], piece))
+        self_out.append(self_attention(blocks[0]))
+        return piece
+
+    def between(parts):
+        if groups > 1:
+            parts, later, self_out[0] = lax.optimization_barrier((parts, packed[1], self_out[0]))
+            blocks.append(spread(later))
+        return parts
+
+    if pair:
         text = text_of_pair(
             text_embed[0, 0],
             cross_key_weight,
@@ -287,14 +311,24 @@
             text_lengths[0],
             encoder_index[0],
             n,
+            before,
+            between,
         )
     else:
+        before(text_lengths)
+        between(text_lengths)
         text = text_of_clip(
             text_embed[0, 0], cross_key_weight, cross_value_weight, encoder_index[0]
         )
-    self_out = self_attention(blocks)
-    out = cross_attention(cross, text, text_lengths, self_out)
-    tokens = lax.all_to_all(out, "seq", split_axis=0, concat_axis=0, tiled=True)
+    tokens = []
+    for g in range(groups):
+        if g > 0:
+            blocks[g], out = lax.optimization_barrier((blocks[g], out))
+            self_out.append(self_attention(blocks[g]))
+            tokens.append(spread(out))
+        first = g * (width // HEAD // groups)
+        out = cross_attention(blocks[g], text, text_lengths, self_out[g], first)
+    tokens.append(spread(out))
     return unpack(tokens)[None]
 
 

time: 238 us -> 210 us (0.88)
  blocking collectives: 32.2 us -> 20.1 us
  other arithmetic: 18.3 us -> 8.65 us
  local copies, waits for them, and re-layouts: 10.3 us -> 7.9 us
    all_to_all x1, blocking collectives: 32.2 us -> 20.1 us  [spread(): lax.all_to_all(flat, 'seq', split_axis=0, concat_axis=0, tiled=True)]
    ppermute x11, starting transfers between devices: 27.8 us -> 16.4 us  [exchange(): return lax.ppermute(value, 'seq', [(i, i ^ 1 << bit) for i in range(n)])]
    all_to_all x2 -> x3, starting transfers between devices: 10.8 us -> 20.6 us  [spread(): lax.all_to_all(flat, 'seq', split_axis=0, concat_axis=0, tiled=True)]
    select_n x6, other arithmetic: 5.41 us -> 0.78 us  [choose(): return jnp.where(keep, own, got)]
    ppermute x11, waiting for transfers between devices: 97.8 us -> 93.8 us  [exchange(): return lax.ppermute(value, 'seq', [(i, i ^ 1 << bit) for i in range(n)])]
    another operation x8, other arithmetic: 3.86 us -> 0.59 us  [in_order(): return jnp.stack([first, second])]
    unnamed x31 -> x17, local copies, waits for them, and re-layouts: 5.37 us -> 3.66 us
    pallas_call x1 -> x2, Pallas kernels: 7.25 us -> 8.41 us  [cross_attention(): pl.pallas_call(body, grid_spec=pltpu.PrefetchScalarGridSpec(num_scalar_pr...]
  transfers between devices with their start and end apart: 16 -> 17, of which waited for: 12 -> 11; matrix products, arithmetic and copies ran while one was open for 8% -> 6% of each run, Pallas kernels for 9% -> 14%
where the time goes in v2:
time: 210 us; the launch traced here: 209 us
  waiting for transfers between devices  98.9 us (47%)
  starting transfers between devices  37.7 us (18%)
  Pallas kernels  30.8 us (15%)
  blocking collectives  20.1 us (10%)
  other arithmetic  8.65 us (4%)
  local copies, waits for them, and re-layouts  7.9 us (4%)
  between operations  3.42 us (2%)
    ppermute x11, waiting for transfers between devices, exchange(): return lax.ppermute(value, 'seq', [(i, i ^ 1 << bit) for i in range(n)])  93.8 us
    all_to_all x3, starting transfers between devices, spread(): lax.all_to_all(flat, 'seq', split_axis=0, concat_axis=0, tiled=True)  20.6 us
    all_to_all x1, blocking collectives, spread(): lax.all_to_all(flat, 'seq', split_axis=0, concat_axis=0, tiled=True)  20.1 us
    pallas_call x2, Pallas kernels, self_attention(): pl.pallas_call(body, grid=(heads, n // step), in_specs=[pl.BlockSpec((ste...  17.8 us
    ppermute x11, starting transfers between devices, exchange(): return lax.ppermute(value, 'seq', [(i, i ^ 1 << bit) for i in range(n)])  16.4 us
    pallas_call x2, Pallas kernels, cross_attention(): pl.pallas_call(body, grid_spec=pltpu.PrefetchScalarGridSpec(num_scalar_pr...  8.41 us
  transfers between devices with their start and end apart: 17, of which 11 were waited for; matrix products, arithmetic and copies ran while one was open for 6% of the time, Pallas kernels for 14%

profile of v2, /device:TPU:0, one launch (start us, length us, event | category | flops | bytes accessed | tf_op | source)
XLA Modules:
  0.0 209.0 jit_solution(12323551079262090053)
XLA Ops:
  0.0 3.4 %dynamic-slice_bitcast_fusion = bf16[512,2048]{1,0:T(8,128)(2,1)} fusion(bf16[1,1,512,4096]{3,2,1,0:T(8,128)(2,1)} %param.13, s32[]{:T(128)S(6)} %select_n.183), kind=kLoop, calls=%fused_computation.3 | loop fusion | bytes 4194308 | tf_op jit(solution)/shard_map/dynamic_slice | solution.py:203
  3.4 0.5 collective-permute-start.1
  3.9 3.0 %pack.1 = (bf16[16,4,128,128]{3,2,1,0:T(8,128)(2,1)}, bf16[16,4,128,128]{3,2,1,0:T(8,128)(2,1)}) custom-call(bf16[128,4096]{1,0:T(8,128)(2,1)S(1)} %bitcast.81, bf16[128,4096]{1,0:T(8,128)(2,1)S(1)} %bitcast.82, bf16[128,4096]{1,0:T(8,128)(2,1)S(1)} %bitcast.83, bf16[128,4096]{1,0:T(8,128)(2,1)S(1)} %bitcast.84), custom_call_target="tpu_custom_call" | custom-call | tf_op jit(solution)/shard_map/pack/pallas_call | solution.py:34
  6.8 7.9 %all-to-all-start = ((bf16[16,512,128]{2,1,0:T(8,128)(2,1)}), bf16[16,512,128]{2,1,0:T(8,128)(2,1)S(1)}, u32[]{:S(2)}, u32[]{:S(2)}) async-start(bf16[16,512,128]{2,1,0:T(8,128)(2,1)} %bitcast.95), calls=%async_computation | async-start | bytes 4194304 | tf_op jit(solution)/shard_map/all_to_all | solution.py:169
  16.0 0.1 pad_add_fusion
  16.1 0.2 collective-permute-start
  16.3 0.9 collective-permute-done
  17.2 0.6 fusion.18
  18.3 1.1 fusion.13
  19.4 3.0 %bitcast_select_fusion = bf16[512,2048]{1,0:T(8,128)(2,1)S(1)} fusion(bf16[512,2048]{1,0:T(8,128)(2,1)} %collective-permute-done.1, bf16[1,1,512,4096]{3,2,1,0:T(8,128)(2,1)} %param.13, s32[]{:T(128)S(6)} %select_n.182, pred[]{:T(512)} %bitcast), kind=kLoop, calls=%fused_computation.2 | loop fusion | flops 1048576 | bytes 6291461 | tf_op jit(solution)/shard_map/jit(_where)/select_n | solution.py:208
  22.5 0.1 fusion.7
  22.5 1.3 copy-done.4
  23.8 1.9 collective-permute-start.4
  26.9 1.5 fusion
  28.5 1.5 collective-permute-start.2
  30.0 19.3 %collective-permute-done.4 = bf16[2,144,1024]{2,1,0:T(8,128)(2,1)S(1)} collective-permute-done((bf16[2,144,1024]{2,1,0:T(8,128)(2,1)S(1)}, bf16[2,144,1024]{2,1,0:T(8,128)(2,1)S(1)}, u32[]{:S(2)}, u32[]{:S(2)}) %collective-permute-start.4) | collective-permute-done | bytes 589856 | tf_op jit(solution)/shard_map/ppermute | solution.py:173
  49.3 0.2 fusion.10
  49.5 1.5 collective-permute-start.5
  51.1 9.8 %collective-permute-done.2 = bf16[2,144,1024]{2,1,0:T(8,128)(2,1)S(1)} collective-permute-done((bf16[2,144,1024]{2,1,0:T(8,128)(2,1)S(1)}, bf16[2,144,1024]{2,1,0:T(8,128)(2,1)S(1)}, u32[]{:S(2)}, u32[]{:S(2)}) %collective-permute-start.2) | collective-permute-done | bytes 589856 | tf_op jit(solution)/shard_map/ppermute | solution.py:173
  60.8 0.1 bitcast_select_fusion.1
  61.0 0.1 collective-permute-start.3
  61.1 4.9 %collective-permute-done.5 = bf16[144,1024]{1,0:T(8,128)(2,1)S(1)} collective-permute-done((bf16[144,1024]{1,0:T(8,128)(2,1)S(1)}, bf16[144,1024]{1,0:T(8,128)(2,1)S(1)}, u32[]{:S(2)}, u32[]{:S(2)}) %collective-permute-start.5) | collective-permute-done | bytes 294944 | tf_op jit(solution)/shard_map/ppermute | solution.py:173
  66.0 0.1 bitcast_select_fusion.2
  66.1 1.7 collective-permute-done.3
  67.8 0.1 bitcast_select_fusion.3
  68.0 0.1 collective-permute-start.6
  68.1 12.5 %collective-permute-done.6 = bf16[144,2048]{1,0:T(8,128)(2,1)S(1)} collective-permute-done((bf16[144,2048]{1,0:T(8,128)(2,1)S(1)}, bf16[144,2048]{1,0:T(8,128)(2,1)S(1)}, u32[]{:S(2)}, u32[]{:S(2)}) %collective-permute-start.6) | collective-permute-done | bytes 589856 | tf_op jit(solution)/shard_map/ppermute | solution.py:173
  80.6 0.1 broadcast_select_fusion
  80.8 0.1 fusion.12
  80.9 6.1 %collective-permute-start.7 = (bf16[144,1024]{1,0:T(8,128)(2,1)S(1)}, bf16[144,1024]{1,0:T(8,128)(2,1)S(1)}, u32[]{:S(2)}, u32[]{:S(2)}) collective-permute-start(bf16[144,1024]{1,0:T(8,128)(2,1)S(1)} %fusion.12), channel_id=1, source_target_pairs={{0,8},{1,9},{2,10},{3,11},{4,12},{5,13},{6,14},{7,15},{8,0},{9,1},... | collective-permute-start | bytes 884744 | tf_op jit(solution)/shard_map/ppermute | solution.py:173
  87.0 9.5 %collective-permute-done.7 = bf16[144,1024]{1,0:T(8,128)(2,1)S(1)} collective-permute-done((bf16[144,1024]{1,0:T(8,128)(2,1)S(1)}, bf16[144,1024]{1,0:T(8,128)(2,1)S(1)}, u32[]{:S(2)}, u32[]{:S(2)}) %collective-permute-start.7) | collective-permute-done | bytes 294944 | tf_op jit(solution)/shard_map/ppermute | solution.py:173
  96.5 0.1 broadcast_select_fusion.1
  96.6 0.1 collective-permute-start.8
  96.7 8.3 %self_attention.2.self_ref = bf16[16,128,128]{2,1,0:T(8,128)(2,1)S(1)} custom-call(bf16[16,4,128,128]{3,2,1,0:T(8,128)(2,1)S(1)} %bitcast.77, bf16[16,4,128,128]{3,2,1,0:T(8,128)(2,1)S(1)} %bitcast.78, bf16[16,4,128,128]{3,2,1,0:T(8,128)(2,1)S(1)} %bitcast.79), custom_call_target="tpu_custom_call" | custom-call | flops 2147483648 | bytes 2097152 | tf_op jit(solution)/shard_map/self_attention/pallas_call | solution.py:94
  105.0 1.0 broadcast_select_fusion.2
  106.0 0.1 collective-permute-start.9
  106.1 2.3 %constant_dynamic-update-slice_fusion.1 = bf16[2048,512]{1,0:T(8,128)(2,1)} fusion(bf16[2048,256]{1,0:T(8,128)(2,1)} %param.14), kind=kLoop, calls=%fused_computation.52 | loop fusion | bytes 2097152
  108.4 7.1 %all-to-all-start.1 = ((bf16[16,512,128]{2,1,0:T(8,128)(2,1)}), bf16[16,512,128]{2,1,0:T(8,128)(2,1)}, u32[]{:S(2)}, u32[]{:S(2)}) async-start(bf16[16,512,128]{2,1,0:T(8,128)(2,1)} %bitcast.94), calls=%async_computation.1 | async-start | bytes 4194304 | tf_op jit(solution)/shard_map/all_to_all | solution.py:169
  115.5 1.9 collective-permute-start.11
  117.5 0.1 pad_maximum_fusion.3
  117.6 0.3 collective-permute-start.10
  117.8 14.0 %collective-permute-done.11 = bf16[144,1024]{1,0:T(8,128)(2,1)S(1)} collective-permute-done((bf16[144,1024]{1,0:T(8,128)(2,1)S(1)}, bf16[144,1024]{1,0:T(8,128)(2,1)S(1)}, u32[]{:S(2)}, u32[]{:S(2)}) %collective-permute-start.11) | collective-permute-done | bytes 294944 | tf_op jit(solution)/shard_map/ppermute | solution.py:173
  131.9 0.1 pad_maximum_fusion.4
  131.9 2.9 %collective-permute-start.12 = (bf16[2,144,1024]{2,1,0:T(8,128)(2,1)S(1)}, bf16[2,144,1024]{2,1,0:T(8,128)(2,1)S(1)}, u32[]{:S(2)}, u32[]{:S(2)}) collective-permute-start(bf16[2,144,1024]{2,1,0:T(8,128)(2,1)S(1)} %pad_maximum_fusion.4), channel_id=1, source_target_pairs={{0,2},{1,3},{2,0},{3,1},{4,6},{5,7},{6,4},{7,5},{8,10},{9,11},{10,... | collective-permute-start | bytes 1769480 | tf_op jit(solution)/shard_map/ppermute | solution.py:173
  134.8 0.1 constant_dynamic-update-slice_fusion
  134.9 22.2 %collective-permute-done.10 = bf16[2,144,1024]{2,1,0:T(8,128)(2,1)S(1)} collective-permute-done((bf16[2,144,1024]{2,1,0:T(8,128)(2,1)S(1)}, bf16[2,144,1024]{2,1,0:T(8,128)(2,1)S(1)}, u32[]{:S(2)}, u32[]{:S(2)}) %collective-permute-start.10) | collective-permute-done | bytes 589856 | tf_op jit(solution)/shard_map/ppermute | solution.py:173
  157.1 0.1 select_bitcast_fusion.3
  157.2 0.1 pad_maximum_fusion
  157.3 0.1 select_bitcast_fusion.1
  157.4 0.1 pad_maximum_fusion.1
  157.5 0.8 fusion.4
  158.3 0.8 convolution_add_fusion
  159.1 0.1 slice.60
  159.2 0.1 pad_select_fusion
  159.3 0.1 collective-permute-start.13
  159.4 2.6 %collective-permute-done.13 = f32[512,512]{1,0:T(8,128)S(1)} collective-permute-done((f32[512,512]{1,0:T(8,128)S(1)}, f32[512,512]{1,0:T(8,128)S(1)}, u32[]{:S(2)}, u32[]{:S(2)}) %collective-permute-start.13) | collective-permute-done | bytes 1048608 | tf_op jit(solution)/shard_map/ppermute | solution.py:177
  162.0 0.3 fusion.2.k_ref.v_ref
  162.3 4.1 %cross_attention.2 = bf16[16,128,128]{2,1,0:T(8,128)(2,1)} custom-call(s32[1]{0:T(128)S(6)} %copy.12.length_ref, bf16[16,4,128,128]{3,2,1,0:T(8,128)(2,1)S(1)} %bitcast.80, bf16[512,512]{1,0:T(8,128)(2,1)S(1)} %fusion.2.k_ref.v_ref, bf16[512,512]{1,0:T(8,128)(2,1)S(1)} %fusion.2.k_ref.v_ref, bf16[16,128,128]{2,1,0:T(8,128)(2,1)S(1)} %self_attention.2.self_ref), custom_call_target="tpu_custom_call" | custom-call | flops 536870912 | bytes 1572864 | tf_op jit(solution)/shard_map/cross_attention/pallas_call | solution.py:142
  166.4 5.6 %all-to-all-start.2 = ((bf16[16,128,128]{2,1,0:T(8,128)(2,1)}), bf16[16,128,128]{2,1,0:T(8,128)(2,1)S(1)}, u32[]{:S(2)}, u32[]{:S(2)}) async-start(bf16[16,128,128]{2,1,0:T(8,128)(2,1)} %cross_attention.2), calls=%async_computation.2 | async-start | bytes 1048576 | tf_op jit(solution)/shard_map/all_to_all | solution.py:169
  172.0 9.5 %self_attention.3.self_ref = bf16[16,128,128]{2,1,0:T(8,128)(2,1)S(1)} custom-call(bf16[16,4,128,128]{3,2,1,0:T(8,128)(2,1)} %bitcast.26.q_ref.k_ref.v_ref, bf16[16,4,128,128]{3,2,1,0:T(8,128)(2,1)} %bitcast.26.q_ref.k_ref.v_ref, bf16[16,4,128,128]{3,2,1,0:T(8,128)(2,1)} %bitcast.26.q_ref.k_ref.v_ref), custom_call_target="tpu_custom_call" | custom-call | flops 2147483648 | bytes 2097152 | tf_op jit(solution)/shard_map/self_attention/pallas_call | solution.py:94
  181.5 4.3 %cross_attention.3 = bf16[16,128,128]{2,1,0:T(8,128)(2,1)S(1)} custom-call(s32[1]{0:T(128)S(6)} %copy.12.length_ref, bf16[16,4,128,128]{3,2,1,0:T(8,128)(2,1)} %bitcast.26.q_ref.k_ref.v_ref, bf16[512,512]{1,0:T(8,128)(2,1)S(1)} %fusion.2.k_ref.v_ref, bf16[512,512]{1,0:T(8,128)(2,1)S(1)} %fusion.2.k_ref.v_ref, bf16[16,128,128]{2,1,0:T(8,128)(2,1)S(1)} %self_attention.3.self_ref), custom_call_target="tpu_custom_call" | custom-call | flops 536870912 | bytes 1572864 | tf_op jit(solution)/shard_map/cross_attention/pallas_call | solution.py:142
  185.8 1.5 all-to-all-done.2.refs_0_
  187.4 20.1 %all_to_all.20.refs_1_ = bf16[16,128,128]{2,1,0:T(8,128)(2,1)S(1)} all-to-all(bf16[16,128,128]{2,1,0:T(8,128)(2,1)S(1)} %cross_attention.3), channel_id=1, replica_groups=mesh['dp'=2,'seq'=16] {'seq'}, dimensions={0} | all-to-all | bytes 1048576 | tf_op jit(solution)/shard_map/all_to_all | solution.py:169
  207.4 1.6 unpack.1
  (33 shorter events, 0.4 us)
Async XLA Ops:
  0.0 3.8 %copy-start = (bf16[1,128,4096]{2,1,0:T(8,128)(2,1)S(1)}, bf16[1,128,4096]{2,1,0:T(8,128)(2,1)}, u32[]{:S(2)}) copy-start(bf16[1,128,4096]{2,1,0:T(8,128)(2,1)} %param.9) | copy-start | bytes 3145732
  0.0 3.8 %copy-start.1 = (bf16[1,128,4096]{2,1,0:T(8,128)(2,1)S(1)}, bf16[1,128,4096]{2,1,0:T(8,128)(2,1)}, u32[]{:S(2)}) copy-start(bf16[1,128,4096]{2,1,0:T(8,128)(2,1)} %param.10) | copy-start | bytes 3145732
  0.0 3.8 %copy-start.2 = (bf16[1,128,4096]{2,1,0:T(8,128)(2,1)S(1)}, bf16[1,128,4096]{2,1,0:T(8,128)(2,1)}, u32[]{:S(2)}) copy-start(bf16[1,128,4096]{2,1,0:T(8,128)(2,1)} %param.11) | copy-start | bytes 3145732
  0.0 3.8 %copy-start.3 = (bf16[1,128,4096]{2,1,0:T(8,128)(2,1)S(1)}, bf16[1,128,4096]{2,1,0:T(8,128)(2,1)}, u32[]{:S(2)}) copy-start(bf16[1,128,4096]{2,1,0:T(8,128)(2,1)} %param.12) | copy-start | bytes 3145732
  3.4 15.0 %collective-permute-start.1 = (bf16[512,2048]{1,0:T(8,128)(2,1)}, bf16[512,2048]{1,0:T(8,128)(2,1)}, u32[]{:S(2)}, u32[]{:S(2)}) collective-permute-start(bf16[512,2048]{1,0:T(8,128)(2,1)} %dynamic-slice_bitcast_fusion), channel_id=1, source_target_pairs={{0,16},{16,0},{1,17},{17,1},{2,18},{18,2},{3,19},{19,3},{4,20},{20... | collective-permute-start | bytes 6291464 | tf_op jit(solution)/shard_map/ppermute | solution.py:177
  6.8 61.2 %all-to-all-start = ((bf16[16,512,128]{2,1,0:T(8,128)(2,1)}), bf16[16,512,128]{2,1,0:T(8,128)(2,1)S(1)}, u32[]{:S(2)}, u32[]{:S(2)}) async-start(bf16[16,512,128]{2,1,0:T(8,128)(2,1)} %bitcast.95), calls=%async_computation | async-start | bytes 4194304 | tf_op jit(solution)/shard_map/all_to_all | solution.py:169
  16.1 1.1 collective-permute-start
  22.5 1.4 copy-start.4
  23.8 25.4 %collective-permute-start.4 = (bf16[2,144,1024]{2,1,0:T(8,128)(2,1)S(1)}, bf16[2,144,1024]{2,1,0:T(8,128)(2,1)S(1)}, u32[]{:S(2)}, u32[]{:S(2)}) collective-permute-start(bf16[2,144,1024]{2,1,0:T(8,128)(2,1)S(1)} %fusion.7), channel_id=1, source_target_pairs={{0,2},{1,3},{2,0},{3,1},{4,6},{5,7},{6,4},{7,5},{8,10},{9,11},{10,... | collective-permute-start | bytes 1769480 | tf_op jit(solution)/shard_map/ppermute | solution.py:173
  26.9 22.4 %copy-start.5 = (bf16[512,2048]{1,0:T(8,128)(2,1)S(1)}, bf16[512,2048]{1,0:T(8,128)(2,1)}, u32[]{:S(2)}) copy-start(bf16[512,2048]{1,0:T(8,128)(2,1)} %copy-done.4) | copy-start | bytes 6291460
  28.5 32.4 %collective-permute-start.2 = (bf16[2,144,1024]{2,1,0:T(8,128)(2,1)S(1)}, bf16[2,144,1024]{2,1,0:T(8,128)(2,1)S(1)}, u32[]{:S(2)}, u32[]{:S(2)}) collective-permute-start(bf16[2,144,1024]{2,1,0:T(8,128)(2,1)S(1)} %dynamic-slice_bitcast_fusion.1), channel_id=1, source_target_pairs={{0,1},{1,0},{2,3},{3,2},{4,5},{5,4},{6,7},{7,6},{8,9},{9,8},{10,11... | collective-permute-start | bytes 1769480 | tf_op jit(solution)/shard_map/ppermute | solution.py:173
  49.5 16.5 %collective-permute-start.5 = (bf16[144,1024]{1,0:T(8,128)(2,1)S(1)}, bf16[144,1024]{1,0:T(8,128)(2,1)S(1)}, u32[]{:S(2)}, u32[]{:S(2)}) collective-permute-start(bf16[144,1024]{1,0:T(8,128)(2,1)S(1)} %dynamic-slice_bitcast_fusion.2), channel_id=1, source_target_pairs={{0,1},{1,0},{2,3},{3,2},{4,5},{5,4},{6,7},{7,6},{8,9},{9,8},{10,11... | collective-permute-start | bytes 884744 | tf_op jit(solution)/shard_map/ppermute | solution.py:173
  61.0 6.8 %collective-permute-start.3 = (bf16[144,1024]{1,0:T(8,128)(2,1)S(1)}, bf16[144,1024]{1,0:T(8,128)(2,1)S(1)}, u32[]{:S(2)}, u32[]{:S(2)}) collective-permute-start(bf16[144,1024]{1,0:T(8,128)(2,1)S(1)} %dynamic-slice_bitcast_fusion.3), channel_id=1, source_target_pairs={{0,2},{1,3},{2,0},{3,1},{4,6},{5,7},{6,4},{7,5},{8,10},{9,11},{10,... | collective-permute-start | bytes 884744 | tf_op jit(solution)/shard_map/ppermute | solution.py:173
  68.0 12.6 %collective-permute-start.6 = (bf16[144,2048]{1,0:T(8,128)(2,1)S(1)}, bf16[144,2048]{1,0:T(8,128)(2,1)S(1)}, u32[]{:S(2)}, u32[]{:S(2)}) collective-permute-start(bf16[144,2048]{1,0:T(8,128)(2,1)S(1)} %pad_maximum_fusion.2), channel_id=1, source_target_pairs={{0,4},{1,5},{2,6},{3,7},{4,0},{5,1},{6,2},{7,3},{8,12},{9,13},{10,... | collective-permute-start | bytes 1769480 | tf_op jit(solution)/shard_map/ppermute | solution.py:173
  80.9 15.6 %collective-permute-start.7 = (bf16[144,1024]{1,0:T(8,128)(2,1)S(1)}, bf16[144,1024]{1,0:T(8,128)(2,1)S(1)}, u32[]{:S(2)}, u32[]{:S(2)}) collective-permute-start(bf16[144,1024]{1,0:T(8,128)(2,1)S(1)} %fusion.12), channel_id=1, source_target_pairs={{0,8},{1,9},{2,10},{3,11},{4,12},{5,13},{6,14},{7,15},{8,0},{9,1},... | collective-permute-start | bytes 884744 | tf_op jit(solution)/shard_map/ppermute | solution.py:173
  96.6 8.4 %collective-permute-start.8 = (bf16[144,1024]{1,0:T(8,128)(2,1)S(1)}, bf16[144,1024]{1,0:T(8,128)(2,1)}, u32[]{:S(2)}, u32[]{:S(2)}) collective-permute-start(bf16[144,1024]{1,0:T(8,128)(2,1)S(1)} %broadcast_select_fusion.1), channel_id=1, source_target_pairs={{0,4},{1,5},{2,6},{3,7},{4,0},{5,1},{6,2},{7,3},{8,12},{9,13},{10,... | collective-permute-start | bytes 884744 | tf_op jit(solution)/shard_map/ppermute | solution.py:173
  106.0 11.4 %collective-permute-start.9 = (bf16[144,1024]{1,0:T(8,128)(2,1)S(1)}, bf16[144,1024]{1,0:T(8,128)(2,1)S(1)}, u32[]{:S(2)}, u32[]{:S(2)}) collective-permute-start(bf16[144,1024]{1,0:T(8,128)(2,1)S(1)} %get-tuple-element.20), channel_id=1, source_target_pairs={{0,2},{1,3},{2,0},{3,1},{4,6},{5,7},{6,4},{7,5},{8,10},{9,11},{10,... | collective-permute-start | bytes 884744 | tf_op jit(solution)/shard_map/ppermute | solution.py:173
  108.4 58.0 %all-to-all-start.1 = ((bf16[16,512,128]{2,1,0:T(8,128)(2,1)}), bf16[16,512,128]{2,1,0:T(8,128)(2,1)}, u32[]{:S(2)}, u32[]{:S(2)}) async-start(bf16[16,512,128]{2,1,0:T(8,128)(2,1)} %bitcast.94), calls=%async_computation.1 | async-start | bytes 4194304 | tf_op jit(solution)/shard_map/all_to_all | solution.py:169
  115.5 16.3 %collective-permute-start.11 = (bf16[144,1024]{1,0:T(8,128)(2,1)S(1)}, bf16[144,1024]{1,0:T(8,128)(2,1)S(1)}, u32[]{:S(2)}, u32[]{:S(2)}) collective-permute-start(bf16[144,1024]{1,0:T(8,128)(2,1)S(1)} %get-tuple-element.21), channel_id=1, source_target_pairs={{0,1},{1,0},{2,3},{3,2},{4,5},{5,4},{6,7},{7,6},{8,9},{9,8},{10,11... | collective-permute-start | bytes 884744 | tf_op jit(solution)/shard_map/ppermute | solution.py:173
  117.5 17.3 %copy-start.7 = (bf16[2048,256]{1,0:T(8,128)(2,1)S(1)}, bf16[2048,256]{1,0:T(8,128)(2,1)}, u32[]{:S(2)}) copy-start(bf16[2048,256]{1,0:T(8,128)(2,1)} %param.15) | copy-start | bytes 3145732
  117.5 17.3 %copy-start.6 = (bf16[2048,512]{1,0:T(8,128)(2,1)S(1)}, bf16[2048,512]{1,0:T(8,128)(2,1)}, u32[]{:S(2)}) copy-start(bf16[2048,512]{1,0:T(8,128)(2,1)} %constant_dynamic-update-slice_fusion.1) | copy-start | bytes 6291460
  117.6 39.6 %collective-permute-start.10 = (bf16[2,144,1024]{2,1,0:T(8,128)(2,1)S(1)}, bf16[2,144,1024]{2,1,0:T(8,128)(2,1)S(1)}, u32[]{:S(2)}, u32[]{:S(2)}) collective-permute-start(bf16[2,144,1024]{2,1,0:T(8,128)(2,1)S(1)} %pad_maximum_fusion.3), channel_id=1, source_target_pairs={{0,1},{1,0},{2,3},{3,2},{4,5},{5,4},{6,7},{7,6},{8,9},{9,8},{10,11... | collective-permute-start | bytes 1769480 | tf_op jit(solution)/shard_map/ppermute | solution.py:173
  131.9 25.4 %collective-permute-start.12 = (bf16[2,144,1024]{2,1,0:T(8,128)(2,1)S(1)}, bf16[2,144,1024]{2,1,0:T(8,128)(2,1)S(1)}, u32[]{:S(2)}, u32[]{:S(2)}) collective-permute-start(bf16[2,144,1024]{2,1,0:T(8,128)(2,1)S(1)} %pad_maximum_fusion.4), channel_id=1, source_target_pairs={{0,2},{1,3},{2,0},{3,1},{4,6},{5,7},{6,4},{7,5},{8,10},{9,11},{10,... | collective-permute-start | bytes 1769480 | tf_op jit(solution)/shard_map/ppermute | solution.py:173
  159.3 2.7 %collective-permute-start.13 = (f32[512,512]{1,0:T(8,128)S(1)}, f32[512,512]{1,0:T(8,128)S(1)}, u32[]{:S(2)}, u32[]{:S(2)}) collective-permute-start(f32[512,512]{1,0:T(8,128)S(1)} %pad_select_fusion), channel_id=1, source_target_pairs={{0,16},{16,0},{1,17},{17,1},{2,18},{18,2},{3,19},{19,3},{4,20},{20... | collective-permute-start | bytes 3145736 | tf_op jit(solution)/shard_map/ppermute | solution.py:177
  166.4 21.0 %all-to-all-start.2 = ((bf16[16,128,128]{2,1,0:T(8,128)(2,1)}), bf16[16,128,128]{2,1,0:T(8,128)(2,1)S(1)}, u32[]{:S(2)}, u32[]{:S(2)}) async-start(bf16[16,128,128]{2,1,0:T(8,128)(2,1)} %cross_attention.2), calls=%async_computation.2 | async-start | bytes 1048576 | tf_op jit(solution)/shard_map/all_to_all | solution.py:169

commit v3 on v2

v3 whole, which is shorter than its diff:
```python
import functools
import math

import jax
import jax.numpy as jnp
from jax import lax
from jax.experimental import pallas as pl
from jax.experimental.pallas import tpu as pltpu
from jax.sharding import PartitionSpec as P

HEAD = 128
QUAD = 4
LOG2E = math.log2(math.e)


def params(mebibytes=48):
    return pltpu.CompilerParams(vmem_limit_bytes=mebibytes * 1024 * 1024)


def pack(arrays, n, items, part):
    rows, columns = arrays[0].shape
    width = columns // n
    per = max(1, n // 4)
    used = sorted({a for a, _ in items})

    def body(*refs):
        for i, (a, g) in enumerate(items):
            for j in range(per):
                start = j * width + g * part
                refs[-1][j, i] = refs[used.index(a)][:, start : start + part]

    return pl.pallas_call(
        body,
        grid=(n // per,),
        in_specs=[pl.BlockSpec((rows, per * width), lambda i: (0, i))] * len(used),
        out_specs=pl.BlockSpec((per, len(items), rows, part), lambda i: (i, 0, 0, 0)),
        out_shape=jax.ShapeDtypeStruct((n, len(items), rows, part), arrays[0].dtype),
        compiler_params=params(60),
        name="pack",
    )(*[arrays[a] for a in used])


def unpack(parts):
    groups = len(parts)
    n, rows, part = parts[0].shape
    width = part * groups
    per = max(1, n // 4)

    def body(*refs):
        for g in range(groups):
            for j in range(per):
                start = j * width + g * part
                refs[groups][:, start : start + part] = refs[g][j]

    return pl.pallas_call(
        body,
        grid=(n // per,),
        in_specs=[pl.BlockSpec((per, rows, part), lambda i: (i, 0, 0))] * groups,
        out_specs=pl.BlockSpec((rows, per * width), lambda i: (0, i)),
        out_shape=jax.ShapeDtypeStruct((rows, n * width), parts[0].dtype),
        compiler_params=params(),
        name="unpack",
    )(*parts)


def result_blocks(n, step, rows, turned):
    if turned:
        lines = n // QUAD
        return (lines, QUAD, rows), pl.BlockSpec(
            (lines, 1, rows, HEAD), lambda h, i, *_: (0, i, 0, h)
        )
    return (n // step, step, rows), pl.BlockSpec(
        (1, step, rows, HEAD), lambda h, i, *_: (i, 0, 0, h)
    )


def self_attention(blocks, first, turned):
    n, _, rows, width = blocks.shape
    heads = width // HEAD
    tokens = n * rows
    per = max(1, min(n, 256 // rows))
    step = n // QUAD if turned else 2 * per
    factor = LOG2E / HEAD**0.5
    shape, out_block = result_blocks(n, step, rows, turned)

    def body(q_ref, k_ref, v_ref, out_ref, values):
        @pl.when(pl.program_id(1) == 0)
        def _():
            values[:, :HEAD] = v_ref[:, 0].reshape(tokens, HEAD)
            values[:, HEAD:] = jnp.ones((tokens, HEAD), jnp.bfloat16)

        keys = k_ref[:, 0].reshape(tokens, HEAD)
        outs = []
        for part in range(step // per):
            q = q_ref[part * per : (part + 1) * per, 0].reshape(per * rows, HEAD)
            scores = lax.dot_general(
                q, keys, (((1,), (1,)), ((), ())), preferred_element_type=jnp.float32
            )
            top = jnp.max(scores, axis=1, keepdims=True)
            probs = jnp.exp2((scores - top) * factor).astype(jnp.bfloat16)
            total = jnp.dot(probs, values[...], preferred_element_type=jnp.float32)
            outs.append((total[:, :HEAD] / total[:, HEAD:]).astype(jnp.bfloat16))
        out_ref[...] = jnp.concatenate(outs).reshape(out_ref.shape)

    return pl.pallas_call(
        body,
        grid=(heads, n // step),
        in_specs=[
            pl.BlockSpec((step, 1, rows, HEAD), lambda h, i: (i, first, 0, h)),
            pl.BlockSpec((n, 1, rows, HEAD), lambda h, i: (0, first + 1, 0, h)),
            pl.BlockSpec((n, 1, rows, HEAD), lambda h, i: (0, first + 2, 0, h)),
        ],
        out_specs=out_block,
        out_shape=jax.ShapeDtypeStruct((*shape, width), jnp.bfloat16),
        scratch_shapes=[pltpu.VMEM((tokens, 2 * HEAD), jnp.bfloat16)],
        compiler_params=params(),
        cost_estimate=pl.CostEstimate(
            flops=16 * heads * tokens * tokens * HEAD,
            bytes_accessed=2 * 4 * tokens * width,
            transcendentals=heads * tokens * tokens,
        ),
        name="self_attention",
    )(blocks, blocks, blocks).reshape(n, rows, width)


def cross_attention(blocks, item, text, head, length, self_out):
    n, _, rows, width = blocks.shape
    heads = width // HEAD
    positions = text.shape[0]
    values_at = text.shape[1] // HEAD // 2 + head
    step = max(1, min(n, 512 // rows))
    factor = LOG2E / HEAD**0.5
    self_block = pl.BlockSpec((step, rows, HEAD), lambda h, i, _: (i, 0, h))

    def body(length_ref, q_ref, k_ref, v_ref, self_ref, out_ref, values):
        @pl.when(pl.program_id(1) == 0)
        def _():
            values[:, :HEAD] = v_ref[...]
            values[:, HEAD:] = jnp.ones((positions, HEAD), jnp.bfloat16)

        q = q_ref[:, 0].reshape(step * rows, HEAD)
        scores = lax.dot_general(
            q, k_ref[...], (((1,), (1,)), ((), ())), preferred_element_type=jnp.float32
        )
        place = lax.broadcasted_iota(jnp.int32, (1, positions), 1)
        scores = jnp.where(place < length_ref[0], scores, -1e30)
        top = jnp.max(scores, axis=1, keepdims=True)
        probs = jnp.exp2((scores - top) * factor).astype(jnp.bfloat16)
        total = jnp.dot(probs, values[...], preferred_element_type=jnp.float32)
        out = (total[:, :HEAD] / total[:, HEAD:]).astype(jnp.bfloat16).astype(jnp.float32)
        out = out.reshape(self_ref.shape) + self_ref[...].astype(jnp.float32)
        out_ref[...] = out.astype(jnp.bfloat16)

    return pl.pallas_call(
        body,
        grid_spec=pltpu.PrefetchScalarGridSpec(
            num_scalar_prefetch=1,
            grid=(heads, n // step),
            in_specs=[
                pl.BlockSpec((step, 1, rows, HEAD), lambda h, i, _: (i, item, 0, h)),
                pl.BlockSpec((positions, HEAD), lambda h, i, _: (0, head + h)),
                pl.BlockSpec((positions, HEAD), lambda h, i, _: (0, values_at + h)),
                self_block,
            ],
            out_specs=self_block,
            scratch_shapes=[pltpu.VMEM((positions, 2 * HEAD), jnp.bfloat16)],
        ),
        out_shape=jax.ShapeDtypeStruct((n, rows, width), jnp.bfloat16),
        compiler_params=params(),
        cost_estimate=pl.CostEstimate(
            flops=32 * heads * n * rows * positions * HEAD,
            bytes_accessed=2 * 3 * n * rows * width,
            transcendentals=heads * n * rows * positions,
        ),
        name="cross_attention",
    )(length, blocks, text, text, self_out)


def spread(blocks, groups=None):
    flat = blocks.reshape(blocks.shape[0], -1, blocks.shape[-1])
    return lax.all_to_all(
        flat, "seq", split_axis=0, concat_axis=0, tiled=True, axis_index_groups=groups
    ).reshape(blocks.shape)


def spread_lines(blocks):
    n = blocks.shape[0]
    return spread(blocks, [[q + QUAD * z for z in range(n // QUAD)] for q in range(QUAD)])


def spread_planes(blocks):
    n = blocks.shape[0]
    shape = blocks.shape[1:]
    turned = blocks.reshape(n // QUAD, QUAD, *shape).swapaxes(0, 1).reshape(n, *shape)
    return spread(turned, [[QUAD * z + q for q in range(QUAD)] for z in range(n // QUAD)])


def exchange(value, apart, n):
    return lax.ppermute(value, "seq", [(i, i ^ apart) for i in range(n)])


def pick(value, index):
    return lax.dynamic_index_in_dim(value, index, 0, keepdims=False)


def swap(value):
    return lax.ppermute(value, "dp", [(0, 1), (1, 0)])


def quarters(embed, other, where):
    positions, columns = embed.shape
    rows_long, rows_short = positions // 4, positions // 32
    rows = rows_long + rows_short
    half, part = columns // 2, columns // 4

    def body(where_ref, own_ref, other_ref, send_a, keep_a, send_b, keep_b):
        x, y = where_ref[2] & 1, where_ref[2] >> 1

        def fill(long_ref, short_ref):
            for i in range(2):
                for ref, place, first in (
                    (send_a, 2 * i + 1 - x, 0),
                    (keep_a, 2 * i + x, 0),
                    (send_b, 2 * (1 - y) + i, part),
                    (keep_b, 2 * y + i, part),
                ):
                    across = slice(first, first + part)
                    at_long = pl.ds(pl.multiple_of(place * rows_long, rows_long), rows_long)
                    at_short = pl.ds(pl.multiple_of(place * rows_short, rows_short), rows_short)
                    ref[i, :rows_long] = long_ref[at_long, across]
                    ref[i, rows_long:] = short_ref[at_short, across]

        @pl.when(where_ref[1] == 1)
        def _():
            fill(own_ref, other_ref)

        @pl.when(where_ref[1] == 0)
        def _():
            fill(other_ref, own_ref)

    return pl.pallas_call(
        body,
        grid_spec=pltpu.PrefetchScalarGridSpec(
            num_scalar_prefetch=1,
            grid=(1,),
            in_specs=[pl.BlockSpec((positions, half), lambda i, w: (0, w[0]))] * 2,
            out_specs=[pl.BlockSpec((2, rows, part), lambda i, w: (0, 0, 0))] * 4,
        ),
        out_shape=[jax.ShapeDtypeStruct((2, rows, part), embed.dtype)] * 4,
        compiler_params=params(),
        name="quarters",
    )(where, embed, other)


def project(pieces, key_weight, value_weight, where, positions):
    rows, columns = pieces[0].shape
    width = key_weight.shape[1]
    half = columns // 2
    rows_long, rows_short = positions // 4, positions // 32

    def body(where_ref, *refs):
        piece_refs, (key_ref, value_ref, mine_ref, sent_ref) = refs[:5], refs[5:]
        halves = [(ref[:, :half], ref[:, half:]) for ref in piece_refs[:3]]
        halves.append((piece_refs[3][...], piece_refs[4][...]))

        def fill(long_ref, short_ref):
            short_ref[4 * rows_short :] = jnp.zeros(
                (positions - 4 * rows_short, 2 * width), jnp.float32
            )
            near = where_ref[2]
            first = pl.ds(pl.multiple_of(near * half, half), half)
            second = pl.ds(pl.multiple_of((1 - near) * half, half), half)
            for i, (left, right) in enumerate(halves):
                place = where_ref[0] ^ i
                at_long = pl.ds(pl.multiple_of(place * rows_long, rows_long), rows_long)
                at_short = pl.ds(pl.multiple_of(place * rows_short, rows_short), rows_short)
                for j, ref in enumerate((key_ref, value_ref)):
                    sums = jnp.dot(left, ref[first], preferred_element_type=jnp.float32)
                    sums += jnp.dot(right, ref[second], preferred_element_type=jnp.float32)
                    across = slice(j * width, (j + 1) * width)
                    long_ref[at_long, across] = sums[:rows_long]
                    short_ref[at_short, across] = sums[rows_long:]

        @pl.when(where_ref[1] == 1)
        def _():
            fill(mine_ref, sent_ref)

        @pl.when(where_ref[1] == 0)
        def _():
            fill(sent_ref, mine_ref)

    def whole(*shape):
        return pl.BlockSpec(shape, lambda i, w: (0, 0))

    return pl.pallas_call(
        body,
        grid_spec=pltpu.PrefetchScalarGridSpec(
            num_scalar_prefetch=1,
            grid=(1,),
            in_specs=[whole(rows, columns)] * 3
            + [whole(rows, half)] * 2
            + [whole(columns, width)] * 2,
            out_specs=[whole(positions, 2 * width)] * 2,
        ),
        out_shape=[jax.ShapeDtypeStruct((positions, 2 * width), jnp.float32)] * 2,
        compiler_params=params(),
        name="project",
    )(where, *pieces, key_weight, value_weight)


def text_of_pair(embed, key_weight, value_weight, length, encoder, n, before, between, after):
    positions, columns = embed.shape
    core = lax.axis_index("dp")
    me = lax.axis_index("seq")
    half = columns // 2
    other = swap(embed)
    other_facts = swap(jnp.stack([length, encoder]))
    mine_long = length > other_facts[0]
    encoder_long = jnp.where(mine_long, encoder, other_facts[1])
    encoder_short = jnp.where(mine_long, other_facts[1], encoder)
    rows_long, rows_short = positions // 4, positions // 32
    rows = rows_long + rows_short
    place = me & 3
    is_long = mine_long.astype(jnp.int32)
    send_a, part_a, send_b, part_b = quarters(embed, other, jnp.stack([core, is_long, place]))
    on_row = lax.broadcasted_iota(jnp.int32, (rows, 1), 0)
    apart = jnp.where(on_row < rows_long, encoder_long, encoder_short) ^ me
    x, y = me & 1, (me >> 1) & 1

    def choose(own, got, bit):
        return jnp.where((apart >> bit) & 1 == 0, own, got)

    part_a = choose(part_a, exchange(send_a, 1, n), 0)
    part_b = choose(part_b, exchange(send_b, 2, n), 1)
    got_a = exchange(pick(part_a, 1 - y), 2, n)
    got_b = exchange(pick(part_b, 1 - x), 1, n)
    piece = jnp.concatenate(
        [choose(pick(part_a, y), got_a, 1), choose(pick(part_b, x), got_b, 0)], axis=1
    )
    piece = before(piece)
    last = n.bit_length() - 2
    for bit in range(2, last):
        piece = choose(piece, exchange(piece, 1 << bit, n), bit)
    near = (me >> 2) & 1
    own = jnp.where(near == 0, piece[:, : half // 2], piece[:, half // 2 :])
    own = choose(own, exchange(own, 1 << last, n), last)
    piece = between(jnp.concatenate([own, exchange(own, 4, n)], axis=1))
    got_x, got_y = exchange(piece, 1, n), after(exchange(piece, 2, n))
    across_a = exchange(got_y[:, : half // 2], 1, n)
    across_b = exchange(got_x[:, half // 2 :], 2, n)
    pieces = [piece, got_x, got_y, across_a, across_b]
    mine, other_sums = project(
        pieces, key_weight, value_weight, jnp.stack([place, is_long, near]), positions
    )
    return (mine + swap(other_sums)).astype(jnp.bfloat16)


def text_of_clip(embed, key_weight, value_weight, encoder):
    kept = jnp.where(lax.axis_index("seq") == encoder, embed, 0).astype(embed.dtype)
    prompt = lax.psum(kept, "seq")
    weight = lax.all_gather(
        jnp.concatenate([key_weight, value_weight], axis=1), "dp", axis=0, tiled=True
    )
    return jnp.dot(prompt, weight, preferred_element_type=jnp.float32).astype(jnp.bfloat16)


def shards(
    n_dp,
    n,
    self_query,
    self_key,
    self_value,
    cross_query,
    text_embed,
    cross_key_weight,
    cross_value_weight,
    text_lengths,
    encoder_index,
):
    heads = cross_key_weight.shape[1] // HEAD
    inputs = [self_query[0], self_key[0], self_value[0], cross_query[0]]
    embed, weights = text_embed[0, 0], (cross_key_weight, cross_value_weight)
    if n_dp != 2 or n < 16 or n & (n - 1) or heads % 2:
        blocks = spread(pack(inputs, n, [(a, 0) for a in range(4)], heads * HEAD))
        text = text_of_clip(embed, *weights, encoder_index[0])
        self_out = self_attention(blocks, 0, False)
        out = cross_attention(blocks, 3, text, 0, text_lengths, self_out)
        return unpack([spread(out)])[None]

    part = heads // 2 * HEAD
    lines = spread_lines(pack(inputs, n, [(0, 0), (1, 0), (2, 0)], part))
    rest = pack(inputs, n, [(3, 0), (0, 1), (1, 1), (2, 1), (3, 1)], part)
    self_first = later = None

    def before(piece):
        nonlocal lines, self_first
        lines, piece = lax.optimization_barrier((lines, piece))
        self_first = self_attention(spread_planes(lines), 0, True)
        return piece

    def between(piece):
        nonlocal rest, later
        piece, rest = lax.optimization_barrier((piece, rest))
        later = spread(rest)
        return piece

    def after(piece):
        nonlocal self_first
        piece, self_first = lax.optimization_barrier((piece, self_first))
        return piece

    text = text_of_pair(
        embed, *weights, text_lengths[0], encoder_index[0], n, before, between, after
    )
    out = cross_attention(later, 0, text, 0, text_lengths, self_first)
    tokens = spread(out)
    later, out = lax.optimization_barrier((later, out))
    self_second = self_attention(later, 1, False)
    out = cross_attention(later, 4, text, heads // 2, text_lengths, self_second)
    tokens, out = lax.optimization_barrier((tokens, out))
    return unpack([tokens, spread(out)])[None]


def solution(mesh):
    placed = (
        P("dp", "seq", None),
        P("dp", "seq", None),
        P("dp", "seq", None),
        P("dp", "seq", None),
        P("dp", "seq", None, None),
        P("dp", "seq"),
        P("dp", "seq"),
        P("dp"),
        P("dp"),
    )
    return jax.shard_map(
        functools.partial(shards, mesh.shape["dp"], mesh.shape["seq"]),
        mesh=mesh,
        in_specs=placed,
        out_specs=P("dp", "seq", None),
        check_vma=False,
    )
```

time: 210 us -> 201 us (0.957)
  Pallas kernels: 30.8 us -> 39.5 us
  waiting for transfers between devices: 98.9 us -> 91.4 us
  other arithmetic: 8.65 us -> 1.29 us
    ppermute x11, waiting for transfers between devices: 93.8 us -> 78.4 us  [exchange(): return lax.ppermute(value, 'seq', [(i, i ^ apart) for i in range(n)])]
    all_to_all x3 -> x4, waiting for transfers between devices: 1.52 us -> 10.4 us  [spread(): lax.all_to_all(flat, 'seq', split_axis=0, concat_axis=0, tiled=True, axis...]
    pallas_call x0 -> x2, Pallas kernels: none -> 6.23 us  [the longest x1 3.31 us: project(): pl.pallas_call(body, grid_spec=pltpu.PrefetchScalarGridSpec(num_scalar_pr...]
    select_n x14 -> x7, other arithmetic: 6.01 us -> 0.69 us  [the longest x6 0.65 us: choose(): return jnp.where(apart >> bit & 1 == 0, own, got)]
    pallas_call x1 -> x2, Pallas kernels: 2.97 us -> 8.29 us  [pack(): pl.pallas_call(body, grid=(n // per,), in_specs=[pl.BlockSpec((rows, per...]
    dynamic_slice x1 -> x0, local copies, waits for them, and re-layouts: 3.36 us -> none  [text_of_pair(): sent_half = lax.dynamic_slice_in_dim(embed, (1 - core) * half, half, 1)]
    transpose x0 -> x1, local copies, waits for them, and re-layouts: none -> 2.73 us  [spread_planes(): blocks.reshape(n // QUAD, QUAD, *shape).swapaxes(0, 1).reshape(n, *shape)]
    unnamed x17 -> x18, local copies, waits for them, and re-layouts: 3.66 us -> 5.36 us
  transfers between devices with their start and end apart: 17 -> 18, of which waited for: 11 -> 13; matrix products, arithmetic and copies ran while one was open for 6% -> 2% of each run, Pallas kernels for 14% -> 17%
where the time goes in v3:
time: 201 us; the launch traced here: 200 us
  waiting for transfers between devices  91.4 us (45%)
  Pallas kernels  39.5 us (20%)
  starting transfers between devices  36.5 us (18%)
  blocking collectives  18.9 us (9%)
  local copies, waits for them, and re-layouts  8.77 us (4%)
  between operations  3.58 us (2%)
    ppermute x11, waiting for transfers between devices, exchange(): return lax.ppermute(value, 'seq', [(i, i ^ apart) for i in range(n)])  78.4 us
    all_to_all x4, starting transfers between devices, spread(): lax.all_to_all(flat, 'seq', split_axis=0, concat_axis=0, tiled=True, axis...  20.7 us
    all_to_all x1, blocking collectives, spread(): lax.all_to_all(flat, 'seq', split_axis=0, concat_axis=0, tiled=True, axis...  18.9 us
    pallas_call x2, Pallas kernels, self_attention(): pl.pallas_call(body, grid=(heads, n // step), in_specs=[pl.BlockSpec((ste...  16.6 us
    ppermute x11, starting transfers between devices, exchange(): return lax.ppermute(value, 'seq', [(i, i ^ apart) for i in range(n)])  15.1 us
    all_to_all x4, waiting for transfers between devices, spread(): lax.all_to_all(flat, 'seq', split_axis=0, concat_axis=0, tiled=True, axis...  10.4 us
    pallas_call x2, Pallas kernels, pack(): pl.pallas_call(body, grid=(n // per,), in_specs=[pl.BlockSpec((rows, per...  8.29 us
    pallas_call x2, Pallas kernels, cross_attention(): pl.pallas_call(body, grid_spec=pltpu.PrefetchScalarGridSpec(num_scalar_pr...  6.8 us
  transfers between devices with their start and end apart: 18, of which 13 were waited for; matrix products, arithmetic and copies ran while one was open for 2% of the time, Pallas kernels for 17%

profile of v3, /device:TPU:0, one launch (start us, length us, event | category | flops | bytes accessed | tf_op | source)
XLA Modules:
  0.0 199.9 jit_solution(7664896172769460942)
XLA Ops:
  0.0 0.5 collective-permute-start.1
  1.8 0.1 pad_add_fusion
  1.8 0.1 collective-permute-start
  1.9 3.9 %pack.2 = bf16[16,3,128,128]{3,2,1,0:T(8,128)(2,1)} custom-call(bf16[128,4096]{1,0:T(8,128)(2,1)} %bitcast.44, bf16[128,4096]{1,0:T(8,128)(2,1)} %bitcast.46, bf16[128,4096]{1,0:T(8,128)(2,1)} %bitcast.48), custom_call_target="tpu_custom_call" | custom-call | tf_op jit(solution)/shard_map/pack/pallas_call | solution.py:32
  5.8 6.3 %all-to-all-start = ((bf16[16,384,128]{2,1,0:T(8,128)(2,1)}), bf16[16,384,128]{2,1,0:T(8,128)(2,1)}, u32[]{:S(2)}, u32[]{:S(2)}) async-start(bf16[16,384,128]{2,1,0:T(8,128)(2,1)} %bitcast.41), calls=%async_computation | async-start | bytes 3145728 | tf_op jit(solution)/shard_map/all_to_all | solution.py:181
  12.1 0.0 collective-permute-done
  12.1 0.6 fusion.1
  13.4 0.1 pad_add_fusion.1.where_ref
  13.5 0.0 collective-permute-done.1.other_ref
  13.5 2.9 %quarters.1 = (bf16[2,144,1024]{2,1,0:T(8,128)(2,1)S(1)}, bf16[2,144,1024]{2,1,0:T(8,128)(2,1)S(1)}, bf16[2,144,1024]{2,1,0:T(8,128)(2,1)S(1)}, bf16[2,144,1024]{2,1,0:T(8,128)(2,1)S(1)}) custom-call(s32[3]{0:T(128)S(1)} %pad_add_fusion.1.where_ref, bf16[512,4096]{1,0:T(8,128)(2,1)} %bitcast.43, bf16[512,4096]{1,0:T(8,128)(2,1)} %collective-permute-done.1.other_ref), custom_call_target="tpu_custom_call" | custom-call | tf_op jit(solution)/shard_map/quarters/pallas_call | solution.py:241
  16.4 1.6 collective-permute-start.2
  19.3 1.6 collective-permute-start.4
  20.9 10.6 %collective-permute-done.2 = bf16[2,144,1024]{2,1,0:T(8,128)(2,1)S(1)} collective-permute-done((bf16[2,144,1024]{2,1,0:T(8,128)(2,1)S(1)}, bf16[2,144,1024]{2,1,0:T(8,128)(2,1)S(1)}, u32[]{:S(2)}, u32[]{:S(2)}) %collective-permute-start.2) | collective-permute-done | bytes 589856 | tf_op jit(solution)/shard_map/ppermute | solution.py:199
  31.5 0.1 broadcast_select_fusion.1
  31.6 1.6 collective-permute-start.3
  33.2 1.5 collective-permute-done.4
  34.7 0.1 broadcast_select_fusion
  34.9 0.1 collective-permute-start.5
  35.0 5.4 %collective-permute-done.3 = bf16[144,1024]{1,0:T(8,128)(2,1)S(1)} collective-permute-done((bf16[144,1024]{1,0:T(8,128)(2,1)S(1)}, bf16[144,1024]{1,0:T(8,128)(2,1)S(1)}, u32[]{:S(2)}, u32[]{:S(2)}) %collective-permute-start.3) | collective-permute-done | bytes 294944 | tf_op jit(solution)/shard_map/ppermute | solution.py:199
  40.4 0.1 bitcast_select_fusion.1
  40.5 1.3 collective-permute-done.5
  41.7 0.1 bitcast_select_fusion
  41.9 7.5 %all-to-all-done = bf16[16,384,128]{2,1,0:T(8,128)(2,1)} async-done(((bf16[16,384,128]{2,1,0:T(8,128)(2,1)}), bf16[16,384,128]{2,1,0:T(8,128)(2,1)}, u32[]{:S(2)}, u32[]{:S(2)}) %all-to-all-start) | async-done | bytes 1572896 | tf_op jit(solution)/shard_map/all_to_all | solution.py:181
  49.4 2.7 %copy.10 = bf16[4,4,3,128,128]{4,3,2,1,0:T(8,128)(2,1)} copy(bf16[4,4,3,128,128]{4,3,2,0,1:T(8,128)(2,1)} %bitcast.19) | data formatting | bytes 3145728 | tf_op jit(solution)/shard_map/transpose | solution.py:194
  52.1 3.7 %all-to-all-start.2 = ((bf16[16,384,128]{2,1,0:T(8,128)(2,1)}), bf16[16,384,128]{2,1,0:T(8,128)(2,1)S(1)}, u32[]{:S(2)}, u32[]{:S(2)}) async-start(bf16[16,384,128]{2,1,0:T(8,128)(2,1)} %bitcast.20), calls=%async_computation.2 | async-start | bytes 3145728 | tf_op jit(solution)/shard_map/all_to_all | solution.py:181
  55.8 7.9 %collective-permute-done.6 = bf16[144,2048]{1,0:T(8,128)(2,1)S(1)} collective-permute-done((bf16[144,2048]{1,0:T(8,128)(2,1)S(1)}, bf16[144,2048]{1,0:T(8,128)(2,1)S(1)}, u32[]{:S(2)}, u32[]{:S(2)}) %collective-permute-start.6) | collective-permute-done | bytes 589856 | tf_op jit(solution)/shard_map/ppermute | solution.py:199
  63.7 0.1 broadcast_select_fusion.2
  63.9 0.1 collective-permute-start.7
  64.0 14.2 %collective-permute-done.7 = bf16[144,1024]{1,0:T(8,128)(2,1)S(1)} collective-permute-done((bf16[144,1024]{1,0:T(8,128)(2,1)S(1)}, bf16[144,1024]{1,0:T(8,128)(2,1)S(1)}, u32[]{:S(2)}, u32[]{:S(2)}) %collective-permute-start.7) | collective-permute-done | bytes 294944 | tf_op jit(solution)/shard_map/ppermute | solution.py:199
  78.2 0.1 broadcast_select_fusion.3
  78.3 0.1 collective-permute-start.8
  78.4 4.4 %pack.3 = bf16[16,5,128,128]{3,2,1,0:T(8,128)(2,1)} custom-call(bf16[128,4096]{1,0:T(8,128)(2,1)} %bitcast.45, bf16[128,4096]{1,0:T(8,128)(2,1)} %bitcast.47, bf16[128,4096]{1,0:T(8,128)(2,1)} %bitcast.49, bf16[128,4096]{1,0:T(8,128)(2,1)} %bitcast.50), custom_call_target="tpu_custom_call" | custom-call | tf_op jit(solution)/shard_map/pack/pallas_call | solution.py:32
  82.8 4.5 %collective-permute-done.8 = bf16[144,1024]{1,0:T(8,128)(2,1)S(1)} collective-permute-done((bf16[144,1024]{1,0:T(8,128)(2,1)S(1)}, bf16[144,1024]{1,0:T(8,128)(2,1)S(1)}, u32[]{:S(2)}, u32[]{:S(2)}) %collective-permute-start.8) | collective-permute-done | bytes 294944 | tf_op jit(solution)/shard_map/ppermute | solution.py:199
  87.4 0.0 all-to-all-done.2
  87.4 1.1 copy-done
  88.5 4.1 %all-to-all-start.1 = ((bf16[16,640,128]{2,1,0:T(8,128)(2,1)}), bf16[16,640,128]{2,1,0:T(8,128)(2,1)S(1)}, u32[]{:S(2)}, u32[]{:S(2)}) async-start(bf16[16,640,128]{2,1,0:T(8,128)(2,1)} %bitcast.40), calls=%async_computation.1 | async-start | bytes 5242880 | tf_op jit(solution)/shard_map/all_to_all | solution.py:181
  92.6 1.9 collective-permute-start.10
  94.6 1.5 collective-permute-start.9
  96.0 1.4 copy-done.1
  97.4 8.3 %self_attention.2 = bf16[4,4,128,128]{3,2,1,0:T(8,128)(2,1)S(1)} custom-call(bf16[16,3,128,128]{3,2,1,0:T(8,128)(2,1)S(1)} %bitcast.35, bf16[16,3,128,128]{3,2,1,0:T(8,128)(2,1)S(1)} %bitcast.36, bf16[16,3,128,128]{3,2,1,0:T(8,128)(2,1)S(1)} %bitcast.37), custom_call_target="tpu_custom_call" | custom-call | flops 8589934592 | bytes 2097152 | tf_op jit(solution)/shard_map/self_attention/pallas_call | solution.py:105
  105.8 0.0 copy-start.7
  105.8 0.0 copy-start.2
  105.8 22.0 %collective-permute-done.10.refs_2_ = bf16[144,2048]{1,0:T(8,128)(2,1)S(1)} collective-permute-done((bf16[144,2048]{1,0:T(8,128)(2,1)S(1)}, bf16[144,2048]{1,0:T(8,128)(2,1)S(1)}, u32[]{:S(2)}, u32[]{:S(2)}) %collective-permute-start.10) | collective-permute-done | bytes 589856 | tf_op jit(solution)/shard_map/ppermute | solution.py:199
  127.8 4.2 %collective-permute-start.11 = (bf16[144,1024]{1,0:T(8,128)(2,1)S(1)}, bf16[144,1024]{1,0:T(8,128)(2,1)S(1)}, u32[]{:S(2)}, u32[]{:S(2)}) collective-permute-start(bf16[144,1024]{1,0:T(8,128)(2,1)S(1)} %slice.23), channel_id=1, source_target_pairs={{0,1},{1,0},{2,3},{3,2},{4,5},{5,4},{6,7},{7,6},{8,9},{9,8},{10,11... | collective-permute-start | bytes 884744 | tf_op jit(solution)/shard_map/ppermute | solution.py:199
  132.0 2.5 %collective-permute-start.12 = (bf16[144,1024]{1,0:T(8,128)(2,1)S(1)}, bf16[144,1024]{1,0:T(8,128)(2,1)S(1)}, u32[]{:S(2)}, u32[]{:S(2)}) collective-permute-start(bf16[144,1024]{1,0:T(8,128)(2,1)S(1)} %slice.27), channel_id=1, source_target_pairs={{0,2},{1,3},{2,0},{3,1},{4,6},{5,7},{6,4},{7,5},{8,10},{9,11},{10,... | collective-permute-start | bytes 884744 | tf_op jit(solution)/shard_map/ppermute | solution.py:199
  134.6 0.1 pad_add_fusion.2.where_ref
  134.6 2.6 %collective-permute-done.11.refs_3_ = bf16[144,1024]{1,0:T(8,128)(2,1)S(1)} collective-permute-done((bf16[144,1024]{1,0:T(8,128)(2,1)S(1)}, bf16[144,1024]{1,0:T(8,128)(2,1)S(1)}, u32[]{:S(2)}, u32[]{:S(2)}) %collective-permute-start.11) | collective-permute-done | bytes 294944 | tf_op jit(solution)/shard_map/ppermute | solution.py:199
  137.2 8.4 %collective-permute-done.12.refs_4_ = bf16[144,1024]{1,0:T(8,128)(2,1)S(1)} collective-permute-done((bf16[144,1024]{1,0:T(8,128)(2,1)S(1)}, bf16[144,1024]{1,0:T(8,128)(2,1)S(1)}, u32[]{:S(2)}, u32[]{:S(2)}) %collective-permute-start.12) | collective-permute-done | bytes 294944 | tf_op jit(solution)/shard_map/ppermute | solution.py:199
  145.6 3.3 %project.1 = (f32[512,512]{1,0:T(8,128)S(1)}, f32[512,512]{1,0:T(8,128)S(1)}) custom-call(s32[3]{0:T(128)S(1)} %pad_add_fusion.2.where_ref, bf16[144,2048]{1,0:T(8,128)(2,1)S(1)} %pad_maximum_fusion.1.refs_0_, bf16[144,2048]{1,0:T(8,128)(2,1)S(1)} %collective-permute-done.9.refs_1_, bf16[144,2048]{1,0:T(8,128)(2,1)S(1)} %collective-permute-done.10.refs_2_, ...), custom_call_target="tpu_custom_call" | custom-call | tf_op jit(solution)/shard_map/project/pallas_call | solution.py:295
  148.9 0.1 collective-permute-start.13
  149.0 2.6 %collective-permute-done.13 = f32[512,512]{1,0:T(8,128)S(1)} collective-permute-done((f32[512,512]{1,0:T(8,128)S(1)}, f32[512,512]{1,0:T(8,128)S(1)}, u32[]{:S(2)}, u32[]{:S(2)}) %collective-permute-start.13) | collective-permute-done | bytes 1048608 | tf_op jit(solution)/shard_map/ppermute | solution.py:207
  151.7 0.3 add_convert_fusion.k_ref.v_ref
  151.9 0.0 copy-start.8
  152.0 1.2 copy-done.8
  153.2 3.4 %cross_attention.2 = bf16[16,128,128]{2,1,0:T(8,128)(2,1)S(1)} custom-call(s32[1]{0:T(128)S(6)} %copy.11.length_ref, bf16[16,5,128,128]{3,2,1,0:T(8,128)(2,1)S(1)} %bitcast.30, bf16[512,512]{1,0:T(8,128)(2,1)S(1)} %add_convert_fusion.k_ref.v_ref, bf16[512,512]{1,0:T(8,128)(2,1)S(1)} %add_convert_fusion.k_ref.v_ref, bf16[16,128,128]{2,1,0:T(8,128)(2,1)S(1)} %bitcast.38), custom_call_target="tpu_custom_call" | custom-call | flops 4294967296 | bytes 1572864 | tf_op jit(solution)/shard_map/cross_attention/pallas_call | solution.py:154
  156.6 0.0 copy-start.5
  156.6 0.8 copy-done.5
  157.4 6.6 %all-to-all-start.3 = ((bf16[16,128,128]{2,1,0:T(8,128)(2,1)}), bf16[16,128,128]{2,1,0:T(8,128)(2,1)S(1)}, u32[]{:S(2)}, u32[]{:S(2)}) async-start(bf16[16,128,128]{2,1,0:T(8,128)(2,1)} %copy-done.5), calls=%async_computation.3 | async-start | bytes 1048576 | tf_op jit(solution)/shard_map/all_to_all | solution.py:181
  164.0 8.3 %self_attention.3 = bf16[4,4,128,128]{3,2,1,0:T(8,128)(2,1)S(1)} custom-call(bf16[16,5,128,128]{3,2,1,0:T(8,128)(2,1)S(1)} %bitcast.31, bf16[16,5,128,128]{3,2,1,0:T(8,128)(2,1)S(1)} %bitcast.32, bf16[16,5,128,128]{3,2,1,0:T(8,128)(2,1)S(1)} %bitcast.33), custom_call_target="tpu_custom_call" | custom-call | flops 8589934592 | bytes 2097152 | tf_op jit(solution)/shard_map/self_attention/pallas_call | solution.py:105
  172.3 3.4 %cross_attention.3 = bf16[16,128,128]{2,1,0:T(8,128)(2,1)S(1)} custom-call(s32[1]{0:T(128)S(6)} %copy.11.length_ref, bf16[16,5,128,128]{3,2,1,0:T(8,128)(2,1)S(1)} %bitcast.34, bf16[512,512]{1,0:T(8,128)(2,1)S(1)} %copy-done.4, bf16[512,512]{1,0:T(8,128)(2,1)S(1)} %copy-done.4, bf16[16,128,128]{2,1,0:T(8,128)(2,1)S(1)} %bitcast.39), custom_call_target="tpu_custom_call" | custom-call | flops 4294967296 | bytes 1572864 | tf_op jit(solution)/shard_map/cross_attention/pallas_call | solution.py:154
  175.7 0.8 copy-done.6
  176.5 2.9 %all-to-all-done.3.refs_0_ = bf16[16,128,128]{2,1,0:T(8,128)(2,1)S(1)} async-done(((bf16[16,128,128]{2,1,0:T(8,128)(2,1)}), bf16[16,128,128]{2,1,0:T(8,128)(2,1)S(1)}, u32[]{:S(2)}, u32[]{:S(2)}) %all-to-all-start.3) | async-done | bytes 524320 | tf_op jit(solution)/shard_map/all_to_all | solution.py:181
  179.4 18.9 %all_to_all.25.refs_1_ = bf16[16,128,128]{2,1,0:T(8,128)(2,1)S(1)} all-to-all(bf16[16,128,128]{2,1,0:T(8,128)(2,1)} %copy-done.6), channel_id=1, replica_groups=mesh['dp'=2,'seq'=16] {'seq'}, dimensions={0} | all-to-all | bytes 1048576 | tf_op jit(solution)/shard_map/all_to_all | solution.py:181
  198.3 1.6 unpack.1
  (23 shorter events, 0.3 us)
Async XLA Ops:
  0.0 13.5 %collective-permute-start.1 = (bf16[512,4096]{1,0:T(8,128)(2,1)}, bf16[512,4096]{1,0:T(8,128)(2,1)}, u32[]{:S(2)}, u32[]{:S(2)}) collective-permute-start(bf16[512,4096]{1,0:T(8,128)(2,1)} %bitcast.42), channel_id=1, source_target_pairs={{0,16},{16,0},{1,17},{17,1},{2,18},{18,2},{3,19},{19,3},{4,20},{20... | collective-permute-start | bytes 12582920 | tf_op jit(solution)/shard_map/ppermute | solution.py:207
  1.8 10.3 %collective-permute-start = (s32[2]{0:T(128)S(1)}, s32[2]{0:T(128)S(1)}, u32[]{:S(2)}, u32[]{:S(2)}) collective-permute-start(s32[2]{0:T(128)S(1)} %pad_add_fusion), channel_id=1, source_target_pairs={{0,16},{16,0},{1,17},{17,1},{2,18},{18,2},{3,19},{19,3},{4,20},{20... | collective-permute-start | bytes 32 | tf_op jit(solution)/shard_map/ppermute | solution.py:207
  5.8 43.6 %all-to-all-start = ((bf16[16,384,128]{2,1,0:T(8,128)(2,1)}), bf16[16,384,128]{2,1,0:T(8,128)(2,1)}, u32[]{:S(2)}, u32[]{:S(2)}) async-start(bf16[16,384,128]{2,1,0:T(8,128)(2,1)} %bitcast.41), calls=%async_computation | async-start | bytes 3145728 | tf_op jit(solution)/shard_map/all_to_all | solution.py:181
  16.4 15.1 %collective-permute-start.2 = (bf16[2,144,1024]{2,1,0:T(8,128)(2,1)S(1)}, bf16[2,144,1024]{2,1,0:T(8,128)(2,1)S(1)}, u32[]{:S(2)}, u32[]{:S(2)}) collective-permute-start(bf16[2,144,1024]{2,1,0:T(8,128)(2,1)S(1)} %get-tuple-element.21), channel_id=1, source_target_pairs={{0,1},{1,0},{2,3},{3,2},{4,5},{5,4},{6,7},{7,6},{8,9},{9,8},{10,11... | collective-permute-start | bytes 1769480 | tf_op jit(solution)/shard_map/ppermute | solution.py:199
  19.3 15.5 %collective-permute-start.4 = (bf16[2,144,1024]{2,1,0:T(8,128)(2,1)S(1)}, bf16[2,144,1024]{2,1,0:T(8,128)(2,1)S(1)}, u32[]{:S(2)}, u32[]{:S(2)}) collective-permute-start(bf16[2,144,1024]{2,1,0:T(8,128)(2,1)S(1)} %get-tuple-element.23), channel_id=1, source_target_pairs={{0,2},{1,3},{2,0},{3,1},{4,6},{5,7},{6,4},{7,5},{8,10},{9,11},{10,... | collective-permute-start | bytes 1769480 | tf_op jit(solution)/shard_map/ppermute | solution.py:199
  31.6 8.7 %collective-permute-start.3 = (bf16[144,1024]{1,0:T(8,128)(2,1)S(1)}, bf16[144,1024]{1,0:T(8,128)(2,1)S(1)}, u32[]{:S(2)}, u32[]{:S(2)}) collective-permute-start(bf16[144,1024]{1,0:T(8,128)(2,1)S(1)} %dynamic-slice_bitcast_fusion.1), channel_id=1, source_target_pairs={{0,2},{1,3},{2,0},{3,1},{4,6},{5,7},{6,4},{7,5},{8,10},{9,11},{10,... | collective-permute-start | bytes 884744 | tf_op jit(solution)/shard_map/ppermute | solution.py:199
  34.9 6.8 %collective-permute-start.5 = (bf16[144,1024]{1,0:T(8,128)(2,1)S(1)}, bf16[144,1024]{1,0:T(8,128)(2,1)S(1)}, u32[]{:S(2)}, u32[]{:S(2)}) collective-permute-start(bf16[144,1024]{1,0:T(8,128)(2,1)S(1)} %dynamic-slice_bitcast_fusion), channel_id=1, source_target_pairs={{0,1},{1,0},{2,3},{3,2},{4,5},{5,4},{6,7},{7,6},{8,9},{9,8},{10,11... | collective-permute-start | bytes 884744 | tf_op jit(solution)/shard_map/ppermute | solution.py:199
  49.4 14.3 %collective-permute-start.6 = (bf16[144,2048]{1,0:T(8,128)(2,1)S(1)}, bf16[144,2048]{1,0:T(8,128)(2,1)S(1)}, u32[]{:S(2)}, u32[]{:S(2)}) collective-permute-start(bf16[144,2048]{1,0:T(8,128)(2,1)S(1)} %pad_maximum_fusion), channel_id=1, source_target_pairs={{0,4},{1,5},{2,6},{3,7},{4,0},{5,1},{6,2},{7,3},{8,12},{9,13},{10,... | collective-permute-start | bytes 1769480 | tf_op jit(solution)/shard_map/ppermute | solution.py:199
  52.1 35.3 %all-to-all-start.2 = ((bf16[16,384,128]{2,1,0:T(8,128)(2,1)}), bf16[16,384,128]{2,1,0:T(8,128)(2,1)S(1)}, u32[]{:S(2)}, u32[]{:S(2)}) async-start(bf16[16,384,128]{2,1,0:T(8,128)(2,1)} %bitcast.20), calls=%async_computation.2 | async-start | bytes 3145728 | tf_op jit(solution)/shard_map/all_to_all | solution.py:181
  63.9 14.4 %collective-permute-start.7 = (bf16[144,1024]{1,0:T(8,128)(2,1)S(1)}, bf16[144,1024]{1,0:T(8,128)(2,1)S(1)}, u32[]{:S(2)}, u32[]{:S(2)}) collective-permute-start(bf16[144,1024]{1,0:T(8,128)(2,1)S(1)} %slice_select_fusion), channel_id=1, source_target_pairs={{0,8},{1,9},{2,10},{3,11},{4,12},{5,13},{6,14},{7,15},{8,0},{9,1},... | collective-permute-start | bytes 884744 | tf_op jit(solution)/shard_map/ppermute | solution.py:199
  78.3 9.0 %collective-permute-start.8 = (bf16[144,1024]{1,0:T(8,128)(2,1)S(1)}, bf16[144,1024]{1,0:T(8,128)(2,1)S(1)}, u32[]{:S(2)}, u32[]{:S(2)}) collective-permute-start(bf16[144,1024]{1,0:T(8,128)(2,1)S(1)} %broadcast_select_fusion.3), channel_id=1, source_target_pairs={{0,4},{1,5},{2,6},{3,7},{4,0},{5,1},{6,2},{7,3},{8,12},{9,13},{10,... | collective-permute-start | bytes 884744 | tf_op jit(solution)/shard_map/ppermute | solution.py:199
  87.4 1.1 copy-start
  88.5 63.4 %all-to-all-start.1 = ((bf16[16,640,128]{2,1,0:T(8,128)(2,1)}), bf16[16,640,128]{2,1,0:T(8,128)(2,1)S(1)}, u32[]{:S(2)}, u32[]{:S(2)}) async-start(bf16[16,640,128]{2,1,0:T(8,128)(2,1)} %bitcast.40), calls=%async_computation.1 | async-start | bytes 5242880 | tf_op jit(solution)/shard_map/all_to_all | solution.py:181
  92.6 35.1 %collective-permute-start.10 = (bf16[144,2048]{1,0:T(8,128)(2,1)S(1)}, bf16[144,2048]{1,0:T(8,128)(2,1)S(1)}, u32[]{:S(2)}, u32[]{:S(2)}) collective-permute-start(bf16[144,2048]{1,0:T(8,128)(2,1)S(1)} %pad_maximum_fusion.1.refs_0_), channel_id=1, source_target_pairs={{0,2},{1,3},{2,0},{3,1},{4,6},{5,7},{6,4},{7,5},{8,10},{9,11},{10,... | collective-permute-start | bytes 1769480 | tf_op jit(solution)/shard_map/ppermute | solution.py:199
  94.6 37.4 %collective-permute-start.9 = (bf16[144,2048]{1,0:T(8,128)(2,1)S(1)}, bf16[144,2048]{1,0:T(8,128)(2,1)S(1)}, u32[]{:S(2)}, u32[]{:S(2)}) collective-permute-start(bf16[144,2048]{1,0:T(8,128)(2,1)S(1)} %pad_maximum_fusion.1.refs_0_), channel_id=1, source_target_pairs={{0,1},{1,0},{2,3},{3,2},{4,5},{5,4},{6,7},{7,6},{8,9},{9,8},{10,11... | collective-permute-start | bytes 1769480 | tf_op jit(solution)/shard_map/ppermute | solution.py:199
  96.0 1.4 copy-start.1
  105.8 31.4 %copy-start.7 = (bf16[4,4,128,128]{3,2,1,0:T(8,128)(2,1)}, bf16[4,4,128,128]{3,2,1,0:T(8,128)(2,1)S(1)}, u32[]{:S(2)}) copy-start(bf16[4,4,128,128]{3,2,1,0:T(8,128)(2,1)S(1)} %self_attention.2) | copy-start | bytes 1572868
  105.8 39.9 %copy-start.2 = (bf16[2048,256]{1,0:T(8,128)(2,1)S(1)}, bf16[2048,256]{1,0:T(8,128)(2,1)}, u32[]{:S(2)}) copy-start(bf16[2048,256]{1,0:T(8,128)(2,1)} %refs_5_.1) | copy-start | bytes 3145732
  127.8 9.4 %collective-permute-start.11 = (bf16[144,1024]{1,0:T(8,128)(2,1)S(1)}, bf16[144,1024]{1,0:T(8,128)(2,1)S(1)}, u32[]{:S(2)}, u32[]{:S(2)}) collective-permute-start(bf16[144,1024]{1,0:T(8,128)(2,1)S(1)} %slice.23), channel_id=1, source_target_pairs={{0,1},{1,0},{2,3},{3,2},{4,5},{5,4},{6,7},{7,6},{8,9},{9,8},{10,11... | collective-permute-start | bytes 884744 | tf_op jit(solution)/shard_map/ppermute | solution.py:199
  132.0 13.6 %collective-permute-start.12 = (bf16[144,1024]{1,0:T(8,128)(2,1)S(1)}, bf16[144,1024]{1,0:T(8,128)(2,1)S(1)}, u32[]{:S(2)}, u32[]{:S(2)}) collective-permute-start(bf16[144,1024]{1,0:T(8,128)(2,1)S(1)} %slice.27), channel_id=1, source_target_pairs={{0,2},{1,3},{2,0},{3,1},{4,6},{5,7},{6,4},{7,5},{8,10},{9,11},{10,... | collective-permute-start | bytes 884744 | tf_op jit(solution)/shard_map/ppermute | solution.py:199
  148.9 2.7 %collective-permute-start.13 = (f32[512,512]{1,0:T(8,128)S(1)}, f32[512,512]{1,0:T(8,128)S(1)}, u32[]{:S(2)}, u32[]{:S(2)}) collective-permute-start(f32[512,512]{1,0:T(8,128)S(1)} %get-tuple-element.30), channel_id=1, source_target_pairs={{0,16},{16,0},{1,17},{17,1},{2,18},{18,2},{3,19},{19,3},{4,20},{20... | collective-permute-start | bytes 3145736 | tf_op jit(solution)/shard_map/ppermute | solution.py:207
  151.9 4.7 %copy-start.3 = (bf16[512,512]{1,0:T(8,128)(2,1)}, bf16[512,512]{1,0:T(8,128)(2,1)S(1)}, u32[]{:S(2)}) copy-start(bf16[512,512]{1,0:T(8,128)(2,1)S(1)} %add_convert_fusion.k_ref.v_ref) | copy-start | bytes 1572868
  151.9 1.2 copy-start.8
  156.6 0.8 copy-start.5
  157.4 22.0 %all-to-all-start.3 = ((bf16[16,128,128]{2,1,0:T(8,128)(2,1)}), bf16[16,128,128]{2,1,0:T(8,128)(2,1)S(1)}, u32[]{:S(2)}, u32[]{:S(2)}) async-start(bf16[16,128,128]{2,1,0:T(8,128)(2,1)} %copy-done.5), calls=%async_computation.3 | async-start | bytes 1048576 | tf_op jit(solution)/shard_map/all_to_all | solution.py:181
  164.0 8.3 %copy-start.4 = (bf16[512,512]{1,0:T(8,128)(2,1)S(1)}, bf16[512,512]{1,0:T(8,128)(2,1)}, u32[]{:S(2)}) copy-start(bf16[512,512]{1,0:T(8,128)(2,1)} %copy-done.3) | copy-start | bytes 1572868
  175.7 0.8 copy-start.6

commit v4 on v3

--- a/solution.py
+++ b/solution.py
@@ -123,14 +123,14 @@
     )(blocks, blocks, blocks).reshape(n, rows, width)
 
 
-def cross_attention(blocks, item, text, head, length, self_out):
+def cross_attention(blocks, item, text, head, length, self_out, turned):
     n, _, rows, width = blocks.shape
     heads = width // HEAD
     positions = text.shape[0]
     values_at = text.shape[1] // HEAD // 2 + head
-    step = max(1, min(n, 512 // rows))
+    step = n // QUAD if turned else max(1, min(n, 512 // rows))
     factor = LOG2E / HEAD**0.5
-    self_block = pl.BlockSpec((step, rows, HEAD), lambda h, i, _: (i, 0, h))
+    shape, out_block = result_blocks(n, step, rows, turned)
 
     def body(length_ref, q_ref, k_ref, v_ref, self_ref, out_ref, values):
         @pl.when(pl.program_id(1) == 0)
@@ -160,12 +160,12 @@
                 pl.BlockSpec((step, 1, rows, HEAD), lambda h, i, _: (i, item, 0, h)),
                 pl.BlockSpec((positions, HEAD), lambda h, i, _: (0, head + h)),
                 pl.BlockSpec((positions, HEAD), lambda h, i, _: (0, values_at + h)),
-                self_block,
+                out_block,
             ],
-            out_specs=self_block,
+            out_specs=out_block,
             scratch_shapes=[pltpu.VMEM((positions, 2 * HEAD), jnp.bfloat16)],
         ),
-        out_shape=jax.ShapeDtypeStruct((n, rows, width), jnp.bfloat16),
+        out_shape=jax.ShapeDtypeStruct((*shape, width), jnp.bfloat16),
         compiler_params=params(),
         cost_estimate=pl.CostEstimate(
             flops=32 * heads * n * rows * positions * HEAD,
@@ -173,7 +173,7 @@
             transcendentals=heads * n * rows * positions,
         ),
         name="cross_attention",
-    )(length, blocks, text, text, self_out)
+    )(length, blocks, text, text, self_out.reshape(*shape, width)).reshape(n, rows, width)
 
 
 def spread(blocks, groups=None):
@@ -253,15 +253,17 @@
 
 
 def project(pieces, key_weight, value_weight, where, positions):
-    rows, columns = pieces[0].shape
-    width = key_weight.shape[1]
-    half = columns // 2
+    rows, half = pieces[0].shape
+    columns, width = key_weight.shape
     rows_long, rows_short = positions // 4, positions // 32
 
     def body(where_ref, *refs):
-        piece_refs, (key_ref, value_ref, mine_ref, sent_ref) = refs[:5], refs[5:]
-        halves = [(ref[:, :half], ref[:, half:]) for ref in piece_refs[:3]]
-        halves.append((piece_refs[3][...], piece_refs[4][...]))
+        piece_refs, (key_ref, value_ref, mine_ref, sent_ref) = refs[:10], refs[10:]
+        whole_pieces = [ref[...] for ref in piece_refs]
+        lefts, rights = [
+            side[:3] + [jnp.concatenate(side[3:], axis=1)]
+            for side in (whole_pieces[:5], whole_pieces[5:])
+        ]
 
         def fill(long_ref, short_ref):
             short_ref[4 * rows_short :] = jnp.zeros(
@@ -270,7 +272,7 @@
             near = where_ref[2]
             first = pl.ds(pl.multiple_of(near * half, half), half)
             second = pl.ds(pl.multiple_of((1 - near) * half, half), half)
-            for i, (left, right) in enumerate(halves):
+            for i, (left, right) in enumerate(zip(lefts, rights)):
                 place = where_ref[0] ^ i
                 at_long = pl.ds(pl.multiple_of(place * rows_long, rows_long), rows_long)
                 at_short = pl.ds(pl.multiple_of(place * rows_short, rows_short), rows_short)
@@ -297,18 +299,20 @@
         grid_spec=pltpu.PrefetchScalarGridSpec(
             num_scalar_prefetch=1,
             grid=(1,),
-            in_specs=[whole(rows, columns)] * 3
-            + [whole(rows, half)] * 2
+            in_specs=([whole(rows, half)] * 3 + [whole(rows, half // 2)] * 2) * 2
             + [whole(columns, width)] * 2,
             out_specs=[whole(positions, 2 * width)] * 2,
         ),
         out_shape=[jax.ShapeDtypeStruct((positions, 2 * width), jnp.float32)] * 2,
         compiler_params=params(),
+        cost_estimate=pl.CostEstimate(
+            flops=18000000000, bytes_accessed=8 * 1024 * 1024, transcendentals=0
+        ),
         name="project",
     )(where, *pieces, key_weight, value_weight)
 
 
-def text_of_pair(embed, key_weight, value_weight, length, encoder, n, before, between, after):
+def text_of_pair(embed, key_weight, value_weight, length, encoder, n, between, after):
     positions, columns = embed.shape
     core = lax.axis_index("dp")
     me = lax.axis_index("seq")
@@ -337,18 +341,21 @@
     piece = jnp.concatenate(
         [choose(pick(part_a, y), got_a, 1), choose(pick(part_b, x), got_b, 0)], axis=1
     )
-    piece = before(piece)
     last = n.bit_length() - 2
     for bit in range(2, last):
         piece = choose(piece, exchange(piece, 1 << bit, n), bit)
     near = (me >> 2) & 1
     own = jnp.where(near == 0, piece[:, : half // 2], piece[:, half // 2 :])
-    own = choose(own, exchange(own, 1 << last, n), last)
-    piece = between(jnp.concatenate([own, exchange(own, 4, n)], axis=1))
-    got_x, got_y = exchange(piece, 1, n), after(exchange(piece, 2, n))
-    across_a = exchange(got_y[:, : half // 2], 1, n)
-    across_b = exchange(got_x[:, half // 2 :], 2, n)
-    pieces = [piece, got_x, got_y, across_a, across_b]
+    own = between(choose(own, exchange(own, 1 << last, n), last))
+    far, own_x, own_y = exchange(own, 4, n), exchange(own, 1, n), after(exchange(own, 2, n))
+    pieces = []
+    for here, at_x, at_y in (
+        (own, own_x, own_y),
+        (far, exchange(far, 1, n), exchange(far, 2, n)),
+    ):
+        across_a = exchange(at_y[:, : half // 4], 1, n)
+        across_b = exchange(at_x[:, half // 4 :], 2, n)
+        pieces += [here, at_x, at_y, across_a, across_b]
     mine, other_sums = project(
         pieces, key_weight, value_weight, jnp.stack([place, is_long, near]), positions
     )
@@ -384,23 +391,19 @@
         blocks = spread(pack(inputs, n, [(a, 0) for a in range(4)], heads * HEAD))
         text = text_of_clip(embed, *weights, encoder_index[0])
         self_out = self_attention(blocks, 0, False)
-        out = cross_attention(blocks, 3, text, 0, text_lengths, self_out)
+        out = cross_attention(blocks, 3, text, 0, text_lengths, self_out, False)
         return unpack([spread(out)])[None]
 
     part = heads // 2 * HEAD
-    lines = spread_lines(pack(inputs, n, [(0, 0), (1, 0), (2, 0)], part))
-    rest = pack(inputs, n, [(3, 0), (0, 1), (1, 1), (2, 1), (3, 1)], part)
+    lines = spread_lines(pack(inputs, n, [(a, 0) for a in range(4)], part))
+    rest = pack(inputs, n, [(a, 1) for a in range(4)], part)
+    earlier = spread_planes(lines)
     self_first = later = None
 
-    def before(piece):
-        nonlocal lines, self_first
-        lines, piece = lax.optimization_barrier((lines, piece))
-        self_first = self_attention(spread_planes(lines), 0, True)
-        return piece
-
     def between(piece):
-        nonlocal rest, later
-        piece, rest = lax.optimization_barrier((piece, rest))
+        nonlocal rest, earlier, self_first, later
+        piece, rest, earlier = lax.optimization_barrier((piece, rest, earlier))
+        self_first = self_attention(earlier, 0, True)
         later = spread(rest)
         return piece
 
@@ -410,13 +413,13 @@
         return piece
 
     text = text_of_pair(
-        embed, *weights, text_lengths[0], encoder_index[0], n, before, between, after
-    )
-    out = cross_attention(later, 0, text, 0, text_lengths, self_first)
+        embed, *weights, text_lengths[0], encoder_index[0], n, between, after
+    )
+    out = cross_attention(earlier, 3, text, 0, text_lengths, self_first, True)
+    later, out = lax.optimization_barrier((later, out))
     tokens = spread(out)
-    later, out = lax.optimization_barrier((later, out))
-    self_second = self_attention(later, 1, False)
-    out = cross_attention(later, 4, text, heads // 2, text_lengths, self_second)
+    self_second = self_attention(later, 0, False)
+    out = cross_attention(later, 3, text, heads // 2, text_lengths, self_second, False)
     tokens, out = lax.optimization_barrier((tokens, out))
     return unpack([tokens, spread(out)])[None]
 

time: 201 us -> 190 us (0.945)
  waiting for transfers between devices: 91.4 us -> 71.7 us
  starting transfers between devices: 36.5 us -> 42.6 us
  local copies, waits for them, and re-layouts: 8.77 us -> 4.7 us
  Pallas kernels: 39.5 us -> 42.7 us
  other arithmetic: 1.29 us -> 3.46 us
    ppermute x11 -> x15, waiting for transfers between devices: 78.4 us -> 48.7 us  [exchange(): return lax.ppermute(value, 'seq', [(i, i ^ apart) for i in range(n)])]
    all_to_all x4, waiting for transfers between devices: 10.4 us -> 19.5 us  [spread(): lax.all_to_all(flat, 'seq', split_axis=0, concat_axis=0, tiled=True, axis...]
    unnamed x18 -> x4, local copies, waits for them, and re-layouts: 5.36 us -> 0.82 us
    another operation x0 -> x1, local copies, waits for them, and re-layouts: none -> 3.19 us  [spread_planes(): blocks.reshape(n // QUAD, QUAD, *shape).swapaxes(0, 1).reshape(n, *shape)]
    all_to_all x4, starting transfers between devices: 20.7 us -> 23.9 us  [spread(): lax.all_to_all(flat, 'seq', split_axis=0, concat_axis=0, tiled=True, axis...]
    ppermute x11 -> x15, starting transfers between devices: 15.1 us -> 18 us  [exchange(): return lax.ppermute(value, 'seq', [(i, i ^ apart) for i in range(n)])]
    transpose x1 -> x0, local copies, waits for them, and re-layouts: 2.73 us -> none  [spread_planes(): blocks.reshape(n // QUAD, QUAD, *shape).swapaxes(0, 1).reshape(n, *shape)]
    select_n x6, other arithmetic: 0.65 us -> 2.86 us  [choose(): return jnp.where(apart >> bit & 1 == 0, own, got)]
  transfers between devices with their start and end apart: 18 -> 22, of which waited for: 13 -> 15; matrix products, arithmetic and copies ran while one was open for 2% -> 4% of each run, Pallas kernels for 17% -> 22%
where the time goes in v4:
time: 190 us; the launch traced here: 189 us
  waiting for transfers between devices  71.7 us (38%)
  Pallas kernels  42.7 us (22%)
  starting transfers between devices  42.6 us (22%)
  blocking collectives  20 us (11%)
  local copies, waits for them, and re-layouts  4.7 us (2%)
  other arithmetic  3.46 us (2%)
  between operations  3.44 us (2%)
    ppermute x15, waiting for transfers between devices, exchange(): return lax.ppermute(value, 'seq', [(i, i ^ apart) for i in range(n)])  48.7 us
    all_to_all x4, starting transfers between devices, spread(): lax.all_to_all(flat, 'seq', split_axis=0, concat_axis=0, tiled=True, axis...  23.9 us
    all_to_all x1, blocking collectives, spread(): lax.all_to_all(flat, 'seq', split_axis=0, concat_axis=0, tiled=True, axis...  20 us
    all_to_all x4, waiting for transfers between devices, spread(): lax.all_to_all(flat, 'seq', split_axis=0, concat_axis=0, tiled=True, axis...  19.5 us
    ppermute x15, starting transfers between devices, exchange(): return lax.ppermute(value, 'seq', [(i, i ^ apart) for i in range(n)])  18 us
    pallas_call x2, Pallas kernels, self_attention(): pl.pallas_call(body, grid=(heads, n // step), in_specs=[pl.BlockSpec((ste...  17.8 us
    pallas_call x2, Pallas kernels, pack(): pl.pallas_call(body, grid=(n // per,), in_specs=[pl.BlockSpec((rows, per...  8.56 us
    pallas_call x2, Pallas kernels, cross_attention(): pl.pallas_call(body, grid_spec=pltpu.PrefetchScalarGridSpec(num_scalar_pr...  8.47 us
  transfers between devices with their start and end apart: 22, of which 15 were waited for; matrix products, arithmetic and copies ran while one was open for 4% of the time, Pallas kernels for 22%

profile of v4, /device:TPU:0, one launch (start us, length us, event | category | flops | bytes accessed | tf_op | source)
XLA Modules:
  0.0 188.7 jit_solution(1693432093832831126)
XLA Ops:
  0.0 0.5 collective-permute-start.1
  0.5 4.3 %pack.3 = bf16[16,4,128,128]{3,2,1,0:T(8,128)(2,1)} custom-call(bf16[128,4096]{1,0:T(8,128)(2,1)} %bitcast.41, bf16[128,4096]{1,0:T(8,128)(2,1)} %bitcast.43, bf16[128,4096]{1,0:T(8,128)(2,1)} %bitcast.45, bf16[128,4096]{1,0:T(8,128)(2,1)} %bitcast.47), custom_call_target="tpu_custom_call" | custom-call | tf_op jit(solution)/shard_map/pack/pallas_call | solution.py:32
  4.8 5.9 %all-to-all-start = ((bf16[16,512,128]{2,1,0:T(8,128)(2,1)}), bf16[16,512,128]{2,1,0:T(8,128)(2,1)}, u32[]{:S(2)}, u32[]{:S(2)}) async-start(bf16[16,512,128]{2,1,0:T(8,128)(2,1)} %bitcast.36), calls=%async_computation | async-start | bytes 4194304 | tf_op jit(solution)/shard_map/all_to_all | solution.py:181
  11.9 0.1 pad_add_fusion
  12.0 0.2 collective-permute-start
  12.2 0.9 collective-permute-done
  13.1 0.6 fusion.1
  14.4 0.1 pad_add_fusion.1.where_ref
  14.4 3.0 %quarters.1 = (bf16[2,144,1024]{2,1,0:T(8,128)(2,1)S(1)}, bf16[2,144,1024]{2,1,0:T(8,128)(2,1)S(1)}, bf16[2,144,1024]{2,1,0:T(8,128)(2,1)S(1)}, bf16[2,144,1024]{2,1,0:T(8,128)(2,1)S(1)}) custom-call(s32[3]{0:T(128)S(1)} %pad_add_fusion.1.where_ref, bf16[512,4096]{1,0:T(8,128)(2,1)} %bitcast.40, bf16[512,4096]{1,0:T(8,128)(2,1)} %collective-permute-done.1.other_ref), custom_call_target="tpu_custom_call" | custom-call | tf_op jit(solution)/shard_map/quarters/pallas_call | solution.py:241
  17.4 1.6 collective-permute-start.4
  20.3 1.6 collective-permute-start.2
  21.9 11.0 %collective-permute-done.4 = bf16[2,144,1024]{2,1,0:T(8,128)(2,1)S(1)} collective-permute-done((bf16[2,144,1024]{2,1,0:T(8,128)(2,1)S(1)}, bf16[2,144,1024]{2,1,0:T(8,128)(2,1)S(1)}, u32[]{:S(2)}, u32[]{:S(2)}) %collective-permute-start.4) | collective-permute-done | bytes 589856 | tf_op jit(solution)/shard_map/ppermute | solution.py:199
  32.9 0.8 copy-done.1
  33.7 1.2 broadcast_select_fusion
  34.9 1.6 collective-permute-start.5
  36.5 0.0 collective-permute-done.2
  36.5 0.1 broadcast_select_fusion.1
  36.7 1.6 collective-permute-start.3
  38.2 5.1 %collective-permute-done.5 = bf16[144,1024]{1,0:T(8,128)(2,1)S(1)} collective-permute-done((bf16[144,1024]{1,0:T(8,128)(2,1)S(1)}, bf16[144,1024]{1,0:T(8,128)(2,1)S(1)}, u32[]{:S(2)}, u32[]{:S(2)}) %collective-permute-start.5) | collective-permute-done | bytes 294944 | tf_op jit(solution)/shard_map/ppermute | solution.py:199
  43.4 0.1 bitcast_select_fusion
  43.5 1.3 collective-permute-done.3
  44.8 0.1 bitcast_select_fusion.1
  45.0 2.1 %collective-permute-start.6 = (bf16[144,2048]{1,0:T(8,128)(2,1)S(1)}, bf16[144,2048]{1,0:T(8,128)(2,1)}, u32[]{:S(2)}, u32[]{:S(2)}) collective-permute-start(bf16[144,2048]{1,0:T(8,128)(2,1)S(1)} %pad_maximum_fusion), channel_id=1, source_target_pairs={{0,4},{1,5},{2,6},{3,7},{4,0},{5,1},{6,2},{7,3},{8,12},{9,13},{10,... | collective-permute-start | bytes 1769480 | tf_op jit(solution)/shard_map/ppermute | solution.py:199
  47.1 12.7 %all-to-all-done = bf16[16,512,128]{2,1,0:T(8,128)(2,1)} async-done(((bf16[16,512,128]{2,1,0:T(8,128)(2,1)}), bf16[16,512,128]{2,1,0:T(8,128)(2,1)}, u32[]{:S(2)}, u32[]{:S(2)}) %all-to-all-start) | async-done | bytes 2097184 | tf_op jit(solution)/shard_map/all_to_all | solution.py:181
  59.7 3.2 %copy.10 = bf16[4,4,4,128,128]{4,3,2,0,1:T(8,128)(2,1)} copy(bf16[4,4,4,128,128]{4,3,2,1,0:T(8,128)(2,1)} %bitcast.14) | data formatting | bytes 4194304 | tf_op jit(solution)/shard_map/reshape;reshape | solution.py:194
  62.9 3.7 %all-to-all-start.1 = ((bf16[16,512,128]{2,1,0:T(8,128)(2,1)}), bf16[16,512,128]{2,1,0:T(8,128)(2,1)S(1)}, u32[]{:S(2)}, u32[]{:S(2)}) async-start(bf16[16,512,128]{2,1,0:T(8,128)(2,1)} %bitcast.38), calls=%async_computation.1 | async-start | bytes 4194304 | tf_op jit(solution)/shard_map/all_to_all | solution.py:181
  66.6 2.6 %collective-permute-done.6 = bf16[144,2048]{1,0:T(8,128)(2,1)} collective-permute-done((bf16[144,2048]{1,0:T(8,128)(2,1)S(1)}, bf16[144,2048]{1,0:T(8,128)(2,1)}, u32[]{:S(2)}, u32[]{:S(2)}) %collective-permute-start.6) | collective-permute-done | bytes 589856 | tf_op jit(solution)/shard_map/ppermute | solution.py:199
  69.2 1.3 broadcast_select_fusion.2
  70.5 2.2 %collective-permute-start.7 = (bf16[144,1024]{1,0:T(8,128)(2,1)S(1)}, bf16[144,1024]{1,0:T(8,128)(2,1)S(1)}, u32[]{:S(2)}, u32[]{:S(2)}) collective-permute-start(bf16[144,1024]{1,0:T(8,128)(2,1)S(1)} %slice_select_fusion), channel_id=1, source_target_pairs={{0,8},{1,9},{2,10},{3,11},{4,12},{5,13},{6,14},{7,15},{8,0},{9,1},... | collective-permute-start | bytes 884744 | tf_op jit(solution)/shard_map/ppermute | solution.py:199
  72.7 4.3 %pack.2 = bf16[16,4,128,128]{3,2,1,0:T(8,128)(2,1)} custom-call(bf16[128,4096]{1,0:T(8,128)(2,1)} %bitcast.42, bf16[128,4096]{1,0:T(8,128)(2,1)} %bitcast.44, bf16[128,4096]{1,0:T(8,128)(2,1)} %bitcast.46, bf16[128,4096]{1,0:T(8,128)(2,1)} %bitcast.48), custom_call_target="tpu_custom_call" | custom-call | tf_op jit(solution)/shard_map/pack/pallas_call | solution.py:32
  77.0 8.8 %collective-permute-done.7 = bf16[144,1024]{1,0:T(8,128)(2,1)S(1)} collective-permute-done((bf16[144,1024]{1,0:T(8,128)(2,1)S(1)}, bf16[144,1024]{1,0:T(8,128)(2,1)S(1)}, u32[]{:S(2)}, u32[]{:S(2)}) %collective-permute-start.7) | collective-permute-done | bytes 294944 | tf_op jit(solution)/shard_map/ppermute | solution.py:199
  85.8 0.1 broadcast_select_fusion.3.refs_0_
  85.9 5.3 %all-to-all-done.1 = bf16[16,512,128]{2,1,0:T(8,128)(2,1)S(1)} async-done(((bf16[16,512,128]{2,1,0:T(8,128)(2,1)}), bf16[16,512,128]{2,1,0:T(8,128)(2,1)S(1)}, u32[]{:S(2)}, u32[]{:S(2)}) %all-to-all-start.1) | async-done | bytes 2097184 | tf_op jit(solution)/shard_map/all_to_all | solution.py:181
  91.1 0.0 collective-permute-start.12
  91.1 1.4 collective-permute-start.8
  92.6 0.6 collective-permute-start.9
  93.1 4.4 %all-to-all-start.2 = ((bf16[16,512,128]{2,1,0:T(8,128)(2,1)}), bf16[16,512,128]{2,1,0:T(8,128)(2,1)}, u32[]{:S(2)}, u32[]{:S(2)}) async-start(bf16[16,512,128]{2,1,0:T(8,128)(2,1)} %bitcast.37), calls=%async_computation.2 | async-start | bytes 4194304 | tf_op jit(solution)/shard_map/all_to_all | solution.py:181
  97.6 0.0 copy-start
  97.6 6.9 %collective-permute-done.12.refs_5_ = bf16[144,1024]{1,0:T(8,128)(2,1)S(1)} collective-permute-done((bf16[144,1024]{1,0:T(8,128)(2,1)S(1)}, bf16[144,1024]{1,0:T(8,128)(2,1)S(1)}, u32[]{:S(2)}, u32[]{:S(2)}) %collective-permute-start.12) | collective-permute-done | bytes 294944 | tf_op jit(solution)/shard_map/ppermute | solution.py:199
  104.5 0.0 collective-permute-start.13
  104.5 0.0 collective-permute-start.14
  104.5 8.3 %self_attention.2 = bf16[4,4,128,128]{3,2,1,0:T(8,128)(2,1)S(1)} custom-call(bf16[16,4,128,128]{3,2,1,0:T(8,128)(2,1)S(1)} %bitcast.31, bf16[16,4,128,128]{3,2,1,0:T(8,128)(2,1)S(1)} %bitcast.32, bf16[16,4,128,128]{3,2,1,0:T(8,128)(2,1)S(1)} %bitcast.33), custom_call_target="tpu_custom_call" | custom-call | flops 8589934592 | bytes 2097152 | tf_op jit(solution)/shard_map/self_attention/pallas_call | solution.py:105
  112.8 0.0 collective-permute-done.9.refs_2_
  112.9 2.1 %collective-permute-start.10 = (bf16[144,512]{1,0:T(8,128)(2,1)S(1)}, bf16[144,512]{1,0:T(8,128)(2,1)S(1)}, u32[]{:S(2)}, u32[]{:S(2)}) collective-permute-start(bf16[144,512]{1,0:T(8,128)(2,1)S(1)} %slice.29), channel_id=1, source_target_pairs={{0,1},{1,0},{2,3},{3,2},{4,5},{5,4},{6,7},{7,6},{8,9},{9,8},{10,11... | collective-permute-start | bytes 442376 | tf_op jit(solution)/shard_map/ppermute | solution.py:199
  115.0 2.1 %collective-permute-start.11 = (bf16[144,512]{1,0:T(8,128)(2,1)S(1)}, bf16[144,512]{1,0:T(8,128)(2,1)S(1)}, u32[]{:S(2)}, u32[]{:S(2)}) collective-permute-start(bf16[144,512]{1,0:T(8,128)(2,1)S(1)} %slice.35), channel_id=1, source_target_pairs={{0,2},{1,3},{2,0},{3,1},{4,6},{5,7},{6,4},{7,5},{8,10},{9,11},{10,... | collective-permute-start | bytes 442376 | tf_op jit(solution)/shard_map/ppermute | solution.py:199
  117.0 7.0 %collective-permute-done.14.refs_7_ = bf16[144,1024]{1,0:T(8,128)(2,1)S(1)} collective-permute-done((bf16[144,1024]{1,0:T(8,128)(2,1)S(1)}, bf16[144,1024]{1,0:T(8,128)(2,1)S(1)}, u32[]{:S(2)}, u32[]{:S(2)}) %collective-permute-start.14) | collective-permute-done | bytes 294944 | tf_op jit(solution)/shard_map/ppermute | solution.py:199
  124.0 1.3 collective-permute-start.15
  125.3 0.1 collective-permute-start.16
  125.4 0.1 pad_add_fusion.2.where_ref
  125.5 2.4 %collective-permute-done.10.refs_3_ = bf16[144,512]{1,0:T(8,128)(2,1)S(1)} collective-permute-done((bf16[144,512]{1,0:T(8,128)(2,1)S(1)}, bf16[144,512]{1,0:T(8,128)(2,1)S(1)}, u32[]{:S(2)}, u32[]{:S(2)}) %collective-permute-start.10) | collective-permute-done | bytes 147488 | tf_op jit(solution)/shard_map/ppermute | solution.py:199
  127.9 2.9 %collective-permute-done.15.refs_8_ = bf16[144,512]{1,0:T(8,128)(2,1)S(1)} collective-permute-done((bf16[144,512]{1,0:T(8,128)(2,1)S(1)}, bf16[144,512]{1,0:T(8,128)(2,1)S(1)}, u32[]{:S(2)}, u32[]{:S(2)}) %collective-permute-start.15) | collective-permute-done | bytes 147488 | tf_op jit(solution)/shard_map/ppermute | solution.py:199
  130.8 0.6 collective-permute-done.16.refs_9_
  131.4 3.3 %project.1 = (f32[512,512]{1,0:T(8,128)S(1)}, f32[512,512]{1,0:T(8,128)S(1)}) custom-call(s32[3]{0:T(128)S(1)} %pad_add_fusion.2.where_ref, bf16[144,1024]{1,0:T(8,128)(2,1)S(1)} %broadcast_select_fusion.3.refs_0_, bf16[144,1024]{1,0:T(8,128)(2,1)S(1)} %collective-permute-done.8.refs_1_, bf16[144,1024]{1,0:T(8,128)(2,1)S(1)} %collective-permute-done.9.refs_2_, ...), custom_call_target="tpu_custom_call" | custom-call | flops 17999998976 | bytes 8388608 | tf_op jit(solution)/shard_map/project/pallas_call | solution.py:297
  134.7 0.1 collective-permute-start.17
  134.8 2.6 %collective-permute-done.17 = f32[512,512]{1,0:T(8,128)S(1)} collective-permute-done((f32[512,512]{1,0:T(8,128)S(1)}, f32[512,512]{1,0:T(8,128)S(1)}, u32[]{:S(2)}, u32[]{:S(2)}) %collective-permute-start.17) | collective-permute-done | bytes 1048608 | tf_op jit(solution)/shard_map/ppermute | solution.py:207
  137.4 0.3 add_convert_fusion.k_ref.v_ref
  137.7 4.1 %cross_attention.2 = bf16[4,4,128,128]{3,2,1,0:T(8,128)(2,1)} custom-call(s32[1]{0:T(128)S(6)} %copy.11.length_ref, bf16[16,4,128,128]{3,2,1,0:T(8,128)(2,1)S(1)} %bitcast.34, bf16[512,512]{1,0:T(8,128)(2,1)S(1)} %add_convert_fusion.k_ref.v_ref, bf16[512,512]{1,0:T(8,128)(2,1)S(1)} %add_convert_fusion.k_ref.v_ref, bf16[4,4,128,128]{3,2,1,0:T(8,128)(2,1)S(1)} %self_attention.2), custom_call_target="tpu_custom_call" | custom-call | flops 4294967296 | bytes 1572864 | tf_op jit(solution)/shard_map/cross_attention/pallas_call | solution.py:154
  141.8 0.0 all-to-all-done.2
  141.8 9.8 %all-to-all-start.3 = ((bf16[16,128,128]{2,1,0:T(8,128)(2,1)}), bf16[16,128,128]{2,1,0:T(8,128)(2,1)S(1)}, u32[]{:S(2)}, u32[]{:S(2)}) async-start(bf16[16,128,128]{2,1,0:T(8,128)(2,1)} %bitcast.23), calls=%async_computation.3 | async-start | bytes 1048576 | tf_op jit(solution)/shard_map/all_to_all | solution.py:181
  151.6 9.5 %self_attention.3.self_ref = bf16[4,4,128,128]{3,2,1,0:T(8,128)(2,1)S(1)} custom-call(bf16[16,4,128,128]{3,2,1,0:T(8,128)(2,1)} %bitcast.19.q_ref.k_ref.v_ref, bf16[16,4,128,128]{3,2,1,0:T(8,128)(2,1)} %bitcast.19.q_ref.k_ref.v_ref, bf16[16,4,128,128]{3,2,1,0:T(8,128)(2,1)} %bitcast.19.q_ref.k_ref.v_ref), custom_call_target="tpu_custom_call" | custom-call | flops 8589934592 | bytes 2097152 | tf_op jit(solution)/shard_map/self_attention/pallas_call | solution.py:105
  161.1 4.3 %cross_attention.3 = bf16[4,4,128,128]{3,2,1,0:T(8,128)(2,1)S(1)} custom-call(s32[1]{0:T(128)S(6)} %copy.11.length_ref, bf16[16,4,128,128]{3,2,1,0:T(8,128)(2,1)} %bitcast.19.q_ref.k_ref.v_ref, bf16[512,512]{1,0:T(8,128)(2,1)S(1)} %add_convert_fusion.k_ref.v_ref, bf16[512,512]{1,0:T(8,128)(2,1)S(1)} %add_convert_fusion.k_ref.v_ref, ...), custom_call_target="tpu_custom_call" | custom-call | flops 4294967296 | bytes 1572864 | tf_op jit(solution)/shard_map/cross_attention/pallas_call | solution.py:154
  165.5 1.5 all-to-all-done.3.refs_0_
  167.0 20.0 %all_to_all.25.refs_1_ = bf16[16,128,128]{2,1,0:T(8,128)(2,1)S(1)} all-to-all(bf16[16,128,128]{2,1,0:T(8,128)(2,1)S(1)} %bitcast.35), channel_id=1, replica_groups=mesh['dp'=2,'seq'=16] {'seq'}, dimensions={0} | all-to-all | bytes 1048576 | tf_op jit(solution)/shard_map/all_to_all | solution.py:181
  187.1 1.6 unpack.1
  (18 shorter events, 0.2 us)
Async XLA Ops:
  0.0 14.4 %collective-permute-start.1 = (bf16[512,4096]{1,0:T(8,128)(2,1)}, bf16[512,4096]{1,0:T(8,128)(2,1)}, u32[]{:S(2)}, u32[]{:S(2)}) collective-permute-start(bf16[512,4096]{1,0:T(8,128)(2,1)} %bitcast.39), channel_id=1, source_target_pairs={{0,16},{16,0},{1,17},{17,1},{2,18},{18,2},{3,19},{19,3},{4,20},{20... | collective-permute-start | bytes 12582920 | tf_op jit(solution)/shard_map/ppermute | solution.py:207
  4.8 55.0 %all-to-all-start = ((bf16[16,512,128]{2,1,0:T(8,128)(2,1)}), bf16[16,512,128]{2,1,0:T(8,128)(2,1)}, u32[]{:S(2)}, u32[]{:S(2)}) async-start(bf16[16,512,128]{2,1,0:T(8,128)(2,1)} %bitcast.36), calls=%async_computation | async-start | bytes 4194304 | tf_op jit(solution)/shard_map/all_to_all | solution.py:181
  12.0 1.1 collective-permute-start
  17.4 15.5 %collective-permute-start.4 = (bf16[2,144,1024]{2,1,0:T(8,128)(2,1)S(1)}, bf16[2,144,1024]{2,1,0:T(8,128)(2,1)S(1)}, u32[]{:S(2)}, u32[]{:S(2)}) collective-permute-start(bf16[2,144,1024]{2,1,0:T(8,128)(2,1)S(1)} %get-tuple-element.23), channel_id=1, source_target_pairs={{0,2},{1,3},{2,0},{3,1},{4,6},{5,7},{6,4},{7,5},{8,10},{9,11},{10,... | collective-permute-start | bytes 1769480 | tf_op jit(solution)/shard_map/ppermute | solution.py:199
  20.3 16.2 %collective-permute-start.2 = (bf16[2,144,1024]{2,1,0:T(8,128)(2,1)S(1)}, bf16[2,144,1024]{2,1,0:T(8,128)(2,1)S(1)}, u32[]{:S(2)}, u32[]{:S(2)}) collective-permute-start(bf16[2,144,1024]{2,1,0:T(8,128)(2,1)S(1)} %get-tuple-element.21), channel_id=1, source_target_pairs={{0,1},{1,0},{2,3},{3,2},{4,5},{5,4},{6,7},{7,6},{8,9},{9,8},{10,11... | collective-permute-start | bytes 1769480 | tf_op jit(solution)/shard_map/ppermute | solution.py:199
  32.9 0.8 copy-start.1
  34.9 8.5 %collective-permute-start.5 = (bf16[144,1024]{1,0:T(8,128)(2,1)S(1)}, bf16[144,1024]{1,0:T(8,128)(2,1)S(1)}, u32[]{:S(2)}, u32[]{:S(2)}) collective-permute-start(bf16[144,1024]{1,0:T(8,128)(2,1)S(1)} %dynamic-slice_bitcast_fusion), channel_id=1, source_target_pairs={{0,1},{1,0},{2,3},{3,2},{4,5},{5,4},{6,7},{7,6},{8,9},{9,8},{10,11... | collective-permute-start | bytes 884744 | tf_op jit(solution)/shard_map/ppermute | solution.py:199
  36.7 8.2 %collective-permute-start.3 = (bf16[144,1024]{1,0:T(8,128)(2,1)S(1)}, bf16[144,1024]{1,0:T(8,128)(2,1)S(1)}, u32[]{:S(2)}, u32[]{:S(2)}) collective-permute-start(bf16[144,1024]{1,0:T(8,128)(2,1)S(1)} %dynamic-slice_bitcast_fusion.1), channel_id=1, source_target_pairs={{0,2},{1,3},{2,0},{3,1},{4,6},{5,7},{6,4},{7,5},{8,10},{9,11},{10,... | collective-permute-start | bytes 884744 | tf_op jit(solution)/shard_map/ppermute | solution.py:199
  45.0 24.2 %collective-permute-start.6 = (bf16[144,2048]{1,0:T(8,128)(2,1)S(1)}, bf16[144,2048]{1,0:T(8,128)(2,1)}, u32[]{:S(2)}, u32[]{:S(2)}) collective-permute-start(bf16[144,2048]{1,0:T(8,128)(2,1)S(1)} %pad_maximum_fusion), channel_id=1, source_target_pairs={{0,4},{1,5},{2,6},{3,7},{4,0},{5,1},{6,2},{7,3},{8,12},{9,13},{10,... | collective-permute-start | bytes 1769480 | tf_op jit(solution)/shard_map/ppermute | solution.py:199
  62.9 28.2 %all-to-all-start.1 = ((bf16[16,512,128]{2,1,0:T(8,128)(2,1)}), bf16[16,512,128]{2,1,0:T(8,128)(2,1)S(1)}, u32[]{:S(2)}, u32[]{:S(2)}) async-start(bf16[16,512,128]{2,1,0:T(8,128)(2,1)} %bitcast.38), calls=%async_computation.1 | async-start | bytes 4194304 | tf_op jit(solution)/shard_map/all_to_all | solution.py:181
  70.5 15.2 %collective-permute-start.7 = (bf16[144,1024]{1,0:T(8,128)(2,1)S(1)}, bf16[144,1024]{1,0:T(8,128)(2,1)S(1)}, u32[]{:S(2)}, u32[]{:S(2)}) collective-permute-start(bf16[144,1024]{1,0:T(8,128)(2,1)S(1)} %slice_select_fusion), channel_id=1, source_target_pairs={{0,8},{1,9},{2,10},{3,11},{4,12},{5,13},{6,14},{7,15},{8,0},{9,1},... | collective-permute-start | bytes 884744 | tf_op jit(solution)/shard_map/ppermute | solution.py:199
  91.1 13.4 %collective-permute-start.12 = (bf16[144,1024]{1,0:T(8,128)(2,1)S(1)}, bf16[144,1024]{1,0:T(8,128)(2,1)S(1)}, u32[]{:S(2)}, u32[]{:S(2)}) collective-permute-start(bf16[144,1024]{1,0:T(8,128)(2,1)S(1)} %broadcast_select_fusion.3.refs_0_), channel_id=1, source_target_pairs={{0,4},{1,5},{2,6},{3,7},{4,0},{5,1},{6,2},{7,3},{8,12},{9,13},{10,... | collective-permute-start | bytes 884744 | tf_op jit(solution)/shard_map/ppermute | solution.py:199
  91.1 23.8 %collective-permute-start.8 = (bf16[144,1024]{1,0:T(8,128)(2,1)S(1)}, bf16[144,1024]{1,0:T(8,128)(2,1)S(1)}, u32[]{:S(2)}, u32[]{:S(2)}) collective-permute-start(bf16[144,1024]{1,0:T(8,128)(2,1)S(1)} %broadcast_select_fusion.3.refs_0_), channel_id=1, source_target_pairs={{0,1},{1,0},{2,3},{3,2},{4,5},{5,4},{6,7},{7,6},{8,9},{9,8},{10,11... | collective-permute-start | bytes 884744 | tf_op jit(solution)/shard_map/ppermute | solution.py:199
  92.6 20.3 %collective-permute-start.9 = (bf16[144,1024]{1,0:T(8,128)(2,1)S(1)}, bf16[144,1024]{1,0:T(8,128)(2,1)S(1)}, u32[]{:S(2)}, u32[]{:S(2)}) collective-permute-start(bf16[144,1024]{1,0:T(8,128)(2,1)S(1)} %broadcast_select_fusion.3.refs_0_), channel_id=1, source_target_pairs={{0,2},{1,3},{2,0},{3,1},{4,6},{5,7},{6,4},{7,5},{8,10},{9,11},{10,... | collective-permute-start | bytes 884744 | tf_op jit(solution)/shard_map/ppermute | solution.py:199
  93.1 48.7 %all-to-all-start.2 = ((bf16[16,512,128]{2,1,0:T(8,128)(2,1)}), bf16[16,512,128]{2,1,0:T(8,128)(2,1)}, u32[]{:S(2)}, u32[]{:S(2)}) async-start(bf16[16,512,128]{2,1,0:T(8,128)(2,1)} %bitcast.37), calls=%async_computation.2 | async-start | bytes 4194304 | tf_op jit(solution)/shard_map/all_to_all | solution.py:181
  97.6 33.8 %copy-start = (bf16[2048,256]{1,0:T(8,128)(2,1)S(1)}, bf16[2048,256]{1,0:T(8,128)(2,1)}, u32[]{:S(2)}) copy-start(bf16[2048,256]{1,0:T(8,128)(2,1)} %refs_10_.1) | copy-start | bytes 3145732
  104.5 20.8 %collective-permute-start.13 = (bf16[144,1024]{1,0:T(8,128)(2,1)S(1)}, bf16[144,1024]{1,0:T(8,128)(2,1)S(1)}, u32[]{:S(2)}, u32[]{:S(2)}) collective-permute-start(bf16[144,1024]{1,0:T(8,128)(2,1)S(1)} %collective-permute-done.12.refs_5_), channel_id=1, source_target_pairs={{0,1},{1,0},{2,3},{3,2},{4,5},{5,4},{6,7},{7,6},{8,9},{9,8},{10,11... | collective-permute-start | bytes 884744 | tf_op jit(solution)/shard_map/ppermute | solution.py:199
  104.5 19.5 %collective-permute-start.14 = (bf16[144,1024]{1,0:T(8,128)(2,1)S(1)}, bf16[144,1024]{1,0:T(8,128)(2,1)S(1)}, u32[]{:S(2)}, u32[]{:S(2)}) collective-permute-start(bf16[144,1024]{1,0:T(8,128)(2,1)S(1)} %collective-permute-done.12.refs_5_), channel_id=1, source_target_pairs={{0,2},{1,3},{2,0},{3,1},{4,6},{5,7},{6,4},{7,5},{8,10},{9,11},{10,... | collective-permute-start | bytes 884744 | tf_op jit(solution)/shard_map/ppermute | solution.py:199
  112.9 15.0 %collective-permute-start.10 = (bf16[144,512]{1,0:T(8,128)(2,1)S(1)}, bf16[144,512]{1,0:T(8,128)(2,1)S(1)}, u32[]{:S(2)}, u32[]{:S(2)}) collective-permute-start(bf16[144,512]{1,0:T(8,128)(2,1)S(1)} %slice.29), channel_id=1, source_target_pairs={{0,1},{1,0},{2,3},{3,2},{4,5},{5,4},{6,7},{7,6},{8,9},{9,8},{10,11... | collective-permute-start | bytes 442376 | tf_op jit(solution)/shard_map/ppermute | solution.py:199
  115.0 12.9 %collective-permute-start.11 = (bf16[144,512]{1,0:T(8,128)(2,1)S(1)}, bf16[144,512]{1,0:T(8,128)(2,1)S(1)}, u32[]{:S(2)}, u32[]{:S(2)}) collective-permute-start(bf16[144,512]{1,0:T(8,128)(2,1)S(1)} %slice.35), channel_id=1, source_target_pairs={{0,2},{1,3},{2,0},{3,1},{4,6},{5,7},{6,4},{7,5},{8,10},{9,11},{10,... | collective-permute-start | bytes 442376 | tf_op jit(solution)/shard_map/ppermute | solution.py:199
  124.0 6.7 %collective-permute-start.15 = (bf16[144,512]{1,0:T(8,128)(2,1)S(1)}, bf16[144,512]{1,0:T(8,128)(2,1)S(1)}, u32[]{:S(2)}, u32[]{:S(2)}) collective-permute-start(bf16[144,512]{1,0:T(8,128)(2,1)S(1)} %slice.36), channel_id=1, source_target_pairs={{0,1},{1,0},{2,3},{3,2},{4,5},{5,4},{6,7},{7,6},{8,9},{9,8},{10,11... | collective-permute-start | bytes 442376 | tf_op jit(solution)/shard_map/ppermute | solution.py:199
  125.3 6.1 %collective-permute-start.16 = (bf16[144,512]{1,0:T(8,128)(2,1)S(1)}, bf16[144,512]{1,0:T(8,128)(2,1)S(1)}, u32[]{:S(2)}, u32[]{:S(2)}) collective-permute-start(bf16[144,512]{1,0:T(8,128)(2,1)S(1)} %slice.37), channel_id=1, source_target_pairs={{0,2},{1,3},{2,0},{3,1},{4,6},{5,7},{6,4},{7,5},{8,10},{9,11},{10,... | collective-permute-start | bytes 442376 | tf_op jit(solution)/shard_map/ppermute | solution.py:199
  134.7 2.7 %collective-permute-start.17 = (f32[512,512]{1,0:T(8,128)S(1)}, f32[512,512]{1,0:T(8,128)S(1)}, u32[]{:S(2)}, u32[]{:S(2)}) collective-permute-start(f32[512,512]{1,0:T(8,128)S(1)} %get-tuple-element.29), channel_id=1, source_target_pairs={{0,16},{16,0},{1,17},{17,1},{2,18},{18,2},{3,19},{19,3},{4,20},{20... | collective-permute-start | bytes 3145736 | tf_op jit(solution)/shard_map/ppermute | solution.py:207
  141.8 25.2 %all-to-all-start.3 = ((bf16[16,128,128]{2,1,0:T(8,128)(2,1)}), bf16[16,128,128]{2,1,0:T(8,128)(2,1)S(1)}, u32[]{:S(2)}, u32[]{:S(2)}) async-start(bf16[16,128,128]{2,1,0:T(8,128)(2,1)} %bitcast.23), calls=%async_computation.3 | async-start | bytes 1048576 | tf_op jit(solution)/shard_map/all_to_all | solution.py:181

commit v5 on v4

--- a/solution.py
+++ b/solution.py
@@ -17,6 +17,10 @@
     return pltpu.CompilerParams(vmem_limit_bytes=mebibytes * 1024 * 1024)
 
 
+def small():
+    return pl.CostEstimate(flops=0, bytes_accessed=4 * 1024 * 1024, transcendentals=0)
+
+
 def pack(arrays, n, items, part):
     rows, columns = arrays[0].shape
     width = columns // n
@@ -36,6 +40,7 @@
         out_specs=pl.BlockSpec((per, len(items), rows, part), lambda i: (i, 0, 0, 0)),
         out_shape=jax.ShapeDtypeStruct((n, len(items), rows, part), arrays[0].dtype),
         compiler_params=params(60),
+        cost_estimate=small(),
         name="pack",
     )(*[arrays[a] for a in used])
 
@@ -59,31 +64,27 @@
         out_specs=pl.BlockSpec((rows, per * width), lambda i: (0, i)),
         out_shape=jax.ShapeDtypeStruct((rows, n * width), parts[0].dtype),
         compiler_params=params(),
+        cost_estimate=small(),
         name="unpack",
     )(*parts)
 
 
-def result_blocks(n, step, rows, turned):
-    if turned:
-        lines = n // QUAD
-        return (lines, QUAD, rows), pl.BlockSpec(
-            (lines, 1, rows, HEAD), lambda h, i, *_: (0, i, 0, h)
-        )
-    return (n // step, step, rows), pl.BlockSpec(
-        (1, step, rows, HEAD), lambda h, i, *_: (i, 0, 0, h)
-    )
-
-
-def self_attention(blocks, first, turned):
+def self_attention(blocks, first, place=None):
     n, _, rows, width = blocks.shape
     heads = width // HEAD
     tokens = n * rows
     per = max(1, min(n, 256 // rows))
-    step = n // QUAD if turned else 2 * per
     factor = LOG2E / HEAD**0.5
-    shape, out_block = result_blocks(n, step, rows, turned)
-
-    def body(q_ref, k_ref, v_ref, out_ref, values):
+    if place is None:
+        step, place = 2 * per, jnp.zeros(1, jnp.int32)
+        shape = (n // step, step, rows)
+        out_block = pl.BlockSpec((1, step, rows, HEAD), lambda h, i, _: (i, 0, 0, h))
+    else:
+        step, place = n // QUAD, place.reshape(1)
+        shape = (step, QUAD, rows)
+        out_block = pl.BlockSpec((step, 1, rows, HEAD), lambda h, i, p: (0, i ^ p[0], 0, h))
+
+    def body(_, q_ref, k_ref, v_ref, out_ref, values):
         @pl.when(pl.program_id(1) == 0)
         def _():
             values[:, :HEAD] = v_ref[:, 0].reshape(tokens, HEAD)
@@ -104,15 +105,18 @@
 
     return pl.pallas_call(
         body,
-        grid=(heads, n // step),
-        in_specs=[
-            pl.BlockSpec((step, 1, rows, HEAD), lambda h, i: (i, first, 0, h)),
-            pl.BlockSpec((n, 1, rows, HEAD), lambda h, i: (0, first + 1, 0, h)),
-            pl.BlockSpec((n, 1, rows, HEAD), lambda h, i: (0, first + 2, 0, h)),
-        ],
-        out_specs=out_block,
+        grid_spec=pltpu.PrefetchScalarGridSpec(
+            num_scalar_prefetch=1,
+            grid=(heads, n // step),
+            in_specs=[
+                pl.BlockSpec((step, 1, rows, HEAD), lambda h, i, _: (i, first, 0, h)),
+                pl.BlockSpec((n, 1, rows, HEAD), lambda h, i, _: (0, first + 1, 0, h)),
+                pl.BlockSpec((n, 1, rows, HEAD), lambda h, i, _: (0, first + 2, 0, h)),
+            ],
+            out_specs=out_block,
+            scratch_shapes=[pltpu.VMEM((tokens, 2 * HEAD), jnp.bfloat16)],
+        ),
         out_shape=jax.ShapeDtypeStruct((*shape, width), jnp.bfloat16),
-        scratch_shapes=[pltpu.VMEM((tokens, 2 * HEAD), jnp.bfloat16)],
         compiler_params=params(),
         cost_estimate=pl.CostEstimate(
             flops=16 * heads * tokens * tokens * HEAD,
@@ -120,19 +124,26 @@
             transcendentals=heads * tokens * tokens,
         ),
         name="self_attention",
-    )(blocks, blocks, blocks).reshape(n, rows, width)
-
-
-def cross_attention(blocks, item, text, head, length, self_out, turned):
+    )(place, blocks, blocks, blocks).reshape(n, rows, width)
+
+
+def cross_attention(blocks, item, text, head, length, self_out, place=None):
     n, _, rows, width = blocks.shape
     heads = width // HEAD
     positions = text.shape[0]
     values_at = text.shape[1] // HEAD // 2 + head
-    step = n // QUAD if turned else max(1, min(n, 512 // rows))
+    step = max(1, min(n, 512 // rows))
     factor = LOG2E / HEAD**0.5
-    shape, out_block = result_blocks(n, step, rows, turned)
-
-    def body(length_ref, q_ref, k_ref, v_ref, self_ref, out_ref, values):
+    if place is None:
+        place = jnp.zeros(1, jnp.int32)
+        shape = (n // step, step, rows)
+        out_block = pl.BlockSpec((1, step, rows, HEAD), lambda h, i, *_: (i, 0, 0, h))
+    else:
+        step, place = n // QUAD, place.reshape(1)
+        shape = (step, QUAD, rows)
+        out_block = pl.BlockSpec((step, 1, rows, HEAD), lambda h, i, _, p: (0, i ^ p[0], 0, h))
+
+    def body(length_ref, _, q_ref, k_ref, v_ref, self_ref, out_ref, values):
         @pl.when(pl.program_id(1) == 0)
         def _():
             values[:, :HEAD] = v_ref[...]
@@ -154,12 +165,12 @@
     return pl.pallas_call(
         body,
         grid_spec=pltpu.PrefetchScalarGridSpec(
-            num_scalar_prefetch=1,
+            num_scalar_prefetch=2,
             grid=(heads, n // step),
             in_specs=[
-                pl.BlockSpec((step, 1, rows, HEAD), lambda h, i, _: (i, item, 0, h)),
-                pl.BlockSpec((positions, HEAD), lambda h, i, _: (0, head + h)),
-                pl.BlockSpec((positions, HEAD), lambda h, i, _: (0, values_at + h)),
+                pl.BlockSpec((step, 1, rows, HEAD), lambda h, i, *_: (i, item, 0, h)),
+                pl.BlockSpec((positions, HEAD), lambda h, i, *_: (0, head + h)),
+                pl.BlockSpec((positions, HEAD), lambda h, i, *_: (0, values_at + h)),
                 out_block,
             ],
             out_specs=out_block,
@@ -173,7 +184,7 @@
             transcendentals=heads * n * rows * positions,
         ),
         name="cross_attention",
-    )(length, blocks, text, text, self_out.reshape(*shape, width)).reshape(n, rows, width)
+    )(length, place, blocks, text, text, self_out.reshape(*shape, width)).reshape(n, rows, width)
 
 
 def spread(blocks, groups=None):
@@ -188,11 +199,33 @@
     return spread(blocks, [[q + QUAD * z for z in range(n // QUAD)] for q in range(QUAD)])
 
 
-def spread_planes(blocks):
+def join(parts):
+    count = len(parts)
+    planes, *rest = parts[0].shape
+
+    def body(*refs):
+        for i in range(count):
+            refs[count][i] = refs[i][...]
+
+    return pl.pallas_call(
+        body,
+        grid=(planes,),
+        in_specs=[pl.BlockSpec((1, *rest), lambda i: (i, 0, 0, 0))] * count,
+        out_specs=pl.BlockSpec((count, 1, *rest), lambda i: (0, i, 0, 0, 0)),
+        out_shape=jax.ShapeDtypeStruct((count, planes, *rest), parts[0].dtype),
+        compiler_params=params(),
+        cost_estimate=pl.CostEstimate(
+            flops=10000000000, bytes_accessed=4 * 1024 * 1024, transcendentals=0
+        ),
+        name="join",
+    )(*parts).reshape(count * planes, *rest)
+
+
+def spread_planes(blocks, place):
     n = blocks.shape[0]
-    shape = blocks.shape[1:]
-    turned = blocks.reshape(n // QUAD, QUAD, *shape).swapaxes(0, 1).reshape(n, *shape)
-    return spread(turned, [[QUAD * z + q for q in range(QUAD)] for z in range(n // QUAD)])
+    lines = blocks.reshape(n // QUAD, QUAD, *blocks.shape[1:])
+    sent = [lax.dynamic_index_in_dim(lines, place ^ r, 1, keepdims=False) for r in range(QUAD)]
+    return join([sent[0]] + [exchange(sent[r], r, n) for r in range(1, QUAD)])
 
 
 def exchange(value, apart, n):
@@ -248,6 +281,7 @@
         ),
         out_shape=[jax.ShapeDtypeStruct((2, rows, part), embed.dtype)] * 4,
         compiler_params=params(),
+        cost_estimate=small(),
         name="quarters",
     )(where, embed, other)
 
@@ -306,13 +340,13 @@
         out_shape=[jax.ShapeDtypeStruct((positions, 2 * width), jnp.float32)] * 2,
         compiler_params=params(),
         cost_estimate=pl.CostEstimate(
-            flops=18000000000, bytes_accessed=8 * 1024 * 1024, transcendentals=0
+            flops=7000000000, bytes_accessed=8 * 1024 * 1024, transcendentals=0
         ),
         name="project",
     )(where, *pieces, key_weight, value_weight)
 
 
-def text_of_pair(embed, key_weight, value_weight, length, encoder, n, between, after):
+def text_of_pair(embed, key_weight, value_weight, length, encoder, n, before, between, after):
     positions, columns = embed.shape
     core = lax.axis_index("dp")
     me = lax.axis_index("seq")
@@ -346,12 +380,13 @@
         piece = choose(piece, exchange(piece, 1 << bit, n), bit)
     near = (me >> 2) & 1
     own = jnp.where(near == 0, piece[:, : half // 2], piece[:, half // 2 :])
+    own = before(own)
     own = between(choose(own, exchange(own, 1 << last, n), last))
-    far, own_x, own_y = exchange(own, 4, n), exchange(own, 1, n), after(exchange(own, 2, n))
+    far, own_x, own_y = exchange(own, 4, n), exchange(own, 1, n), exchange(own, 2, n)
     pieces = []
     for here, at_x, at_y in (
         (own, own_x, own_y),
-        (far, exchange(far, 1, n), exchange(far, 2, n)),
+        (far, exchange(far, 1, n), after(exchange(far, 2, n))),
     ):
         across_a = exchange(at_y[:, : half // 4], 1, n)
         across_b = exchange(at_x[:, half // 4 :], 2, n)
@@ -390,20 +425,30 @@
     if n_dp != 2 or n < 16 or n & (n - 1) or heads % 2:
         blocks = spread(pack(inputs, n, [(a, 0) for a in range(4)], heads * HEAD))
         text = text_of_clip(embed, *weights, encoder_index[0])
-        self_out = self_attention(blocks, 0, False)
-        out = cross_attention(blocks, 3, text, 0, text_lengths, self_out, False)
+        self_out = self_attention(blocks, 0)
+        out = cross_attention(blocks, 3, text, 0, text_lengths, self_out)
         return unpack([spread(out)])[None]
 
     part = heads // 2 * HEAD
+    place = lax.axis_index("seq") & (QUAD - 1)
     lines = spread_lines(pack(inputs, n, [(a, 0) for a in range(4)], part))
-    rest = pack(inputs, n, [(a, 1) for a in range(4)], part)
-    earlier = spread_planes(lines)
+    cross_second = pack(inputs, n, [(3, 1)], part)
+    lines, cross_second = lax.optimization_barrier((lines, cross_second))
+    cross_second = spread(cross_second)
+    earlier = spread_planes(lines[:, :3], place)
+    cross_first = spread_planes(lines[:, 3:], place)
+    rest = pack(inputs, n, [(a, 1) for a in range(3)], part)
     self_first = later = None
+
+    def before(piece):
+        nonlocal cross_second
+        piece, cross_second = lax.optimization_barrier((piece, cross_second))
+        return piece
 
     def between(piece):
         nonlocal rest, earlier, self_first, later
         piece, rest, earlier = lax.optimization_barrier((piece, rest, earlier))
-        self_first = self_attention(earlier, 0, True)
+        self_first = self_attention(earlier, 0, place)
         later = spread(rest)
         return piece
 
@@ -413,13 +458,13 @@
         return piece
 
     text = text_of_pair(
-        embed, *weights, text_lengths[0], encoder_index[0], n, between, after
-    )
-    out = cross_attention(earlier, 3, text, 0, text_lengths, self_first, True)
+        embed, *weights, text_lengths[0], encoder_index[0], n, before, between, after
+    )
+    out = cross_attention(cross_first, 0, text, 0, text_lengths, self_first, place)
     later, out = lax.optimization_barrier((later, out))
     tokens = spread(out)
-    self_second = self_attention(later, 0, False)
-    out = cross_attention(later, 3, text, heads // 2, text_lengths, self_second, False)
+    self_second = self_attention(later, 0)
+    out = cross_attention(cross_second, 0, text, heads // 2, text_lengths, self_second)
     tokens, out = lax.optimization_barrier((tokens, out))
     return unpack([tokens, spread(out)])[None]
 

time: 190 us -> 185 us (0.974)
  waiting for transfers between devices: 71.7 us -> 61.8 us
  starting transfers between devices: 42.6 us -> 47.6 us
  local copies, waits for them, and re-layouts: 4.7 us -> 7.75 us
  blocking collectives: 20 us -> 18 us
    ppermute x15 -> x21, starting transfers between devices: 18 us -> 26.7 us  [exchange(): return lax.ppermute(value, 'seq', [(i, i ^ apart) for i in range(n)])]
    ppermute x15 -> x21, waiting for transfers between devices: 48.7 us -> 42.9 us  [exchange(): return lax.ppermute(value, 'seq', [(i, i ^ apart) for i in range(n)])]
    all_to_all x4, waiting for transfers between devices: 19.5 us -> 15.6 us  [spread(): lax.all_to_all(flat, 'seq', split_axis=0, concat_axis=0, tiled=True, axis...]
    all_to_all x4, starting transfers between devices: 23.9 us -> 20.2 us  [spread(): lax.all_to_all(flat, 'seq', split_axis=0, concat_axis=0, tiled=True, axis...]
    another operation x1 -> x0, local copies, waits for them, and re-layouts: 3.19 us -> none  [spread_planes(): blocks.reshape(n // QUAD, QUAD, *shape).swapaxes(0, 1).reshape(n, *shape)]
    pallas_call x2 -> x3, Pallas kernels: 8.56 us -> 11.5 us  [pack(): pl.pallas_call(body, grid=(n // per,), in_specs=[pl.BlockSpec((rows, per...]
    slice x0 -> x2, local copies, waits for them, and re-layouts: none -> 2.6 us  [the longest x1 1.52 us: shards(): earlier = spread_planes(lines[:, :3], place)]
    unnamed x4 -> x8, local copies, waits for them, and re-layouts: 0.82 us -> 3.34 us
  transfers between devices with their start and end apart: 22 -> 28, of which waited for: 15 -> 17; matrix products, arithmetic and copies ran while one was open for 4% -> 4% of each run, Pallas kernels for 22% -> 23%
where the time goes in v5:
time: 185 us; the launch traced here: 184 us
  waiting for transfers between devices  61.8 us (33%)
  starting transfers between devices  47.6 us (26%)
  Pallas kernels  43.3 us (23%)
  blocking collectives  18 us (10%)
  local copies, waits for them, and re-layouts  7.75 us (4%)
  between operations  3.56 us (2%)
  other arithmetic  2.4 us (1%)
    ppermute x21, waiting for transfers between devices, exchange(): return lax.ppermute(value, 'seq', [(i, i ^ apart) for i in range(n)])  42.9 us
    ppermute x21, starting transfers between devices, exchange(): return lax.ppermute(value, 'seq', [(i, i ^ apart) for i in range(n)])  26.7 us
    all_to_all x4, starting transfers between devices, spread(): lax.all_to_all(flat, 'seq', split_axis=0, concat_axis=0, tiled=True, axis...  20.2 us
    all_to_all x1, blocking collectives, spread(): lax.all_to_all(flat, 'seq', split_axis=0, concat_axis=0, tiled=True, axis...  18 us
    pallas_call x2, Pallas kernels, self_attention(): pl.pallas_call(body, grid_spec=pltpu.PrefetchScalarGridSpec(num_scalar_pr...  16.6 us
    all_to_all x4, waiting for transfers between devices, spread(): lax.all_to_all(flat, 'seq', split_axis=0, concat_axis=0, tiled=True, axis...  15.6 us
    pallas_call x3, Pallas kernels, pack(): pl.pallas_call(body, grid=(n // per,), in_specs=[pl.BlockSpec((rows, per...  11.5 us
    pallas_call x2, Pallas kernels, cross_attention(): pl.pallas_call(body, grid_spec=pltpu.PrefetchScalarGridSpec(num_scalar_pr...  6.82 us
  transfers between devices with their start and end apart: 28, of which 17 were waited for; matrix products, arithmetic and copies ran while one was open for 4% of the time, Pallas kernels for 23%

profile of v5, /device:TPU:0, one launch (start us, length us, event | category | flops | bytes accessed | tf_op | source)
XLA Modules:
  0.0 184.4 jit_solution(5858170475305706594)
XLA Ops:
  0.0 0.5 collective-permute-start.1
  0.5 4.3 %pack.3 = bf16[16,4,128,128]{3,2,1,0:T(8,128)(2,1)} custom-call(bf16[128,4096]{1,0:T(8,128)(2,1)} %bitcast.66, bf16[128,4096]{1,0:T(8,128)(2,1)} %bitcast.68, bf16[128,4096]{1,0:T(8,128)(2,1)} %bitcast.70, bf16[128,4096]{1,0:T(8,128)(2,1)} %bitcast.64), custom_call_target="tpu_custom_call" | custom-call | bytes 4194304 | tf_op jit(solution)/shard_map/pack/pallas_call | solution.py:36
  4.7 5.9 %all-to-all-start = ((bf16[16,512,128]{2,1,0:T(8,128)(2,1)}), bf16[16,512,128]{2,1,0:T(8,128)(2,1)}, u32[]{:S(2)}, u32[]{:S(2)}) async-start(bf16[16,512,128]{2,1,0:T(8,128)(2,1)} %bitcast.59), calls=%async_computation | async-start | bytes 4194304 | tf_op jit(solution)/shard_map/all_to_all | solution.py:192
  12.0 0.2 collective-permute-start
  12.2 0.9 collective-permute-done
  13.1 0.6 fusion.1
  14.4 3.0 %quarters.1 = (bf16[2,144,1024]{2,1,0:T(8,128)(2,1)S(1)}, bf16[2,144,1024]{2,1,0:T(8,128)(2,1)S(1)}, bf16[2,144,1024]{2,1,0:T(8,128)(2,1)S(1)}, bf16[2,144,1024]{2,1,0:T(8,128)(2,1)S(1)}) custom-call(s32[3]{0:T(128)S(1)} %pad_add_fusion.1.where_ref, bf16[512,4096]{1,0:T(8,128)(2,1)} %bitcast.63, bf16[512,4096]{1,0:T(8,128)(2,1)} %collective-permute-done.1.other_ref), custom_call_target="tpu_custom_call" | custom-call | bytes 4194304 | tf_op jit(solution)/shard_map/quarters/pallas_call | solution.py:274
  17.4 1.6 collective-permute-start.4
  20.3 1.6 collective-permute-start.2
  21.9 11.0 %collective-permute-done.4 = bf16[2,144,1024]{2,1,0:T(8,128)(2,1)S(1)} collective-permute-done((bf16[2,144,1024]{2,1,0:T(8,128)(2,1)S(1)}, bf16[2,144,1024]{2,1,0:T(8,128)(2,1)S(1)}, u32[]{:S(2)}, u32[]{:S(2)}) %collective-permute-start.4) | collective-permute-done | bytes 589856 | tf_op jit(solution)/shard_map/ppermute | solution.py:232
  32.9 0.1 broadcast_select_fusion
  33.0 1.6 collective-permute-start.5
  34.6 1.2 collective-permute-done.2
  35.7 0.1 broadcast_select_fusion.1
  35.9 0.4 collective-permute-start.3
  36.3 5.4 %collective-permute-done.5 = bf16[144,1024]{1,0:T(8,128)(2,1)S(1)} collective-permute-done((bf16[144,1024]{1,0:T(8,128)(2,1)S(1)}, bf16[144,1024]{1,0:T(8,128)(2,1)S(1)}, u32[]{:S(2)}, u32[]{:S(2)}) %collective-permute-start.5) | collective-permute-done | bytes 294944 | tf_op jit(solution)/shard_map/ppermute | solution.py:232
  41.9 1.8 collective-permute-done.3
  43.9 2.1 %collective-permute-start.6 = (bf16[144,2048]{1,0:T(8,128)(2,1)S(1)}, bf16[144,2048]{1,0:T(8,128)(2,1)}, u32[]{:S(2)}, u32[]{:S(2)}) collective-permute-start(bf16[144,2048]{1,0:T(8,128)(2,1)S(1)} %pad_maximum_fusion), channel_id=1, source_target_pairs={{0,4},{1,5},{2,6},{3,7},{4,0},{5,1},{6,2},{7,3},{8,12},{9,13},{10,... | collective-permute-start | bytes 1769480 | tf_op jit(solution)/shard_map/ppermute | solution.py:232
  45.9 3.3 %pack.4 = bf16[16,1,128,128]{3,2,1,0:T(8,128)(2,1)} custom-call(bf16[128,4096]{1,0:T(8,128)(2,1)} %bitcast.65), custom_call_target="tpu_custom_call" | custom-call | bytes 4194304 | tf_op jit(solution)/shard_map/pack/pallas_call | solution.py:36
  49.2 3.9 %pack.5 = bf16[16,3,128,128]{3,2,1,0:T(8,128)(2,1)} custom-call(bf16[128,4096]{1,0:T(8,128)(2,1)} %bitcast.67, bf16[128,4096]{1,0:T(8,128)(2,1)} %bitcast.69, bf16[128,4096]{1,0:T(8,128)(2,1)} %bitcast.71), custom_call_target="tpu_custom_call" | custom-call | bytes 4194304 | tf_op jit(solution)/shard_map/pack/pallas_call | solution.py:36
  53.1 6.6 %all-to-all-done = bf16[16,512,128]{2,1,0:T(8,128)(2,1)} async-done(((bf16[16,512,128]{2,1,0:T(8,128)(2,1)}), bf16[16,512,128]{2,1,0:T(8,128)(2,1)}, u32[]{:S(2)}, u32[]{:S(2)}) %all-to-all-start) | async-done | bytes 2097184 | tf_op jit(solution)/shard_map/all_to_all | solution.py:192
  59.7 4.7 %all-to-all-start.1 = ((bf16[16,128,128]{2,1,0:T(8,128)(2,1)}), bf16[16,128,128]{2,1,0:T(8,128)(2,1)S(1)}, u32[]{:S(2)}, u32[]{:S(2)}) async-start(bf16[16,128,128]{2,1,0:T(8,128)(2,1)} %bitcast.15), calls=%async_computation.1 | async-start | bytes 1048576 | tf_op jit(solution)/shard_map/all_to_all | solution.py:192
  64.4 1.5 slice.35
  66.0 1.1 dynamic-slice_bitcast_fusion
  67.0 1.9 %collective-permute-start.8 = (bf16[4,3,128,128]{3,2,1,0:T(8,128)(2,1)}, bf16[4,3,128,128]{3,2,1,0:T(8,128)(2,1)S(1)}, u32[]{:S(2)}, u32[]{:S(2)}) collective-permute-start(bf16[4,3,128,128]{3,2,1,0:T(8,128)(2,1)} %get-tuple-element.45), channel_id=1, source_target_pairs={{0,1},{1,0},{2,3},{3,2},{4,5},{5,4},{6,7},{7,6},{8,9},{9,8},{10,11... | collective-permute-start | bytes 1179656 | tf_op jit(solution)/shard_map/ppermute | solution.py:232
  69.0 1.5 collective-permute-start.9
  70.5 1.7 collective-permute-done.6
  72.2 1.3 broadcast_select_fusion.2
  73.5 5.6 %all-to-all-done.1 = bf16[16,128,128]{2,1,0:T(8,128)(2,1)S(1)} async-done(((bf16[16,128,128]{2,1,0:T(8,128)(2,1)}), bf16[16,128,128]{2,1,0:T(8,128)(2,1)S(1)}, u32[]{:S(2)}, u32[]{:S(2)}) %all-to-all-start.1) | async-done | bytes 524320 | tf_op jit(solution)/shard_map/all_to_all | solution.py:192
  79.2 0.7 collective-permute-start.7
  79.9 3.3 %collective-permute-done.8.refs_1_ = bf16[4,3,128,128]{3,2,1,0:T(8,128)(2,1)S(1)} collective-permute-done((bf16[4,3,128,128]{3,2,1,0:T(8,128)(2,1)}, bf16[4,3,128,128]{3,2,1,0:T(8,128)(2,1)S(1)}, u32[]{:S(2)}, u32[]{:S(2)}) %collective-permute-start.8) | collective-permute-done | bytes 393248 | tf_op jit(solution)/shard_map/ppermute | solution.py:232
  83.2 6.2 %collective-permute-done.9.refs_2_ = bf16[4,3,128,128]{3,2,1,0:T(8,128)(2,1)S(1)} collective-permute-done((bf16[4,3,128,128]{3,2,1,0:T(8,128)(2,1)}, bf16[4,3,128,128]{3,2,1,0:T(8,128)(2,1)S(1)}, u32[]{:S(2)}, u32[]{:S(2)}) %collective-permute-start.9) | collective-permute-done | bytes 393248 | tf_op jit(solution)/shard_map/ppermute | solution.py:232
  89.4 1.6 collective-permute-done.10.refs_3_
  91.1 0.3 join.2
  91.3 1.1 copy-done.2
  92.7 1.0 collective-permute-start.18
  93.7 1.2 collective-permute-start.14
  94.9 0.6 collective-permute-start.15
  95.4 5.3 %all-to-all-start.2 = ((bf16[16,384,128]{2,1,0:T(8,128)(2,1)}), bf16[16,384,128]{2,1,0:T(8,128)(2,1)S(1)}, u32[]{:S(2)}, u32[]{:S(2)}) async-start(bf16[16,384,128]{2,1,0:T(8,128)(2,1)} %bitcast.60), calls=%async_computation.2 | async-start | bytes 3145728 | tf_op jit(solution)/shard_map/all_to_all | solution.py:192
  100.8 2.0 %collective-permute-start.19 = (bf16[144,1024]{1,0:T(8,128)(2,1)S(1)}, bf16[144,1024]{1,0:T(8,128)(2,1)S(1)}, u32[]{:S(2)}, u32[]{:S(2)}) collective-permute-start(bf16[144,1024]{1,0:T(8,128)(2,1)S(1)} %collective-permute-done.18.refs_5_), channel_id=1, source_target_pairs={{0,1},{1,0},{2,3},{3,2},{4,5},{5,4},{6,7},{7,6},{8,9},{9,8},{10,11... | collective-permute-start | bytes 884744 | tf_op jit(solution)/shard_map/ppermute | solution.py:232
  102.8 1.5 collective-permute-start.20
  104.2 1.4 copy-done.3
  105.7 8.3 %self_attention.2 = bf16[4,4,128,128]{3,2,1,0:T(8,128)(2,1)S(1)} custom-call(s32[1]{0:T(128)} %bitcast.3._, bf16[16,3,128,128]{3,2,1,0:T(8,128)(2,1)S(1)} %bitcast.55, bf16[16,3,128,128]{3,2,1,0:T(8,128)(2,1)S(1)} %bitcast.56, bf16[16,3,128,128]{3,2,1,0:T(8,128)(2,1)S(1)} %bitcast.57), custom_call_target="tpu_custom_call" | custom-call | flops 8589934592 | bytes 2097152 | tf_op jit(solution)/shard_map/self_attention/pallas_call | solution.py:106
  114.0 0.6 collective-permute-start.16
  114.7 0.2 collective-permute-start.17
  114.8 7.0 %collective-permute-done.20.refs_7_ = bf16[144,1024]{1,0:T(8,128)(2,1)S(1)} collective-permute-done((bf16[144,1024]{1,0:T(8,128)(2,1)S(1)}, bf16[144,1024]{1,0:T(8,128)(2,1)S(1)}, u32[]{:S(2)}, u32[]{:S(2)}) %collective-permute-start.20) | collective-permute-done | bytes 294944 | tf_op jit(solution)/shard_map/ppermute | solution.py:232
  121.9 2.1 %collective-permute-start.21 = (bf16[144,512]{1,0:T(8,128)(2,1)S(1)}, bf16[144,512]{1,0:T(8,128)(2,1)S(1)}, u32[]{:S(2)}, u32[]{:S(2)}) collective-permute-start(bf16[144,512]{1,0:T(8,128)(2,1)S(1)} %slice.39), channel_id=1, source_target_pairs={{0,1},{1,0},{2,3},{3,2},{4,5},{5,4},{6,7},{7,6},{8,9},{9,8},{10,11... | collective-permute-start | bytes 442376 | tf_op jit(solution)/shard_map/ppermute | solution.py:232
  124.0 2.7 %collective-permute-start.22 = (bf16[144,512]{1,0:T(8,128)(2,1)S(1)}, bf16[144,512]{1,0:T(8,128)(2,1)S(1)}, u32[]{:S(2)}, u32[]{:S(2)}) collective-permute-start(bf16[144,512]{1,0:T(8,128)(2,1)S(1)} %slice.45), channel_id=1, source_target_pairs={{0,2},{1,3},{2,0},{3,1},{4,6},{5,7},{6,4},{7,5},{8,10},{9,11},{10,... | collective-permute-start | bytes 442376 | tf_op jit(solution)/shard_map/ppermute | solution.py:232
  126.7 1.1 slice.36
  128.1 3.4 %collective-permute-start.13 = (bf16[4,1,128,128]{3,2,1,0:T(8,128)(2,1)S(1)}, bf16[4,1,128,128]{3,2,1,0:T(8,128)(2,1)S(1)}, u32[]{:S(2)}, u32[]{:S(2)}) collective-permute-start(bf16[4,1,128,128]{3,2,1,0:T(8,128)(2,1)S(1)} %get-tuple-element.47), channel_id=1, source_target_pairs={{0,3},{1,2},{2,1},{3,0},{4,7},{5,6},{6,5},{7,4},{8,11},{9,10},{10,... | collective-permute-start | bytes 393224 | tf_op jit(solution)/shard_map/ppermute | solution.py:232
  131.4 1.9 %collective-permute-done.21.refs_8_ = bf16[144,512]{1,0:T(8,128)(2,1)S(1)} collective-permute-done((bf16[144,512]{1,0:T(8,128)(2,1)S(1)}, bf16[144,512]{1,0:T(8,128)(2,1)S(1)}, u32[]{:S(2)}, u32[]{:S(2)}) %collective-permute-start.21) | collective-permute-done | bytes 147488 | tf_op jit(solution)/shard_map/ppermute | solution.py:232
  133.4 1.5 collective-permute-done.22.refs_9_
  134.9 3.4 %project.1 = (f32[512,512]{1,0:T(8,128)S(1)}, f32[512,512]{1,0:T(8,128)S(1)}) custom-call(s32[3]{0:T(128)S(1)} %pad_add_fusion.2.where_ref, bf16[144,1024]{1,0:T(8,128)(2,1)S(1)} %broadcast_select_fusion.3.refs_0_, bf16[144,1024]{1,0:T(8,128)(2,1)S(1)} %collective-permute-done.14.refs_1_, bf16[144,1024]{1,0:T(8,128)(2,1)S(1)} %collective-permute-done.15.refs_2_, ...), custom_call_target="tpu_custom_call" | custom-call | flops 7000000000 | bytes 8388608 | tf_op jit(solution)/shard_map/project/pallas_call | solution.py:331
  138.4 0.2 join.3
  138.6 2.5 %collective-permute-done.23 = f32[512,512]{1,0:T(8,128)S(1)} collective-permute-done((f32[512,512]{1,0:T(8,128)S(1)}, f32[512,512]{1,0:T(8,128)S(1)}, u32[]{:S(2)}, u32[]{:S(2)}) %collective-permute-start.23) | collective-permute-done | bytes 1048608 | tf_op jit(solution)/shard_map/ppermute | solution.py:240
  141.0 0.3 add_convert_fusion.k_ref.v_ref
  141.3 3.5 %cross_attention.2 = bf16[4,4,128,128]{3,2,1,0:T(8,128)(2,1)S(1)} custom-call(s32[1]{0:T(128)S(6)} %copy.10.length_ref, s32[1]{0:T(128)} %bitcast.3._, bf16[16,1,128,128]{3,2,1,0:T(8,128)(2,1)S(1)} %bitcast.58, bf16[512,512]{1,0:T(8,128)(2,1)S(1)} %add_convert_fusion.k_ref.v_ref, bf16[512,512]{1,0:T(8,128)(2,1)S(1)} %add_convert_fusion.k_ref.v_ref, ...), custom_call_target="tpu_custom_call" | custom-call | flops 4294967296 | bytes 1572864 | tf_op jit(solution)/shard_map/cross_attention/pallas_call | solution.py:165
  144.8 0.8 copy-done
  145.5 4.2 %all-to-all-start.3 = ((bf16[16,128,128]{2,1,0:T(8,128)(2,1)}), bf16[16,128,128]{2,1,0:T(8,128)(2,1)S(1)}, u32[]{:S(2)}, u32[]{:S(2)}) async-start(bf16[16,128,128]{2,1,0:T(8,128)(2,1)} %bitcast.53), calls=%async_computation.3 | async-start | bytes 1048576 | tf_op jit(solution)/shard_map/all_to_all | solution.py:192
  149.8 8.3 %self_attention.3.self_ref = bf16[4,4,128,128]{3,2,1,0:T(8,128)(2,1)S(1)} custom-call(s32[1]{0:T(128)} %constant.57.clone.1._, bf16[16,3,128,128]{3,2,1,0:T(8,128)(2,1)S(1)} %bitcast.49, bf16[16,3,128,128]{3,2,1,0:T(8,128)(2,1)S(1)} %bitcast.50, bf16[16,3,128,128]{3,2,1,0:T(8,128)(2,1)S(1)} %bitcast.51), custom_call_target="tpu_custom_call" | custom-call | flops 8589934592 | bytes 2097152 | tf_op jit(solution)/shard_map/self_attention/pallas_call | solution.py:106
  158.1 3.4 %cross_attention.3 = bf16[4,4,128,128]{3,2,1,0:T(8,128)(2,1)S(1)} custom-call(s32[1]{0:T(128)S(6)} %copy.10.length_ref, s32[1]{0:T(128)} %constant.57.clone.1._, bf16[16,1,128,128]{3,2,1,0:T(8,128)(2,1)S(1)} %bitcast.52, bf16[512,512]{1,0:T(8,128)(2,1)S(1)} %add_convert_fusion.k_ref.v_ref, bf16[512,512]{1,0:T(8,128)(2,1)S(1)} %add_convert_fusion.k_ref.v_ref, ...), custom_call_target="tpu_custom_call" | custom-call | flops 4294967296 | bytes 1572864 | tf_op jit(solution)/shard_map/cross_attention/pallas_call | solution.py:165
  161.4 3.4 %all-to-all-done.3.refs_0_ = bf16[16,128,128]{2,1,0:T(8,128)(2,1)S(1)} async-done(((bf16[16,128,128]{2,1,0:T(8,128)(2,1)}), bf16[16,128,128]{2,1,0:T(8,128)(2,1)S(1)}, u32[]{:S(2)}, u32[]{:S(2)}) %all-to-all-start.3) | async-done | bytes 524320 | tf_op jit(solution)/shard_map/all_to_all | solution.py:192
  164.8 18.0 %all_to_all.25.refs_1_ = bf16[16,128,128]{2,1,0:T(8,128)(2,1)S(1)} all-to-all(bf16[16,128,128]{2,1,0:T(8,128)(2,1)S(1)} %bitcast.54), channel_id=1, replica_groups=mesh['dp'=2,'seq'=16] {'seq'}, dimensions={0} | all-to-all | bytes 1048576 | tf_op jit(solution)/shard_map/all_to_all | solution.py:192
  182.7 1.6 unpack.1
  (40 shorter events, 1.2 us)
Async XLA Ops:
  0.0 14.4 %collective-permute-start.1 = (bf16[512,4096]{1,0:T(8,128)(2,1)}, bf16[512,4096]{1,0:T(8,128)(2,1)}, u32[]{:S(2)}, u32[]{:S(2)}) collective-permute-start(bf16[512,4096]{1,0:T(8,128)(2,1)} %bitcast.62), channel_id=1, source_target_pairs={{0,16},{16,0},{1,17},{17,1},{2,18},{18,2},{3,19},{19,3},{4,20},{20... | collective-permute-start | bytes 12582920 | tf_op jit(solution)/shard_map/ppermute | solution.py:240
  4.7 55.0 %all-to-all-start = ((bf16[16,512,128]{2,1,0:T(8,128)(2,1)}), bf16[16,512,128]{2,1,0:T(8,128)(2,1)}, u32[]{:S(2)}, u32[]{:S(2)}) async-start(bf16[16,512,128]{2,1,0:T(8,128)(2,1)} %bitcast.59), calls=%async_computation | async-start | bytes 4194304 | tf_op jit(solution)/shard_map/all_to_all | solution.py:192
  12.0 1.1 collective-permute-start
  17.4 15.4 %collective-permute-start.4 = (bf16[2,144,1024]{2,1,0:T(8,128)(2,1)S(1)}, bf16[2,144,1024]{2,1,0:T(8,128)(2,1)S(1)}, u32[]{:S(2)}, u32[]{:S(2)}) collective-permute-start(bf16[2,144,1024]{2,1,0:T(8,128)(2,1)S(1)} %get-tuple-element.27), channel_id=1, source_target_pairs={{0,2},{1,3},{2,0},{3,1},{4,6},{5,7},{6,4},{7,5},{8,10},{9,11},{10,... | collective-permute-start | bytes 1769480 | tf_op jit(solution)/shard_map/ppermute | solution.py:232
  20.3 15.5 %collective-permute-start.2 = (bf16[2,144,1024]{2,1,0:T(8,128)(2,1)S(1)}, bf16[2,144,1024]{2,1,0:T(8,128)(2,1)S(1)}, u32[]{:S(2)}, u32[]{:S(2)}) collective-permute-start(bf16[2,144,1024]{2,1,0:T(8,128)(2,1)S(1)} %get-tuple-element.25), channel_id=1, source_target_pairs={{0,1},{1,0},{2,3},{3,2},{4,5},{5,4},{6,7},{7,6},{8,9},{9,8},{10,11... | collective-permute-start | bytes 1769480 | tf_op jit(solution)/shard_map/ppermute | solution.py:232
  33.0 8.8 %collective-permute-start.5 = (bf16[144,1024]{1,0:T(8,128)(2,1)S(1)}, bf16[144,1024]{1,0:T(8,128)(2,1)S(1)}, u32[]{:S(2)}, u32[]{:S(2)}) collective-permute-start(bf16[144,1024]{1,0:T(8,128)(2,1)S(1)} %dynamic-slice_bitcast_fusion.4), channel_id=1, source_target_pairs={{0,1},{1,0},{2,3},{3,2},{4,5},{5,4},{6,7},{7,6},{8,9},{9,8},{10,11... | collective-permute-start | bytes 884744 | tf_op jit(solution)/shard_map/ppermute | solution.py:232
  35.9 7.8 %collective-permute-start.3 = (bf16[144,1024]{1,0:T(8,128)(2,1)S(1)}, bf16[144,1024]{1,0:T(8,128)(2,1)S(1)}, u32[]{:S(2)}, u32[]{:S(2)}) collective-permute-start(bf16[144,1024]{1,0:T(8,128)(2,1)S(1)} %dynamic-slice_bitcast_fusion.5), channel_id=1, source_target_pairs={{0,2},{1,3},{2,0},{3,1},{4,6},{5,7},{6,4},{7,5},{8,10},{9,11},{10,... | collective-permute-start | bytes 884744 | tf_op jit(solution)/shard_map/ppermute | solution.py:232
  43.9 28.4 %collective-permute-start.6 = (bf16[144,2048]{1,0:T(8,128)(2,1)S(1)}, bf16[144,2048]{1,0:T(8,128)(2,1)}, u32[]{:S(2)}, u32[]{:S(2)}) collective-permute-start(bf16[144,2048]{1,0:T(8,128)(2,1)S(1)} %pad_maximum_fusion), channel_id=1, source_target_pairs={{0,4},{1,5},{2,6},{3,7},{4,0},{5,1},{6,2},{7,3},{8,12},{9,13},{10,... | collective-permute-start | bytes 1769480 | tf_op jit(solution)/shard_map/ppermute | solution.py:232
  59.7 19.5 %all-to-all-start.1 = ((bf16[16,128,128]{2,1,0:T(8,128)(2,1)}), bf16[16,128,128]{2,1,0:T(8,128)(2,1)S(1)}, u32[]{:S(2)}, u32[]{:S(2)}) async-start(bf16[16,128,128]{2,1,0:T(8,128)(2,1)} %bitcast.15), calls=%async_computation.1 | async-start | bytes 1048576 | tf_op jit(solution)/shard_map/all_to_all | solution.py:192
  67.0 16.1 %collective-permute-start.8 = (bf16[4,3,128,128]{3,2,1,0:T(8,128)(2,1)}, bf16[4,3,128,128]{3,2,1,0:T(8,128)(2,1)S(1)}, u32[]{:S(2)}, u32[]{:S(2)}) collective-permute-start(bf16[4,3,128,128]{3,2,1,0:T(8,128)(2,1)} %get-tuple-element.45), channel_id=1, source_target_pairs={{0,1},{1,0},{2,3},{3,2},{4,5},{5,4},{6,7},{7,6},{8,9},{9,8},{10,11... | collective-permute-start | bytes 1179656 | tf_op jit(solution)/shard_map/ppermute | solution.py:232
  69.0 20.4 %collective-permute-start.9 = (bf16[4,3,128,128]{3,2,1,0:T(8,128)(2,1)}, bf16[4,3,128,128]{3,2,1,0:T(8,128)(2,1)S(1)}, u32[]{:S(2)}, u32[]{:S(2)}) collective-permute-start(bf16[4,3,128,128]{3,2,1,0:T(8,128)(2,1)} %get-tuple-element.44), channel_id=1, source_target_pairs={{0,2},{1,3},{2,0},{3,1},{4,6},{5,7},{6,4},{7,5},{8,10},{9,11},{10,... | collective-permute-start | bytes 1179656 | tf_op jit(solution)/shard_map/ppermute | solution.py:232
  70.4 20.6 %collective-permute-start.10 = (bf16[4,3,128,128]{3,2,1,0:T(8,128)(2,1)}, bf16[4,3,128,128]{3,2,1,0:T(8,128)(2,1)S(1)}, u32[]{:S(2)}, u32[]{:S(2)}) collective-permute-start(bf16[4,3,128,128]{3,2,1,0:T(8,128)(2,1)} %get-tuple-element.43), channel_id=1, source_target_pairs={{0,3},{1,2},{2,1},{3,0},{4,7},{5,6},{6,5},{7,4},{8,11},{9,10},{10,... | collective-permute-start | bytes 1179656 | tf_op jit(solution)/shard_map/ppermute | solution.py:232
  79.2 13.4 %collective-permute-start.7 = (bf16[144,1024]{1,0:T(8,128)(2,1)S(1)}, bf16[144,1024]{1,0:T(8,128)(2,1)S(1)}, u32[]{:S(2)}, u32[]{:S(2)}) collective-permute-start(bf16[144,1024]{1,0:T(8,128)(2,1)S(1)} %slice_select_fusion), channel_id=1, source_target_pairs={{0,8},{1,9},{2,10},{3,11},{4,12},{5,13},{6,14},{7,15},{8,0},{9,1},... | collective-permute-start | bytes 884744 | tf_op jit(solution)/shard_map/ppermute | solution.py:232
  91.3 1.1 copy-start.2
  92.7 8.1 %collective-permute-start.18 = (bf16[144,1024]{1,0:T(8,128)(2,1)S(1)}, bf16[144,1024]{1,0:T(8,128)(2,1)S(1)}, u32[]{:S(2)}, u32[]{:S(2)}) collective-permute-start(bf16[144,1024]{1,0:T(8,128)(2,1)S(1)} %broadcast_select_fusion.3.refs_0_), channel_id=1, source_target_pairs={{0,4},{1,5},{2,6},{3,7},{4,0},{5,1},{6,2},{7,3},{8,12},{9,13},{10,... | collective-permute-start | bytes 884744 | tf_op jit(solution)/shard_map/ppermute | solution.py:232
  93.7 21.0 %collective-permute-start.14 = (bf16[144,1024]{1,0:T(8,128)(2,1)S(1)}, bf16[144,1024]{1,0:T(8,128)(2,1)S(1)}, u32[]{:S(2)}, u32[]{:S(2)}) collective-permute-start(bf16[144,1024]{1,0:T(8,128)(2,1)S(1)} %broadcast_select_fusion.3.refs_0_), channel_id=1, source_target_pairs={{0,1},{1,0},{2,3},{3,2},{4,5},{5,4},{6,7},{7,6},{8,9},{9,8},{10,11... | collective-permute-start | bytes 884744 | tf_op jit(solution)/shard_map/ppermute | solution.py:232
  94.9 19.1 %collective-permute-start.15 = (bf16[144,1024]{1,0:T(8,128)(2,1)S(1)}, bf16[144,1024]{1,0:T(8,128)(2,1)S(1)}, u32[]{:S(2)}, u32[]{:S(2)}) collective-permute-start(bf16[144,1024]{1,0:T(8,128)(2,1)S(1)} %broadcast_select_fusion.3.refs_0_), channel_id=1, source_target_pairs={{0,2},{1,3},{2,0},{3,1},{4,6},{5,7},{6,4},{7,5},{8,10},{9,11},{10,... | collective-permute-start | bytes 884744 | tf_op jit(solution)/shard_map/ppermute | solution.py:232
  95.4 50.1 %all-to-all-start.2 = ((bf16[16,384,128]{2,1,0:T(8,128)(2,1)}), bf16[16,384,128]{2,1,0:T(8,128)(2,1)S(1)}, u32[]{:S(2)}, u32[]{:S(2)}) async-start(bf16[16,384,128]{2,1,0:T(8,128)(2,1)} %bitcast.60), calls=%async_computation.2 | async-start | bytes 3145728 | tf_op jit(solution)/shard_map/all_to_all | solution.py:192
  100.8 23.2 %collective-permute-start.19 = (bf16[144,1024]{1,0:T(8,128)(2,1)S(1)}, bf16[144,1024]{1,0:T(8,128)(2,1)S(1)}, u32[]{:S(2)}, u32[]{:S(2)}) collective-permute-start(bf16[144,1024]{1,0:T(8,128)(2,1)S(1)} %collective-permute-done.18.refs_5_), channel_id=1, source_target_pairs={{0,1},{1,0},{2,3},{3,2},{4,5},{5,4},{6,7},{7,6},{8,9},{9,8},{10,11... | collective-permute-start | bytes 884744 | tf_op jit(solution)/shard_map/ppermute | solution.py:232
  102.8 19.1 %collective-permute-start.20 = (bf16[144,1024]{1,0:T(8,128)(2,1)S(1)}, bf16[144,1024]{1,0:T(8,128)(2,1)S(1)}, u32[]{:S(2)}, u32[]{:S(2)}) collective-permute-start(bf16[144,1024]{1,0:T(8,128)(2,1)S(1)} %collective-permute-done.18.refs_5_), channel_id=1, source_target_pairs={{0,2},{1,3},{2,0},{3,1},{4,6},{5,7},{6,4},{7,5},{8,10},{9,11},{10,... | collective-permute-start | bytes 884744 | tf_op jit(solution)/shard_map/ppermute | solution.py:232
  104.2 1.4 copy-start.3
  114.0 20.9 %copy-start.1 = (bf16[2048,256]{1,0:T(8,128)(2,1)S(1)}, bf16[2048,256]{1,0:T(8,128)(2,1)}, u32[]{:S(2)}) copy-start(bf16[2048,256]{1,0:T(8,128)(2,1)} %refs_10_.1) | copy-start | bytes 3145732
  114.0 14.0 %collective-permute-start.16 = (bf16[144,512]{1,0:T(8,128)(2,1)S(1)}, bf16[144,512]{1,0:T(8,128)(2,1)S(1)}, u32[]{:S(2)}, u32[]{:S(2)}) collective-permute-start(bf16[144,512]{1,0:T(8,128)(2,1)S(1)} %slice.43), channel_id=1, source_target_pairs={{0,1},{1,0},{2,3},{3,2},{4,5},{5,4},{6,7},{7,6},{8,9},{9,8},{10,11... | collective-permute-start | bytes 442376 | tf_op jit(solution)/shard_map/ppermute | solution.py:232
  114.7 13.4 %collective-permute-start.17 = (bf16[144,512]{1,0:T(8,128)(2,1)S(1)}, bf16[144,512]{1,0:T(8,128)(2,1)S(1)}, u32[]{:S(2)}, u32[]{:S(2)}) collective-permute-start(bf16[144,512]{1,0:T(8,128)(2,1)S(1)} %slice.44), channel_id=1, source_target_pairs={{0,2},{1,3},{2,0},{3,1},{4,6},{5,7},{6,4},{7,5},{8,10},{9,11},{10,... | collective-permute-start | bytes 442376 | tf_op jit(solution)/shard_map/ppermute | solution.py:232
  121.9 11.5 %collective-permute-start.21 = (bf16[144,512]{1,0:T(8,128)(2,1)S(1)}, bf16[144,512]{1,0:T(8,128)(2,1)S(1)}, u32[]{:S(2)}, u32[]{:S(2)}) collective-permute-start(bf16[144,512]{1,0:T(8,128)(2,1)S(1)} %slice.39), channel_id=1, source_target_pairs={{0,1},{1,0},{2,3},{3,2},{4,5},{5,4},{6,7},{7,6},{8,9},{9,8},{10,11... | collective-permute-start | bytes 442376 | tf_op jit(solution)/shard_map/ppermute | solution.py:232
  124.0 10.9 %collective-permute-start.22 = (bf16[144,512]{1,0:T(8,128)(2,1)S(1)}, bf16[144,512]{1,0:T(8,128)(2,1)S(1)}, u32[]{:S(2)}, u32[]{:S(2)}) collective-permute-start(bf16[144,512]{1,0:T(8,128)(2,1)S(1)} %slice.45), channel_id=1, source_target_pairs={{0,2},{1,3},{2,0},{3,1},{4,6},{5,7},{6,4},{7,5},{8,10},{9,11},{10,... | collective-permute-start | bytes 442376 | tf_op jit(solution)/shard_map/ppermute | solution.py:232
  127.9 10.5 %collective-permute-start.11 = (bf16[4,1,128,128]{3,2,1,0:T(8,128)(2,1)S(1)}, bf16[4,1,128,128]{3,2,1,0:T(8,128)(2,1)S(1)}, u32[]{:S(2)}, u32[]{:S(2)}) collective-permute-start(bf16[4,1,128,128]{3,2,1,0:T(8,128)(2,1)S(1)} %get-tuple-element.49), channel_id=1, source_target_pairs={{0,1},{1,0},{2,3},{3,2},{4,5},{5,4},{6,7},{7,6},{8,9},{9,8},{10,11... | collective-permute-start | bytes 393224 | tf_op jit(solution)/shard_map/ppermute | solution.py:232
  128.0 10.4 %collective-permute-start.12 = (bf16[4,1,128,128]{3,2,1,0:T(8,128)(2,1)S(1)}, bf16[4,1,128,128]{3,2,1,0:T(8,128)(2,1)S(1)}, u32[]{:S(2)}, u32[]{:S(2)}) collective-permute-start(bf16[4,1,128,128]{3,2,1,0:T(8,128)(2,1)S(1)} %get-tuple-element.48), channel_id=1, source_target_pairs={{0,2},{1,3},{2,0},{3,1},{4,6},{5,7},{6,4},{7,5},{8,10},{9,11},{10,... | collective-permute-start | bytes 393224 | tf_op jit(solution)/shard_map/ppermute | solution.py:232
  128.1 10.3 %collective-permute-start.13 = (bf16[4,1,128,128]{3,2,1,0:T(8,128)(2,1)S(1)}, bf16[4,1,128,128]{3,2,1,0:T(8,128)(2,1)S(1)}, u32[]{:S(2)}, u32[]{:S(2)}) collective-permute-start(bf16[4,1,128,128]{3,2,1,0:T(8,128)(2,1)S(1)} %get-tuple-element.47), channel_id=1, source_target_pairs={{0,3},{1,2},{2,1},{3,0},{4,7},{5,6},{6,5},{7,4},{8,11},{9,10},{10,... | collective-permute-start | bytes 393224 | tf_op jit(solution)/shard_map/ppermute | solution.py:232
  138.3 2.7 %collective-permute-start.23 = (f32[512,512]{1,0:T(8,128)S(1)}, f32[512,512]{1,0:T(8,128)S(1)}, u32[]{:S(2)}, u32[]{:S(2)}) collective-permute-start(f32[512,512]{1,0:T(8,128)S(1)} %get-tuple-element.36), channel_id=1, source_target_pairs={{0,16},{16,0},{1,17},{17,1},{2,18},{18,2},{3,19},{19,3},{4,20},{20... | collective-permute-start | bytes 3145736 | tf_op jit(solution)/shard_map/ppermute | solution.py:240
  144.7 0.8 copy-start
  145.5 19.2 %all-to-all-start.3 = ((bf16[16,128,128]{2,1,0:T(8,128)(2,1)}), bf16[16,128,128]{2,1,0:T(8,128)(2,1)S(1)}, u32[]{:S(2)}, u32[]{:S(2)}) async-start(bf16[16,128,128]{2,1,0:T(8,128)(2,1)} %bitcast.53), calls=%async_computation.3 | async-start | bytes 1048576 | tf_op jit(solution)/shard_map/all_to_all | solution.py:192

commit v6 on v5

--- a/solution.py
+++ b/solution.py
@@ -75,34 +75,36 @@
     tokens = n * rows
     per = max(1, min(n, 256 // rows))
     factor = LOG2E / HEAD**0.5
-    if place is None:
-        step, place = 2 * per, jnp.zeros(1, jnp.int32)
-        shape = (n // step, step, rows)
-        out_block = pl.BlockSpec((1, step, rows, HEAD), lambda h, i, _: (i, 0, 0, h))
-    else:
-        step, place = n // QUAD, place.reshape(1)
-        shape = (step, QUAD, rows)
-        out_block = pl.BlockSpec((step, 1, rows, HEAD), lambda h, i, p: (0, i ^ p[0], 0, h))
-
-    def body(_, q_ref, k_ref, v_ref, out_ref, values):
+    turned = place is not None
+    step = n if turned else min(n, 16)
+    shape = (n // QUAD, QUAD) if turned else (n,)
+
+    def body(place_ref, q_ref, k_ref, v_ref, out_ref, values):
         @pl.when(pl.program_id(1) == 0)
         def _():
             values[:, :HEAD] = v_ref[:, 0].reshape(tokens, HEAD)
             values[:, HEAD:] = jnp.ones((tokens, HEAD), jnp.bfloat16)
 
         keys = k_ref[:, 0].reshape(tokens, HEAD)
-        outs = []
-        for part in range(step // per):
-            q = q_ref[part * per : (part + 1) * per, 0].reshape(per * rows, HEAD)
+        for at in range(0, step, per):
+            q = q_ref[at : at + per, 0].reshape(per * rows, HEAD)
             scores = lax.dot_general(
                 q, keys, (((1,), (1,)), ((), ())), preferred_element_type=jnp.float32
             )
             top = jnp.max(scores, axis=1, keepdims=True)
             probs = jnp.exp2((scores - top) * factor).astype(jnp.bfloat16)
             total = jnp.dot(probs, values[...], preferred_element_type=jnp.float32)
-            outs.append((total[:, :HEAD] / total[:, HEAD:]).astype(jnp.bfloat16))
-        out_ref[...] = jnp.concatenate(outs).reshape(out_ref.shape)
-
+            out = (total[:, :HEAD] / total[:, HEAD:]).astype(jnp.bfloat16).reshape(per, rows, HEAD)
+            if turned:
+                r, z = divmod(at, n // QUAD)
+                out_ref[z : z + per, r ^ place_ref[0]] = out
+            else:
+                out_ref[at : at + per] = out
+
+    if turned:
+        out_block = pl.BlockSpec((*shape, rows, HEAD), lambda h, i, _: (0, 0, 0, h))
+    else:
+        out_block = pl.BlockSpec((step, rows, HEAD), lambda h, i, _: (i, 0, h))
     return pl.pallas_call(
         body,
         grid_spec=pltpu.PrefetchScalarGridSpec(
@@ -116,7 +118,7 @@
             out_specs=out_block,
             scratch_shapes=[pltpu.VMEM((tokens, 2 * HEAD), jnp.bfloat16)],
         ),
-        out_shape=jax.ShapeDtypeStruct((*shape, width), jnp.bfloat16),
+        out_shape=jax.ShapeDtypeStruct((*shape, rows, width), jnp.bfloat16),
         compiler_params=params(),
         cost_estimate=pl.CostEstimate(
             flops=16 * heads * tokens * tokens * HEAD,
@@ -124,7 +126,9 @@
             transcendentals=heads * tokens * tokens,
         ),
         name="self_attention",
-    )(place, blocks, blocks, blocks).reshape(n, rows, width)
+    )(
+        place.reshape(1) if turned else jnp.zeros(1, jnp.int32), blocks, blocks, blocks
+    ).reshape(n, rows, width)
 
 
 def cross_attention(blocks, item, text, head, length, self_out, place=None):
@@ -132,51 +136,46 @@
     heads = width // HEAD
     positions = text.shape[0]
     values_at = text.shape[1] // HEAD // 2 + head
-    step = max(1, min(n, 512 // rows))
     factor = LOG2E / HEAD**0.5
-    if place is None:
-        place = jnp.zeros(1, jnp.int32)
-        shape = (n // step, step, rows)
-        out_block = pl.BlockSpec((1, step, rows, HEAD), lambda h, i, *_: (i, 0, 0, h))
-    else:
-        step, place = n // QUAD, place.reshape(1)
-        shape = (step, QUAD, rows)
-        out_block = pl.BlockSpec((step, 1, rows, HEAD), lambda h, i, _, p: (0, i ^ p[0], 0, h))
-
-    def body(length_ref, _, q_ref, k_ref, v_ref, self_ref, out_ref, values):
-        @pl.when(pl.program_id(1) == 0)
-        def _():
-            values[:, :HEAD] = v_ref[...]
-            values[:, HEAD:] = jnp.ones((positions, HEAD), jnp.bfloat16)
-
-        q = q_ref[:, 0].reshape(step * rows, HEAD)
-        scores = lax.dot_general(
-            q, k_ref[...], (((1,), (1,)), ((), ())), preferred_element_type=jnp.float32
-        )
-        place = lax.broadcasted_iota(jnp.int32, (1, positions), 1)
-        scores = jnp.where(place < length_ref[0], scores, -1e30)
-        top = jnp.max(scores, axis=1, keepdims=True)
-        probs = jnp.exp2((scores - top) * factor).astype(jnp.bfloat16)
-        total = jnp.dot(probs, values[...], preferred_element_type=jnp.float32)
-        out = (total[:, :HEAD] / total[:, HEAD:]).astype(jnp.bfloat16).astype(jnp.float32)
-        out = out.reshape(self_ref.shape) + self_ref[...].astype(jnp.float32)
-        out_ref[...] = out.astype(jnp.bfloat16)
-
+    turned = place is not None
+    shape = (n // QUAD, QUAD) if turned else (n,)
+
+    def body(length_ref, place_ref, q_ref, k_ref, v_ref, self_ref, out_ref, values):
+        values[:, :HEAD] = v_ref[...]
+        values[:, HEAD:] = jnp.ones((positions, HEAD), jnp.bfloat16)
+        valid = lax.broadcasted_iota(jnp.int32, (1, positions), 1) < length_ref[0]
+        for at in range(n):
+            scores = lax.dot_general(
+                q_ref[at, 0],
+                k_ref[...],
+                (((1,), (1,)), ((), ())),
+                preferred_element_type=jnp.float32,
+            )
+            scores = jnp.where(valid, scores, -1e30)
+            top = jnp.max(scores, axis=1, keepdims=True)
+            probs = jnp.exp2((scores - top) * factor).astype(jnp.bfloat16)
+            total = jnp.dot(probs, values[...], preferred_element_type=jnp.float32)
+            out = (total[:, :HEAD] / total[:, HEAD:]).astype(jnp.bfloat16).astype(jnp.float32)
+            r, z = divmod(at, n // QUAD)
+            block = (z, r ^ place_ref[0]) if turned else at
+            out_ref[block] = (out + self_ref[block].astype(jnp.float32)).astype(jnp.bfloat16)
+
+    whole = pl.BlockSpec((*shape, rows, HEAD), lambda h, *_: (0,) * len(shape) + (0, h))
     return pl.pallas_call(
         body,
         grid_spec=pltpu.PrefetchScalarGridSpec(
             num_scalar_prefetch=2,
-            grid=(heads, n // step),
+            grid=(heads,),
             in_specs=[
-                pl.BlockSpec((step, 1, rows, HEAD), lambda h, i, *_: (i, item, 0, h)),
-                pl.BlockSpec((positions, HEAD), lambda h, i, *_: (0, head + h)),
-                pl.BlockSpec((positions, HEAD), lambda h, i, *_: (0, values_at + h)),
-                out_block,
+                pl.BlockSpec((n, 1, rows, HEAD), lambda h, *_: (0, item, 0, h)),
+                pl.BlockSpec((positions, HEAD), lambda h, *_: (0, head + h)),
+                pl.BlockSpec((positions, HEAD), lambda h, *_: (0, values_at + h)),
+                whole,
             ],
-            out_specs=out_block,
+            out_specs=whole,
             scratch_shapes=[pltpu.VMEM((positions, 2 * HEAD), jnp.bfloat16)],
         ),
-        out_shape=jax.ShapeDtypeStruct((*shape, width), jnp.bfloat16),
+        out_shape=jax.ShapeDtypeStruct((*shape, rows, width), jnp.bfloat16),
         compiler_params=params(),
         cost_estimate=pl.CostEstimate(
             flops=32 * heads * n * rows * positions * HEAD,
@@ -184,7 +183,14 @@
             transcendentals=heads * n * rows * positions,
         ),
         name="cross_attention",
-    )(length, place, blocks, text, text, self_out.reshape(*shape, width)).reshape(n, rows, width)
+    )(
+        length,
+        place.reshape(1) if turned else jnp.zeros(1, jnp.int32),
+        blocks,
+        text,
+        text,
+        self_out.reshape(*shape, rows, width),
+    ).reshape(n, rows, width)
 
 
 def spread(blocks, groups=None):

time: 185 us -> 184 us (level)
  Pallas kernels: 43.3 us -> 34.5 us
  waiting for transfers between devices: 61.8 us -> 68.8 us
    pallas_call x2, Pallas kernels: 16.6 us -> 11.4 us  [self_attention(): pl.pallas_call(body, grid_spec=pltpu.PrefetchScalarGridSpec(num_scalar_pr...]
    all_to_all x4, waiting for transfers between devices: 15.6 us -> 20.1 us  [spread(): lax.all_to_all(flat, 'seq', split_axis=0, concat_axis=0, tiled=True, axis...]
    pallas_call x2, Pallas kernels: 6.82 us -> 3.1 us  [cross_attention(): pl.pallas_call(body, grid_spec=pltpu.PrefetchScalarGridSpec(num_scalar_pr...]
    ppermute x21, waiting for transfers between devices: 42.9 us -> 45.3 us  [exchange(): return lax.ppermute(value, 'seq', [(i, i ^ apart) for i in range(n)])]
  transfers between devices with their start and end apart: 28 -> 28, of which waited for: 17 -> 16; matrix products, arithmetic and copies ran while one was open for 4% -> 4% of each run, Pallas kernels for 23% -> 18%
where the time goes in v6:
time: 184 us; the launch traced here: 183 us
  waiting for transfers between devices  68.8 us (37%)
  starting transfers between devices  47.6 us (26%)
  Pallas kernels  34.5 us (19%)
  blocking collectives  18.1 us (10%)
  local copies, waits for them, and re-layouts  7.75 us (4%)
  between operations  3.55 us (2%)
  other arithmetic  2.4 us (1%)
    ppermute x21, waiting for transfers between devices, exchange(): return lax.ppermute(value, 'seq', [(i, i ^ apart) for i in range(n)])  45.3 us
    ppermute x21, starting transfers between devices, exchange(): return lax.ppermute(value, 'seq', [(i, i ^ apart) for i in range(n)])  26.7 us
    all_to_all x4, starting transfers between devices, spread(): lax.all_to_all(flat, 'seq', split_axis=0, concat_axis=0, tiled=True, axis...  20.2 us
    all_to_all x4, waiting for transfers between devices, spread(): lax.all_to_all(flat, 'seq', split_axis=0, concat_axis=0, tiled=True, axis...  20.1 us
    all_to_all x1, blocking collectives, spread(): lax.all_to_all(flat, 'seq', split_axis=0, concat_axis=0, tiled=True, axis...  18.1 us
    pallas_call x3, Pallas kernels, pack(): pl.pallas_call(body, grid=(n // per,), in_specs=[pl.BlockSpec((rows, per...  11.5 us
    pallas_call x2, Pallas kernels, self_attention(): pl.pallas_call(body, grid_spec=pltpu.PrefetchScalarGridSpec(num_scalar_pr...  11.4 us
  transfers between devices with their start and end apart: 28, of which 16 were waited for; matrix products, arithmetic and copies ran while one was open for 4% of the time, Pallas kernels for 18%

profile of v6, /device:TPU:0, one launch (start us, length us, event | category | flops | bytes accessed | tf_op | source)
XLA Modules:
  0.0 182.8 jit_solution(6595977794426403099)
XLA Ops:
  0.0 0.5 collective-permute-start.1
  0.5 4.3 %pack.3 = bf16[16,4,128,128]{3,2,1,0:T(8,128)(2,1)} custom-call(bf16[128,4096]{1,0:T(8,128)(2,1)} %bitcast.64, bf16[128,4096]{1,0:T(8,128)(2,1)} %bitcast.66, bf16[128,4096]{1,0:T(8,128)(2,1)} %bitcast.68, bf16[128,4096]{1,0:T(8,128)(2,1)} %bitcast.62), custom_call_target="tpu_custom_call" | custom-call | bytes 4194304 | tf_op jit(solution)/shard_map/pack/pallas_call | solution.py:36
  4.7 5.9 %all-to-all-start = ((bf16[16,512,128]{2,1,0:T(8,128)(2,1)}), bf16[16,512,128]{2,1,0:T(8,128)(2,1)}, u32[]{:S(2)}, u32[]{:S(2)}) async-start(bf16[16,512,128]{2,1,0:T(8,128)(2,1)} %bitcast.57), calls=%async_computation | async-start | bytes 4194304 | tf_op jit(solution)/shard_map/all_to_all | solution.py:198
  12.0 0.2 collective-permute-start
  12.2 0.9 collective-permute-done
  13.1 0.6 fusion.1
  14.4 3.0 %quarters.1 = (bf16[2,144,1024]{2,1,0:T(8,128)(2,1)S(1)}, bf16[2,144,1024]{2,1,0:T(8,128)(2,1)S(1)}, bf16[2,144,1024]{2,1,0:T(8,128)(2,1)S(1)}, bf16[2,144,1024]{2,1,0:T(8,128)(2,1)S(1)}) custom-call(s32[3]{0:T(128)S(1)} %pad_add_fusion.1.where_ref, bf16[512,4096]{1,0:T(8,128)(2,1)} %bitcast.61, bf16[512,4096]{1,0:T(8,128)(2,1)} %collective-permute-done.1.other_ref), custom_call_target="tpu_custom_call" | custom-call | bytes 4194304 | tf_op jit(solution)/shard_map/quarters/pallas_call | solution.py:280
  17.4 1.6 collective-permute-start.4
  20.3 1.6 collective-permute-start.2
  21.9 11.0 %collective-permute-done.4 = bf16[2,144,1024]{2,1,0:T(8,128)(2,1)S(1)} collective-permute-done((bf16[2,144,1024]{2,1,0:T(8,128)(2,1)S(1)}, bf16[2,144,1024]{2,1,0:T(8,128)(2,1)S(1)}, u32[]{:S(2)}, u32[]{:S(2)}) %collective-permute-start.4) | collective-permute-done | bytes 589856 | tf_op jit(solution)/shard_map/ppermute | solution.py:238
  32.9 0.1 broadcast_select_fusion
  33.0 1.6 collective-permute-start.5
  34.6 1.2 collective-permute-done.2
  35.7 0.1 broadcast_select_fusion.1
  35.9 0.4 collective-permute-start.3
  36.3 5.4 %collective-permute-done.5 = bf16[144,1024]{1,0:T(8,128)(2,1)S(1)} collective-permute-done((bf16[144,1024]{1,0:T(8,128)(2,1)S(1)}, bf16[144,1024]{1,0:T(8,128)(2,1)S(1)}, u32[]{:S(2)}, u32[]{:S(2)}) %collective-permute-start.5) | collective-permute-done | bytes 294944 | tf_op jit(solution)/shard_map/ppermute | solution.py:238
  41.9 1.8 %collective-permute-done.3 = bf16[144,1024]{1,0:T(8,128)(2,1)S(1)} collective-permute-done((bf16[144,1024]{1,0:T(8,128)(2,1)S(1)}, bf16[144,1024]{1,0:T(8,128)(2,1)S(1)}, u32[]{:S(2)}, u32[]{:S(2)}) %collective-permute-start.3) | collective-permute-done | bytes 294944 | tf_op jit(solution)/shard_map/ppermute | solution.py:238
  43.9 2.1 %collective-permute-start.6 = (bf16[144,2048]{1,0:T(8,128)(2,1)S(1)}, bf16[144,2048]{1,0:T(8,128)(2,1)}, u32[]{:S(2)}, u32[]{:S(2)}) collective-permute-start(bf16[144,2048]{1,0:T(8,128)(2,1)S(1)} %pad_maximum_fusion), channel_id=1, source_target_pairs={{0,4},{1,5},{2,6},{3,7},{4,0},{5,1},{6,2},{7,3},{8,12},{9,13},{10,... | collective-permute-start | bytes 1769480 | tf_op jit(solution)/shard_map/ppermute | solution.py:238
  45.9 3.3 %pack.4 = bf16[16,1,128,128]{3,2,1,0:T(8,128)(2,1)} custom-call(bf16[128,4096]{1,0:T(8,128)(2,1)} %bitcast.63), custom_call_target="tpu_custom_call" | custom-call | bytes 4194304 | tf_op jit(solution)/shard_map/pack/pallas_call | solution.py:36
  49.2 3.9 %pack.5 = bf16[16,3,128,128]{3,2,1,0:T(8,128)(2,1)} custom-call(bf16[128,4096]{1,0:T(8,128)(2,1)} %bitcast.65, bf16[128,4096]{1,0:T(8,128)(2,1)} %bitcast.67, bf16[128,4096]{1,0:T(8,128)(2,1)} %bitcast.69), custom_call_target="tpu_custom_call" | custom-call | bytes 4194304 | tf_op jit(solution)/shard_map/pack/pallas_call | solution.py:36
  53.1 6.6 %all-to-all-done = bf16[16,512,128]{2,1,0:T(8,128)(2,1)} async-done(((bf16[16,512,128]{2,1,0:T(8,128)(2,1)}), bf16[16,512,128]{2,1,0:T(8,128)(2,1)}, u32[]{:S(2)}, u32[]{:S(2)}) %all-to-all-start) | async-done | bytes 2097184 | tf_op jit(solution)/shard_map/all_to_all | solution.py:198
  59.7 4.7 %all-to-all-start.1 = ((bf16[16,128,128]{2,1,0:T(8,128)(2,1)}), bf16[16,128,128]{2,1,0:T(8,128)(2,1)S(1)}, u32[]{:S(2)}, u32[]{:S(2)}) async-start(bf16[16,128,128]{2,1,0:T(8,128)(2,1)} %bitcast.15), calls=%async_computation.1 | async-start | bytes 1048576 | tf_op jit(solution)/shard_map/all_to_all | solution.py:198
  64.4 1.5 slice.35
  66.0 1.1 dynamic-slice_bitcast_fusion
  67.0 1.9 %collective-permute-start.8 = (bf16[4,3,128,128]{3,2,1,0:T(8,128)(2,1)}, bf16[4,3,128,128]{3,2,1,0:T(8,128)(2,1)S(1)}, u32[]{:S(2)}, u32[]{:S(2)}) collective-permute-start(bf16[4,3,128,128]{3,2,1,0:T(8,128)(2,1)} %get-tuple-element.45), channel_id=1, source_target_pairs={{0,1},{1,0},{2,3},{3,2},{4,5},{5,4},{6,7},{7,6},{8,9},{9,8},{10,11... | collective-permute-start | bytes 1179656 | tf_op jit(solution)/shard_map/ppermute | solution.py:238
  69.0 1.5 collective-permute-start.9
  70.4 0.1 collective-permute-start.10
  70.5 1.7 collective-permute-done.6
  72.2 1.3 broadcast_select_fusion.2
  73.5 5.6 %all-to-all-done.1 = bf16[16,128,128]{2,1,0:T(8,128)(2,1)S(1)} async-done(((bf16[16,128,128]{2,1,0:T(8,128)(2,1)}), bf16[16,128,128]{2,1,0:T(8,128)(2,1)S(1)}, u32[]{:S(2)}, u32[]{:S(2)}) %all-to-all-start.1) | async-done | bytes 524320 | tf_op jit(solution)/shard_map/all_to_all | solution.py:198
  79.2 0.7 collective-permute-start.7
  79.9 3.3 %collective-permute-done.8.refs_1_ = bf16[4,3,128,128]{3,2,1,0:T(8,128)(2,1)S(1)} collective-permute-done((bf16[4,3,128,128]{3,2,1,0:T(8,128)(2,1)}, bf16[4,3,128,128]{3,2,1,0:T(8,128)(2,1)S(1)}, u32[]{:S(2)}, u32[]{:S(2)}) %collective-permute-start.8) | collective-permute-done | bytes 393248 | tf_op jit(solution)/shard_map/ppermute | solution.py:238
  83.2 6.2 %collective-permute-done.9.refs_2_ = bf16[4,3,128,128]{3,2,1,0:T(8,128)(2,1)S(1)} collective-permute-done((bf16[4,3,128,128]{3,2,1,0:T(8,128)(2,1)}, bf16[4,3,128,128]{3,2,1,0:T(8,128)(2,1)S(1)}, u32[]{:S(2)}, u32[]{:S(2)}) %collective-permute-start.9) | collective-permute-done | bytes 393248 | tf_op jit(solution)/shard_map/ppermute | solution.py:238
  89.4 1.6 collective-permute-done.10.refs_3_
  91.1 0.3 join.2
  91.3 1.1 copy-done.2
  92.7 1.0 collective-permute-start.18
  93.7 1.2 collective-permute-start.14
  94.9 0.6 collective-permute-start.15
  95.4 5.3 %all-to-all-start.2 = ((bf16[16,384,128]{2,1,0:T(8,128)(2,1)}), bf16[16,384,128]{2,1,0:T(8,128)(2,1)S(1)}, u32[]{:S(2)}, u32[]{:S(2)}) async-start(bf16[16,384,128]{2,1,0:T(8,128)(2,1)} %bitcast.58), calls=%async_computation.2 | async-start | bytes 3145728 | tf_op jit(solution)/shard_map/all_to_all | solution.py:198
  100.8 2.0 %collective-permute-start.19 = (bf16[144,1024]{1,0:T(8,128)(2,1)S(1)}, bf16[144,1024]{1,0:T(8,128)(2,1)S(1)}, u32[]{:S(2)}, u32[]{:S(2)}) collective-permute-start(bf16[144,1024]{1,0:T(8,128)(2,1)S(1)} %collective-permute-done.18.refs_5_), channel_id=1, source_target_pairs={{0,1},{1,0},{2,3},{3,2},{4,5},{5,4},{6,7},{7,6},{8,9},{9,8},{10,11... | collective-permute-start | bytes 884744 | tf_op jit(solution)/shard_map/ppermute | solution.py:238
  102.8 1.5 collective-permute-start.20
  104.2 1.4 copy-done.3
  105.7 5.7 %self_attention.2 = bf16[4,4,128,128]{3,2,1,0:T(8,128)(2,1)S(1)} custom-call(s32[1]{0:T(128)} %bitcast.3.place_ref, bf16[16,3,128,128]{3,2,1,0:T(8,128)(2,1)S(1)} %bitcast.53, bf16[16,3,128,128]{3,2,1,0:T(8,128)(2,1)S(1)} %bitcast.54, bf16[16,3,128,128]{3,2,1,0:T(8,128)(2,1)S(1)} %bitcast.55), custom_call_target="tpu_custom_call" | custom-call | flops 8589934592 | bytes 2097152 | tf_op jit(solution)/shard_map/self_attention/pallas_call | solution.py:108
  111.4 0.6 collective-permute-start.16
  112.0 0.2 collective-permute-start.17
  112.2 9.7 %collective-permute-done.20.refs_7_ = bf16[144,1024]{1,0:T(8,128)(2,1)S(1)} collective-permute-done((bf16[144,1024]{1,0:T(8,128)(2,1)S(1)}, bf16[144,1024]{1,0:T(8,128)(2,1)S(1)}, u32[]{:S(2)}, u32[]{:S(2)}) %collective-permute-start.20) | collective-permute-done | bytes 294944 | tf_op jit(solution)/shard_map/ppermute | solution.py:238
  121.9 2.1 %collective-permute-start.21 = (bf16[144,512]{1,0:T(8,128)(2,1)S(1)}, bf16[144,512]{1,0:T(8,128)(2,1)S(1)}, u32[]{:S(2)}, u32[]{:S(2)}) collective-permute-start(bf16[144,512]{1,0:T(8,128)(2,1)S(1)} %slice.39), channel_id=1, source_target_pairs={{0,1},{1,0},{2,3},{3,2},{4,5},{5,4},{6,7},{7,6},{8,9},{9,8},{10,11... | collective-permute-start | bytes 442376 | tf_op jit(solution)/shard_map/ppermute | solution.py:238
  124.0 2.7 %collective-permute-start.22 = (bf16[144,512]{1,0:T(8,128)(2,1)S(1)}, bf16[144,512]{1,0:T(8,128)(2,1)S(1)}, u32[]{:S(2)}, u32[]{:S(2)}) collective-permute-start(bf16[144,512]{1,0:T(8,128)(2,1)S(1)} %slice.45), channel_id=1, source_target_pairs={{0,2},{1,3},{2,0},{3,1},{4,6},{5,7},{6,4},{7,5},{8,10},{9,11},{10,... | collective-permute-start | bytes 442376 | tf_op jit(solution)/shard_map/ppermute | solution.py:238
  126.7 1.1 slice.36
  128.1 3.4 %collective-permute-start.13 = (bf16[4,1,128,128]{3,2,1,0:T(8,128)(2,1)S(1)}, bf16[4,1,128,128]{3,2,1,0:T(8,128)(2,1)S(1)}, u32[]{:S(2)}, u32[]{:S(2)}) collective-permute-start(bf16[4,1,128,128]{3,2,1,0:T(8,128)(2,1)S(1)} %get-tuple-element.47), channel_id=1, source_target_pairs={{0,3},{1,2},{2,1},{3,0},{4,7},{5,6},{6,5},{7,4},{8,11},{9,10},{10,... | collective-permute-start | bytes 393224 | tf_op jit(solution)/shard_map/ppermute | solution.py:238
  131.4 3.3 %collective-permute-done.22.refs_9_ = bf16[144,512]{1,0:T(8,128)(2,1)S(1)} collective-permute-done((bf16[144,512]{1,0:T(8,128)(2,1)S(1)}, bf16[144,512]{1,0:T(8,128)(2,1)S(1)}, u32[]{:S(2)}, u32[]{:S(2)}) %collective-permute-start.22) | collective-permute-done | bytes 147488 | tf_op jit(solution)/shard_map/ppermute | solution.py:238
  134.7 3.5 %project.1 = (f32[512,512]{1,0:T(8,128)S(1)}, f32[512,512]{1,0:T(8,128)S(1)}) custom-call(s32[3]{0:T(128)S(1)} %pad_add_fusion.2.where_ref, bf16[144,1024]{1,0:T(8,128)(2,1)S(1)} %broadcast_select_fusion.3.refs_0_, bf16[144,1024]{1,0:T(8,128)(2,1)S(1)} %collective-permute-done.14.refs_1_, bf16[144,1024]{1,0:T(8,128)(2,1)S(1)} %collective-permute-done.15.refs_2_, ...), custom_call_target="tpu_custom_call" | custom-call | flops 7000000000 | bytes 8388608 | tf_op jit(solution)/shard_map/project/pallas_call | solution.py:337
  138.4 0.2 join.3
  138.5 2.5 %collective-permute-done.23 = f32[512,512]{1,0:T(8,128)S(1)} collective-permute-done((f32[512,512]{1,0:T(8,128)S(1)}, f32[512,512]{1,0:T(8,128)S(1)}, u32[]{:S(2)}, u32[]{:S(2)}) %collective-permute-start.23) | collective-permute-done | bytes 1048608 | tf_op jit(solution)/shard_map/ppermute | solution.py:246
  141.0 0.3 add_convert_fusion.k_ref.v_ref
  141.2 1.6 cross_attention.2
  142.8 0.8 copy-done
  143.6 4.2 %all-to-all-start.3 = ((bf16[16,128,128]{2,1,0:T(8,128)(2,1)}), bf16[16,128,128]{2,1,0:T(8,128)(2,1)S(1)}, u32[]{:S(2)}, u32[]{:S(2)}) async-start(bf16[16,128,128]{2,1,0:T(8,128)(2,1)} %bitcast.52), calls=%async_computation.3 | async-start | bytes 1048576 | tf_op jit(solution)/shard_map/all_to_all | solution.py:198
  147.9 5.7 %self_attention.3.self_ref = bf16[16,128,128]{2,1,0:T(8,128)(2,1)S(1)} custom-call(s32[1]{0:T(128)} %constant.57.clone.1.place_ref, bf16[16,3,128,128]{3,2,1,0:T(8,128)(2,1)S(1)} %bitcast.48, bf16[16,3,128,128]{3,2,1,0:T(8,128)(2,1)S(1)} %bitcast.49, bf16[16,3,128,128]{3,2,1,0:T(8,128)(2,1)S(1)} %bitcast.50), custom_call_target="tpu_custom_call" | custom-call | flops 8589934592 | bytes 2097152 | tf_op jit(solution)/shard_map/self_attention/pallas_call | solution.py:108
  153.6 1.5 cross_attention.3
  155.1 7.9 %all-to-all-done.3.refs_0_ = bf16[16,128,128]{2,1,0:T(8,128)(2,1)S(1)} async-done(((bf16[16,128,128]{2,1,0:T(8,128)(2,1)}), bf16[16,128,128]{2,1,0:T(8,128)(2,1)S(1)}, u32[]{:S(2)}, u32[]{:S(2)}) %all-to-all-start.3) | async-done | bytes 524320 | tf_op jit(solution)/shard_map/all_to_all | solution.py:198
  163.0 18.1 %all_to_all.25.refs_1_ = bf16[16,128,128]{2,1,0:T(8,128)(2,1)S(1)} all-to-all(bf16[16,128,128]{2,1,0:T(8,128)(2,1)S(1)} %cross_attention.3), channel_id=1, replica_groups=mesh['dp'=2,'seq'=16] {'seq'}, dimensions={0} | all-to-all | bytes 1048576 | tf_op jit(solution)/shard_map/all_to_all | solution.py:198
  181.1 1.6 unpack.1
  (40 shorter events, 1.1 us)
Async XLA Ops:
  0.0 14.4 %collective-permute-start.1 = (bf16[512,4096]{1,0:T(8,128)(2,1)}, bf16[512,4096]{1,0:T(8,128)(2,1)}, u32[]{:S(2)}, u32[]{:S(2)}) collective-permute-start(bf16[512,4096]{1,0:T(8,128)(2,1)} %bitcast.60), channel_id=1, source_target_pairs={{0,16},{16,0},{1,17},{17,1},{2,18},{18,2},{3,19},{19,3},{4,20},{20... | collective-permute-start | bytes 12582920 | tf_op jit(solution)/shard_map/ppermute | solution.py:246
  4.7 55.0 %all-to-all-start = ((bf16[16,512,128]{2,1,0:T(8,128)(2,1)}), bf16[16,512,128]{2,1,0:T(8,128)(2,1)}, u32[]{:S(2)}, u32[]{:S(2)}) async-start(bf16[16,512,128]{2,1,0:T(8,128)(2,1)} %bitcast.57), calls=%async_computation | async-start | bytes 4194304 | tf_op jit(solution)/shard_map/all_to_all | solution.py:198
  12.0 1.1 collective-permute-start
  17.4 15.4 %collective-permute-start.4 = (bf16[2,144,1024]{2,1,0:T(8,128)(2,1)S(1)}, bf16[2,144,1024]{2,1,0:T(8,128)(2,1)S(1)}, u32[]{:S(2)}, u32[]{:S(2)}) collective-permute-start(bf16[2,144,1024]{2,1,0:T(8,128)(2,1)S(1)} %get-tuple-element.27), channel_id=1, source_target_pairs={{0,2},{1,3},{2,0},{3,1},{4,6},{5,7},{6,4},{7,5},{8,10},{9,11},{10,... | collective-permute-start | bytes 1769480 | tf_op jit(solution)/shard_map/ppermute | solution.py:238
  20.3 15.5 %collective-permute-start.2 = (bf16[2,144,1024]{2,1,0:T(8,128)(2,1)S(1)}, bf16[2,144,1024]{2,1,0:T(8,128)(2,1)S(1)}, u32[]{:S(2)}, u32[]{:S(2)}) collective-permute-start(bf16[2,144,1024]{2,1,0:T(8,128)(2,1)S(1)} %get-tuple-element.25), channel_id=1, source_target_pairs={{0,1},{1,0},{2,3},{3,2},{4,5},{5,4},{6,7},{7,6},{8,9},{9,8},{10,11... | collective-permute-start | bytes 1769480 | tf_op jit(solution)/shard_map/ppermute | solution.py:238
  33.0 8.8 %collective-permute-start.5 = (bf16[144,1024]{1,0:T(8,128)(2,1)S(1)}, bf16[144,1024]{1,0:T(8,128)(2,1)S(1)}, u32[]{:S(2)}, u32[]{:S(2)}) collective-permute-start(bf16[144,1024]{1,0:T(8,128)(2,1)S(1)} %dynamic-slice_bitcast_fusion.4), channel_id=1, source_target_pairs={{0,1},{1,0},{2,3},{3,2},{4,5},{5,4},{6,7},{7,6},{8,9},{9,8},{10,11... | collective-permute-start | bytes 884744 | tf_op jit(solution)/shard_map/ppermute | solution.py:238
  35.9 7.8 %collective-permute-start.3 = (bf16[144,1024]{1,0:T(8,128)(2,1)S(1)}, bf16[144,1024]{1,0:T(8,128)(2,1)S(1)}, u32[]{:S(2)}, u32[]{:S(2)}) collective-permute-start(bf16[144,1024]{1,0:T(8,128)(2,1)S(1)} %dynamic-slice_bitcast_fusion.5), channel_id=1, source_target_pairs={{0,2},{1,3},{2,0},{3,1},{4,6},{5,7},{6,4},{7,5},{8,10},{9,11},{10,... | collective-permute-start | bytes 884744 | tf_op jit(solution)/shard_map/ppermute | solution.py:238
  43.9 28.4 %collective-permute-start.6 = (bf16[144,2048]{1,0:T(8,128)(2,1)S(1)}, bf16[144,2048]{1,0:T(8,128)(2,1)}, u32[]{:S(2)}, u32[]{:S(2)}) collective-permute-start(bf16[144,2048]{1,0:T(8,128)(2,1)S(1)} %pad_maximum_fusion), channel_id=1, source_target_pairs={{0,4},{1,5},{2,6},{3,7},{4,0},{5,1},{6,2},{7,3},{8,12},{9,13},{10,... | collective-permute-start | bytes 1769480 | tf_op jit(solution)/shard_map/ppermute | solution.py:238
  59.7 19.5 %all-to-all-start.1 = ((bf16[16,128,128]{2,1,0:T(8,128)(2,1)}), bf16[16,128,128]{2,1,0:T(8,128)(2,1)S(1)}, u32[]{:S(2)}, u32[]{:S(2)}) async-start(bf16[16,128,128]{2,1,0:T(8,128)(2,1)} %bitcast.15), calls=%async_computation.1 | async-start | bytes 1048576 | tf_op jit(solution)/shard_map/all_to_all | solution.py:198
  67.0 16.1 %collective-permute-start.8 = (bf16[4,3,128,128]{3,2,1,0:T(8,128)(2,1)}, bf16[4,3,128,128]{3,2,1,0:T(8,128)(2,1)S(1)}, u32[]{:S(2)}, u32[]{:S(2)}) collective-permute-start(bf16[4,3,128,128]{3,2,1,0:T(8,128)(2,1)} %get-tuple-element.45), channel_id=1, source_target_pairs={{0,1},{1,0},{2,3},{3,2},{4,5},{5,4},{6,7},{7,6},{8,9},{9,8},{10,11... | collective-permute-start | bytes 1179656 | tf_op jit(solution)/shard_map/ppermute | solution.py:238
  69.0 20.4 %collective-permute-start.9 = (bf16[4,3,128,128]{3,2,1,0:T(8,128)(2,1)}, bf16[4,3,128,128]{3,2,1,0:T(8,128)(2,1)S(1)}, u32[]{:S(2)}, u32[]{:S(2)}) collective-permute-start(bf16[4,3,128,128]{3,2,1,0:T(8,128)(2,1)} %get-tuple-element.44), channel_id=1, source_target_pairs={{0,2},{1,3},{2,0},{3,1},{4,6},{5,7},{6,4},{7,5},{8,10},{9,11},{10,... | collective-permute-start | bytes 1179656 | tf_op jit(solution)/shard_map/ppermute | solution.py:238
  70.4 20.6 %collective-permute-start.10 = (bf16[4,3,128,128]{3,2,1,0:T(8,128)(2,1)}, bf16[4,3,128,128]{3,2,1,0:T(8,128)(2,1)S(1)}, u32[]{:S(2)}, u32[]{:S(2)}) collective-permute-start(bf16[4,3,128,128]{3,2,1,0:T(8,128)(2,1)} %get-tuple-element.43), channel_id=1, source_target_pairs={{0,3},{1,2},{2,1},{3,0},{4,7},{5,6},{6,5},{7,4},{8,11},{9,10},{10,... | collective-permute-start | bytes 1179656 | tf_op jit(solution)/shard_map/ppermute | solution.py:238
  79.2 13.4 %collective-permute-start.7 = (bf16[144,1024]{1,0:T(8,128)(2,1)S(1)}, bf16[144,1024]{1,0:T(8,128)(2,1)S(1)}, u32[]{:S(2)}, u32[]{:S(2)}) collective-permute-start(bf16[144,1024]{1,0:T(8,128)(2,1)S(1)} %slice_select_fusion), channel_id=1, source_target_pairs={{0,8},{1,9},{2,10},{3,11},{4,12},{5,13},{6,14},{7,15},{8,0},{9,1},... | collective-permute-start | bytes 884744 | tf_op jit(solution)/shard_map/ppermute | solution.py:238
  91.3 1.1 copy-start.2
  92.7 8.1 %collective-permute-start.18 = (bf16[144,1024]{1,0:T(8,128)(2,1)S(1)}, bf16[144,1024]{1,0:T(8,128)(2,1)S(1)}, u32[]{:S(2)}, u32[]{:S(2)}) collective-permute-start(bf16[144,1024]{1,0:T(8,128)(2,1)S(1)} %broadcast_select_fusion.3.refs_0_), channel_id=1, source_target_pairs={{0,4},{1,5},{2,6},{3,7},{4,0},{5,1},{6,2},{7,3},{8,12},{9,13},{10,... | collective-permute-start | bytes 884744 | tf_op jit(solution)/shard_map/ppermute | solution.py:238
  93.7 18.3 %collective-permute-start.14 = (bf16[144,1024]{1,0:T(8,128)(2,1)S(1)}, bf16[144,1024]{1,0:T(8,128)(2,1)S(1)}, u32[]{:S(2)}, u32[]{:S(2)}) collective-permute-start(bf16[144,1024]{1,0:T(8,128)(2,1)S(1)} %broadcast_select_fusion.3.refs_0_), channel_id=1, source_target_pairs={{0,1},{1,0},{2,3},{3,2},{4,5},{5,4},{6,7},{7,6},{8,9},{9,8},{10,11... | collective-permute-start | bytes 884744 | tf_op jit(solution)/shard_map/ppermute | solution.py:238
  94.9 16.5 %collective-permute-start.15 = (bf16[144,1024]{1,0:T(8,128)(2,1)S(1)}, bf16[144,1024]{1,0:T(8,128)(2,1)S(1)}, u32[]{:S(2)}, u32[]{:S(2)}) collective-permute-start(bf16[144,1024]{1,0:T(8,128)(2,1)S(1)} %broadcast_select_fusion.3.refs_0_), channel_id=1, source_target_pairs={{0,2},{1,3},{2,0},{3,1},{4,6},{5,7},{6,4},{7,5},{8,10},{9,11},{10,... | collective-permute-start | bytes 884744 | tf_op jit(solution)/shard_map/ppermute | solution.py:238
  95.4 48.2 %all-to-all-start.2 = ((bf16[16,384,128]{2,1,0:T(8,128)(2,1)}), bf16[16,384,128]{2,1,0:T(8,128)(2,1)S(1)}, u32[]{:S(2)}, u32[]{:S(2)}) async-start(bf16[16,384,128]{2,1,0:T(8,128)(2,1)} %bitcast.58), calls=%async_computation.2 | async-start | bytes 3145728 | tf_op jit(solution)/shard_map/all_to_all | solution.py:198
  100.8 23.2 %collective-permute-start.19 = (bf16[144,1024]{1,0:T(8,128)(2,1)S(1)}, bf16[144,1024]{1,0:T(8,128)(2,1)S(1)}, u32[]{:S(2)}, u32[]{:S(2)}) collective-permute-start(bf16[144,1024]{1,0:T(8,128)(2,1)S(1)} %collective-permute-done.18.refs_5_), channel_id=1, source_target_pairs={{0,1},{1,0},{2,3},{3,2},{4,5},{5,4},{6,7},{7,6},{8,9},{9,8},{10,11... | collective-permute-start | bytes 884744 | tf_op jit(solution)/shard_map/ppermute | solution.py:238
  102.8 19.1 %collective-permute-start.20 = (bf16[144,1024]{1,0:T(8,128)(2,1)S(1)}, bf16[144,1024]{1,0:T(8,128)(2,1)S(1)}, u32[]{:S(2)}, u32[]{:S(2)}) collective-permute-start(bf16[144,1024]{1,0:T(8,128)(2,1)S(1)} %collective-permute-done.18.refs_5_), channel_id=1, source_target_pairs={{0,2},{1,3},{2,0},{3,1},{4,6},{5,7},{6,4},{7,5},{8,10},{9,11},{10,... | collective-permute-start | bytes 884744 | tf_op jit(solution)/shard_map/ppermute | solution.py:238
  104.2 1.4 copy-start.3
  111.3 23.4 %copy-start.1 = (bf16[2048,256]{1,0:T(8,128)(2,1)S(1)}, bf16[2048,256]{1,0:T(8,128)(2,1)}, u32[]{:S(2)}) copy-start(bf16[2048,256]{1,0:T(8,128)(2,1)} %refs_10_.1) | copy-start | bytes 3145732
  111.4 16.6 %collective-permute-start.16 = (bf16[144,512]{1,0:T(8,128)(2,1)S(1)}, bf16[144,512]{1,0:T(8,128)(2,1)S(1)}, u32[]{:S(2)}, u32[]{:S(2)}) collective-permute-start(bf16[144,512]{1,0:T(8,128)(2,1)S(1)} %slice.43), channel_id=1, source_target_pairs={{0,1},{1,0},{2,3},{3,2},{4,5},{5,4},{6,7},{7,6},{8,9},{9,8},{10,11... | collective-permute-start | bytes 442376 | tf_op jit(solution)/shard_map/ppermute | solution.py:238
  112.0 16.0 %collective-permute-start.17 = (bf16[144,512]{1,0:T(8,128)(2,1)S(1)}, bf16[144,512]{1,0:T(8,128)(2,1)S(1)}, u32[]{:S(2)}, u32[]{:S(2)}) collective-permute-start(bf16[144,512]{1,0:T(8,128)(2,1)S(1)} %slice.44), channel_id=1, source_target_pairs={{0,2},{1,3},{2,0},{3,1},{4,6},{5,7},{6,4},{7,5},{8,10},{9,11},{10,... | collective-permute-start | bytes 442376 | tf_op jit(solution)/shard_map/ppermute | solution.py:238
  121.9 9.6 %collective-permute-start.21 = (bf16[144,512]{1,0:T(8,128)(2,1)S(1)}, bf16[144,512]{1,0:T(8,128)(2,1)S(1)}, u32[]{:S(2)}, u32[]{:S(2)}) collective-permute-start(bf16[144,512]{1,0:T(8,128)(2,1)S(1)} %slice.39), channel_id=1, source_target_pairs={{0,1},{1,0},{2,3},{3,2},{4,5},{5,4},{6,7},{7,6},{8,9},{9,8},{10,11... | collective-permute-start | bytes 442376 | tf_op jit(solution)/shard_map/ppermute | solution.py:238
  124.0 10.7 %collective-permute-start.22 = (bf16[144,512]{1,0:T(8,128)(2,1)S(1)}, bf16[144,512]{1,0:T(8,128)(2,1)S(1)}, u32[]{:S(2)}, u32[]{:S(2)}) collective-permute-start(bf16[144,512]{1,0:T(8,128)(2,1)S(1)} %slice.45), channel_id=1, source_target_pairs={{0,2},{1,3},{2,0},{3,1},{4,6},{5,7},{6,4},{7,5},{8,10},{9,11},{10,... | collective-permute-start | bytes 442376 | tf_op jit(solution)/shard_map/ppermute | solution.py:238
  127.9 10.5 %collective-permute-start.11 = (bf16[4,1,128,128]{3,2,1,0:T(8,128)(2,1)S(1)}, bf16[4,1,128,128]{3,2,1,0:T(8,128)(2,1)S(1)}, u32[]{:S(2)}, u32[]{:S(2)}) collective-permute-start(bf16[4,1,128,128]{3,2,1,0:T(8,128)(2,1)S(1)} %get-tuple-element.49), channel_id=1, source_target_pairs={{0,1},{1,0},{2,3},{3,2},{4,5},{5,4},{6,7},{7,6},{8,9},{9,8},{10,11... | collective-permute-start | bytes 393224 | tf_op jit(solution)/shard_map/ppermute | solution.py:238
  128.0 10.4 %collective-permute-start.12 = (bf16[4,1,128,128]{3,2,1,0:T(8,128)(2,1)S(1)}, bf16[4,1,128,128]{3,2,1,0:T(8,128)(2,1)S(1)}, u32[]{:S(2)}, u32[]{:S(2)}) collective-permute-start(bf16[4,1,128,128]{3,2,1,0:T(8,128)(2,1)S(1)} %get-tuple-element.48), channel_id=1, source_target_pairs={{0,2},{1,3},{2,0},{3,1},{4,6},{5,7},{6,4},{7,5},{8,10},{9,11},{10,... | collective-permute-start | bytes 393224 | tf_op jit(solution)/shard_map/ppermute | solution.py:238
  128.1 10.3 %collective-permute-start.13 = (bf16[4,1,128,128]{3,2,1,0:T(8,128)(2,1)S(1)}, bf16[4,1,128,128]{3,2,1,0:T(8,128)(2,1)S(1)}, u32[]{:S(2)}, u32[]{:S(2)}) collective-permute-start(bf16[4,1,128,128]{3,2,1,0:T(8,128)(2,1)S(1)} %get-tuple-element.47), channel_id=1, source_target_pairs={{0,3},{1,2},{2,1},{3,0},{4,7},{5,6},{6,5},{7,4},{8,11},{9,10},{10,... | collective-permute-start | bytes 393224 | tf_op jit(solution)/shard_map/ppermute | solution.py:238
  138.3 2.7 %collective-permute-start.23 = (f32[512,512]{1,0:T(8,128)S(1)}, f32[512,512]{1,0:T(8,128)S(1)}, u32[]{:S(2)}, u32[]{:S(2)}) collective-permute-start(f32[512,512]{1,0:T(8,128)S(1)} %get-tuple-element.36), channel_id=1, source_target_pairs={{0,16},{16,0},{1,17},{17,1},{2,18},{18,2},{3,19},{19,3},{4,20},{20... | collective-permute-start | bytes 3145736 | tf_op jit(solution)/shard_map/ppermute | solution.py:246
  142.8 0.8 copy-start
  143.6 19.4 %all-to-all-start.3 = ((bf16[16,128,128]{2,1,0:T(8,128)(2,1)}), bf16[16,128,128]{2,1,0:T(8,128)(2,1)S(1)}, u32[]{:S(2)}, u32[]{:S(2)}) async-start(bf16[16,128,128]{2,1,0:T(8,128)(2,1)} %bitcast.52), calls=%async_computation.3 | async-start | bytes 1048576 | tf_op jit(solution)/shard_map/all_to_all | solution.py:198

commit v7 on v6

--- a/solution.py
+++ b/solution.py
@@ -23,26 +23,28 @@
 
 def pack(arrays, n, items, part):
     rows, columns = arrays[0].shape
-    width = columns // n
+    groups = columns // n // part
     per = max(1, n // 4)
-    used = sorted({a for a, _ in items})
+    count = len(items)
 
     def body(*refs):
-        for i, (a, g) in enumerate(items):
-            for j in range(per):
-                start = j * width + g * part
-                refs[-1][j, i] = refs[used.index(a)][:, start : start + part]
+        for j in range(per):
+            for i in range(count):
+                refs[-1][j, i] = refs[j * count + i][...]
+
+    def block(j, g):
+        return pl.BlockSpec((rows, part), lambda i: (0, (i * per + j) * groups + g))
 
     return pl.pallas_call(
         body,
         grid=(n // per,),
-        in_specs=[pl.BlockSpec((rows, per * width), lambda i: (0, i))] * len(used),
-        out_specs=pl.BlockSpec((per, len(items), rows, part), lambda i: (i, 0, 0, 0)),
-        out_shape=jax.ShapeDtypeStruct((n, len(items), rows, part), arrays[0].dtype),
+        in_specs=[block(j, g) for j in range(per) for _, g in items],
+        out_specs=pl.BlockSpec((per, count, rows, part), lambda i: (i, 0, 0, 0)),
+        out_shape=jax.ShapeDtypeStruct((n, count, rows, part), arrays[0].dtype),
         compiler_params=params(60),
         cost_estimate=small(),
         name="pack",
-    )(*[arrays[a] for a in used])
+    )(*[arrays[a] for _ in range(per) for a, _ in items])
 
 
 def unpack(parts):
@@ -227,11 +229,16 @@
     )(*parts).reshape(count * planes, *rest)
 
 
-def spread_planes(blocks, place):
-    n = blocks.shape[0]
-    lines = blocks.reshape(n // QUAD, QUAD, *blocks.shape[1:])
-    sent = [lax.dynamic_index_in_dim(lines, place ^ r, 1, keepdims=False) for r in range(QUAD)]
-    return join([sent[0]] + [exchange(sent[r], r, n) for r in range(1, QUAD)])
+def spread_planes(blocks, place, first, count):
+    n, items, rows, width = blocks.shape
+    lines = blocks.reshape(n // QUAD, QUAD, items, rows, width)
+    parts = []
+    for r in range(QUAD):
+        part = lax.dynamic_slice(
+            lines, (0, place ^ r, first, 0, 0), (n // QUAD, 1, count, rows, width)
+        )[:, 0]
+        parts.append(exchange(part, r, n) if r else part)
+    return parts
 
 
 def exchange(value, apart, n):
@@ -346,13 +353,13 @@
         out_shape=[jax.ShapeDtypeStruct((positions, 2 * width), jnp.float32)] * 2,
         compiler_params=params(),
         cost_estimate=pl.CostEstimate(
-            flops=7000000000, bytes_accessed=8 * 1024 * 1024, transcendentals=0
+            flops=16000000000, bytes_accessed=8 * 1024 * 1024, transcendentals=0
         ),
         name="project",
     )(where, *pieces, key_weight, value_weight)
 
 
-def text_of_pair(embed, key_weight, value_weight, length, encoder, n, before, between, after):
+def text_of_pair(embed, key_weight, value_weight, length, encoder, n, between, after):
     positions, columns = embed.shape
     core = lax.axis_index("dp")
     me = lax.axis_index("seq")
@@ -386,7 +393,6 @@
         piece = choose(piece, exchange(piece, 1 << bit, n), bit)
     near = (me >> 2) & 1
     own = jnp.where(near == 0, piece[:, : half // 2], piece[:, half // 2 :])
-    own = before(own)
     own = between(choose(own, exchange(own, 1 << last, n), last))
     far, own_x, own_y = exchange(own, 4, n), exchange(own, 1, n), exchange(own, 2, n)
     pieces = []
@@ -437,19 +443,13 @@
 
     part = heads // 2 * HEAD
     place = lax.axis_index("seq") & (QUAD - 1)
-    lines = spread_lines(pack(inputs, n, [(a, 0) for a in range(4)], part))
-    cross_second = pack(inputs, n, [(3, 1)], part)
-    lines, cross_second = lax.optimization_barrier((lines, cross_second))
-    cross_second = spread(cross_second)
-    earlier = spread_planes(lines[:, :3], place)
-    cross_first = spread_planes(lines[:, 3:], place)
-    rest = pack(inputs, n, [(a, 1) for a in range(3)], part)
+    lines = pack(inputs, n, [(a, 0) for a in range(4)], part)
+    lines, embed = lax.optimization_barrier((lines, embed))
+    lines = spread_lines(lines)
+    earlier = join(spread_planes(lines, place, 0, 3))
+    cross_first = join(spread_planes(lines, place, 3, 1))
+    rest = pack(inputs, n, [(a, 1) for a in range(4)], part)
     self_first = later = None
-
-    def before(piece):
-        nonlocal cross_second
-        piece, cross_second = lax.optimization_barrier((piece, cross_second))
-        return piece
 
     def between(piece):
         nonlocal rest, earlier, self_first, later
@@ -464,13 +464,13 @@
         return piece
 
     text = text_of_pair(
-        embed, *weights, text_lengths[0], encoder_index[0], n, before, between, after
+        embed, *weights, text_lengths[0], encoder_index[0], n, between, after
     )
     out = cross_attention(cross_first, 0, text, 0, text_lengths, self_first, place)
     later, out = lax.optimization_barrier((later, out))
     tokens = spread(out)
     self_second = self_attention(later, 0)
-    out = cross_attention(cross_second, 0, text, heads // 2, text_lengths, self_second)
+    out = cross_attention(later, 3, text, heads // 2, text_lengths, self_second)
     tokens, out = lax.optimization_barrier((tokens, out))
     return unpack([tokens, spread(out)])[None]
 

time: 184 us -> 183 us (level)
  waiting for transfers between devices: 68.8 us -> 73.9 us
  Pallas kernels: 34.5 us -> 30.5 us
    ppermute x21, waiting for transfers between devices: 45.3 us -> 55.9 us  [exchange(): return lax.ppermute(value, 'seq', [(i, i ^ apart) for i in range(n)])]
    pallas_call x3 -> x2, Pallas kernels: 11.5 us -> 7.49 us  [pack(): pl.pallas_call(body, grid=(n // per,), in_specs=[block(j, g) for j in ran...]
    all_to_all x4 -> x3, waiting for transfers between devices: 20.1 us -> 17.2 us  [spread(): lax.all_to_all(flat, 'seq', split_axis=0, concat_axis=0, tiled=True, axis...]
    slice x2 -> x0, local copies, waits for them, and re-layouts: 2.6 us -> none  [the longest x1 1.52 us: shards(): earlier = spread_planes(lines[:, :3], place)]
    ppermute x3, waiting for transfers between devices: 3.36 us -> 0.92 us  [swap(): return lax.ppermute(value, 'dp', [(0, 1), (1, 0)])]
    unnamed x8 -> x10, local copies, waits for them, and re-layouts: 3.34 us -> 4.12 us
    all_to_all x4 -> x3, starting transfers between devices: 20.2 us -> 19.8 us  [spread(): lax.all_to_all(flat, 'seq', split_axis=0, concat_axis=0, tiled=True, axis...]
  transfers between devices with their start and end apart: 28 -> 27, of which waited for: 16 -> 13; matrix products, arithmetic and copies ran while one was open for 4% -> 3% of each run, Pallas kernels for 18% -> 14%
where the time goes in v7:
time: 183 us; the launch traced here: 182 us
  waiting for transfers between devices  73.9 us (40%)
  starting transfers between devices  46.6 us (25%)
  Pallas kernels  30.5 us (17%)
  blocking collectives  18.4 us (10%)
  local copies, waits for them, and re-layouts  7.54 us (4%)
  between operations  3.57 us (2%)
    ppermute x21, waiting for transfers between devices, exchange(): return lax.ppermute(value, 'seq', [(i, i ^ apart) for i in range(n)])  55.9 us
    ppermute x21, starting transfers between devices, exchange(): return lax.ppermute(value, 'seq', [(i, i ^ apart) for i in range(n)])  26 us
    all_to_all x3, starting transfers between devices, spread(): lax.all_to_all(flat, 'seq', split_axis=0, concat_axis=0, tiled=True, axis...  19.8 us
    all_to_all x1, blocking collectives, spread(): lax.all_to_all(flat, 'seq', split_axis=0, concat_axis=0, tiled=True, axis...  18.4 us
    all_to_all x3, waiting for transfers between devices, spread(): lax.all_to_all(flat, 'seq', split_axis=0, concat_axis=0, tiled=True, axis...  17.2 us
    pallas_call x2, Pallas kernels, self_attention(): pl.pallas_call(body, grid_spec=pltpu.PrefetchScalarGridSpec(num_scalar_pr...  11.4 us
    pallas_call x2, Pallas kernels, pack(): pl.pallas_call(body, grid=(n // per,), in_specs=[block(j, g) for j in ran...  7.49 us
    unnamed x10, local copies, waits for them, and re-layouts  4.12 us
  transfers between devices with their start and end apart: 27, of which 13 were waited for; matrix products, arithmetic and copies ran while one was open for 3% of the time, Pallas kernels for 14%

profile of v7, /device:TPU:0, one launch (start us, length us, event | category | flops | bytes accessed | tf_op | source)
XLA Modules:
  0.0 181.9 jit_solution(4319775067489230348)
XLA Ops:
  0.0 3.8 %pack.2 = bf16[16,4,128,128]{3,2,1,0:T(8,128)(2,1)} custom-call(bf16[128,4096]{1,0:T(8,128)(2,1)} %bitcast.53, bf16[128,4096]{1,0:T(8,128)(2,1)} %bitcast.61, bf16[128,4096]{1,0:T(8,128)(2,1)} %bitcast.69, bf16[128,4096]{1,0:T(8,128)(2,1)} %bitcast.77, bf16[128,4096]{1,0:T(8,128)(2,1)} %bitcast.54, bf16[128,4096]{1,0:T(8,128)(2,1)} %bitcast.62, ...), custom_call_target="tpu_custom_call" | custom-call | bytes 4194304 | tf_op jit(solution)/shard_map/pack/pallas_call | solution.py:38
  3.8 0.5 collective-permute-start.1
  4.3 5.9 %all-to-all-start = ((bf16[16,512,128]{2,1,0:T(8,128)(2,1)}), bf16[16,512,128]{2,1,0:T(8,128)(2,1)}, u32[]{:S(2)}, u32[]{:S(2)}) async-start(bf16[16,512,128]{2,1,0:T(8,128)(2,1)} %bitcast.86), calls=%async_computation | async-start | bytes 4194304 | tf_op jit(solution)/shard_map/all_to_all | solution.py:200
  11.6 0.2 collective-permute-start
  11.8 0.9 collective-permute-done
  12.7 0.7 fusion.1
  14.0 2.9 %quarters.1 = (bf16[2,144,1024]{2,1,0:T(8,128)(2,1)S(1)}, bf16[2,144,1024]{2,1,0:T(8,128)(2,1)S(1)}, bf16[2,144,1024]{2,1,0:T(8,128)(2,1)S(1)}, bf16[2,144,1024]{2,1,0:T(8,128)(2,1)S(1)}) custom-call(s32[3]{0:T(128)S(1)} %pad_add_fusion.1.where_ref, bf16[512,4096]{1,0:T(8,128)(2,1)} %bitcast.88, bf16[512,4096]{1,0:T(8,128)(2,1)} %collective-permute-done.1.other_ref), custom_call_target="tpu_custom_call" | custom-call | bytes 4194304 | tf_op jit(solution)/shard_map/quarters/pallas_call | solution.py:287
  16.9 1.6 collective-permute-start.4
  19.9 1.6 collective-permute-start.2
  21.5 11.0 %collective-permute-done.4 = bf16[2,144,1024]{2,1,0:T(8,128)(2,1)S(1)} collective-permute-done((bf16[2,144,1024]{2,1,0:T(8,128)(2,1)S(1)}, bf16[2,144,1024]{2,1,0:T(8,128)(2,1)S(1)}, u32[]{:S(2)}, u32[]{:S(2)}) %collective-permute-start.4) | collective-permute-done | bytes 589856 | tf_op jit(solution)/shard_map/ppermute | solution.py:245
  32.4 0.1 broadcast_select_fusion
  32.6 1.6 collective-permute-start.5
  34.1 1.3 collective-permute-done.2
  35.4 0.1 broadcast_select_fusion.1
  35.6 0.3 collective-permute-start.3
  35.9 5.5 %collective-permute-done.5 = bf16[144,1024]{1,0:T(8,128)(2,1)S(1)} collective-permute-done((bf16[144,1024]{1,0:T(8,128)(2,1)S(1)}, bf16[144,1024]{1,0:T(8,128)(2,1)S(1)}, u32[]{:S(2)}, u32[]{:S(2)}) %collective-permute-start.5) | collective-permute-done | bytes 294944 | tf_op jit(solution)/shard_map/ppermute | solution.py:245
  41.4 0.1 bitcast_select_fusion
  41.5 1.9 %collective-permute-done.3 = bf16[144,1024]{1,0:T(8,128)(2,1)S(1)} collective-permute-done((bf16[144,1024]{1,0:T(8,128)(2,1)S(1)}, bf16[144,1024]{1,0:T(8,128)(2,1)S(1)}, u32[]{:S(2)}, u32[]{:S(2)}) %collective-permute-start.3) | collective-permute-done | bytes 294944 | tf_op jit(solution)/shard_map/ppermute | solution.py:245
  43.6 2.1 %collective-permute-start.6 = (bf16[144,2048]{1,0:T(8,128)(2,1)S(1)}, bf16[144,2048]{1,0:T(8,128)(2,1)S(1)}, u32[]{:S(2)}, u32[]{:S(2)}) collective-permute-start(bf16[144,2048]{1,0:T(8,128)(2,1)S(1)} %pad_maximum_fusion), channel_id=1, source_target_pairs={{0,4},{1,5},{2,6},{3,7},{4,0},{5,1},{6,2},{7,3},{8,12},{9,13},{10,... | collective-permute-start | bytes 1769480 | tf_op jit(solution)/shard_map/ppermute | solution.py:245
  45.6 3.7 %pack.3 = bf16[16,4,128,128]{3,2,1,0:T(8,128)(2,1)} custom-call(bf16[128,4096]{1,0:T(8,128)(2,1)} %bitcast.57, bf16[128,4096]{1,0:T(8,128)(2,1)} %bitcast.65, bf16[128,4096]{1,0:T(8,128)(2,1)} %bitcast.73, bf16[128,4096]{1,0:T(8,128)(2,1)} %bitcast.81, bf16[128,4096]{1,0:T(8,128)(2,1)} %bitcast.58, bf16[128,4096]{1,0:T(8,128)(2,1)} %bitcast.66, ...), custom_call_target="tpu_custom_call" | custom-call | bytes 4194304 | tf_op jit(solution)/shard_map/pack/pallas_call | solution.py:38
  49.4 9.8 %all-to-all-done = bf16[16,512,128]{2,1,0:T(8,128)(2,1)} async-done(((bf16[16,512,128]{2,1,0:T(8,128)(2,1)}), bf16[16,512,128]{2,1,0:T(8,128)(2,1)}, u32[]{:S(2)}, u32[]{:S(2)}) %all-to-all-start) | async-done | bytes 2097184 | tf_op jit(solution)/shard_map/all_to_all | solution.py:200
  59.2 1.5 dynamic-slice_bitcast_fusion
  60.8 1.6 collective-permute-start.8
  62.3 1.5 collective-permute-start.9
  63.8 0.5 collective-permute-start.10
  64.3 3.0 %collective-permute-done.6 = bf16[144,2048]{1,0:T(8,128)(2,1)S(1)} collective-permute-done((bf16[144,2048]{1,0:T(8,128)(2,1)S(1)}, bf16[144,2048]{1,0:T(8,128)(2,1)S(1)}, u32[]{:S(2)}, u32[]{:S(2)}) %collective-permute-start.6) | collective-permute-done | bytes 589856 | tf_op jit(solution)/shard_map/ppermute | solution.py:245
  67.4 0.2 broadcast_select_fusion.2
  67.6 2.3 %collective-permute-start.7 = (bf16[144,1024]{1,0:T(8,128)(2,1)S(1)}, bf16[144,1024]{1,0:T(8,128)(2,1)S(1)}, u32[]{:S(2)}, u32[]{:S(2)}) collective-permute-start(bf16[144,1024]{1,0:T(8,128)(2,1)S(1)} %slice_select_fusion), channel_id=1, source_target_pairs={{0,8},{1,9},{2,10},{3,11},{4,12},{5,13},{6,14},{7,15},{8,0},{9,1},... | collective-permute-start | bytes 884744 | tf_op jit(solution)/shard_map/ppermute | solution.py:245
  70.0 2.9 %collective-permute-done.8.refs_1_ = bf16[4,3,128,128]{3,2,1,0:T(8,128)(2,1)S(1)} collective-permute-done((bf16[4,3,128,128]{3,2,1,0:T(8,128)(2,1)S(1)}, bf16[4,3,128,128]{3,2,1,0:T(8,128)(2,1)S(1)}, u32[]{:S(2)}, u32[]{:S(2)}) %collective-permute-start.8) | collective-permute-done | bytes 393248 | tf_op jit(solution)/shard_map/ppermute | solution.py:245
  72.9 7.9 %collective-permute-done.9.refs_2_ = bf16[4,3,128,128]{3,2,1,0:T(8,128)(2,1)S(1)} collective-permute-done((bf16[4,3,128,128]{3,2,1,0:T(8,128)(2,1)S(1)}, bf16[4,3,128,128]{3,2,1,0:T(8,128)(2,1)S(1)}, u32[]{:S(2)}, u32[]{:S(2)}) %collective-permute-start.9) | collective-permute-done | bytes 393248 | tf_op jit(solution)/shard_map/ppermute | solution.py:245
  80.8 0.3 join.2
  81.1 1.1 copy-done.3
  82.2 0.1 broadcast_select_fusion.3.refs_0_
  82.3 0.4 collective-permute-start.18
  82.7 1.5 collective-permute-start.14
  84.2 0.3 collective-permute-start.15
  84.5 5.9 %all-to-all-start.1 = ((bf16[16,512,128]{2,1,0:T(8,128)(2,1)}), bf16[16,512,128]{2,1,0:T(8,128)(2,1)S(1)}, u32[]{:S(2)}, u32[]{:S(2)}) async-start(bf16[16,512,128]{2,1,0:T(8,128)(2,1)} %bitcast.85), calls=%async_computation.1 | async-start | bytes 4194304 | tf_op jit(solution)/shard_map/all_to_all | solution.py:200
  90.5 2.0 %collective-permute-start.19 = (bf16[144,1024]{1,0:T(8,128)(2,1)S(1)}, bf16[144,1024]{1,0:T(8,128)(2,1)S(1)}, u32[]{:S(2)}, u32[]{:S(2)}) collective-permute-start(bf16[144,1024]{1,0:T(8,128)(2,1)S(1)} %collective-permute-done.18.refs_5_), channel_id=1, source_target_pairs={{0,1},{1,0},{2,3},{3,2},{4,5},{5,4},{6,7},{7,6},{8,9},{9,8},{10,11... | collective-permute-start | bytes 884744 | tf_op jit(solution)/shard_map/ppermute | solution.py:245
  92.4 1.5 collective-permute-start.20
  93.9 1.4 copy-done.4
  95.3 5.7 %self_attention.2 = bf16[4,4,128,128]{3,2,1,0:T(8,128)(2,1)S(1)} custom-call(s32[1]{0:T(128)} %bitcast.3.place_ref, bf16[16,3,128,128]{3,2,1,0:T(8,128)(2,1)S(1)} %bitcast.49, bf16[16,3,128,128]{3,2,1,0:T(8,128)(2,1)S(1)} %bitcast.50, bf16[16,3,128,128]{3,2,1,0:T(8,128)(2,1)S(1)} %bitcast.51), custom_call_target="tpu_custom_call" | custom-call | flops 8589934592 | bytes 2097152 | tf_op jit(solution)/shard_map/self_attention/pallas_call | solution.py:110
  101.0 0.6 collective-permute-start.16
  101.7 0.2 collective-permute-start.17
  101.9 13.7 %collective-permute-done.20.refs_7_ = bf16[144,1024]{1,0:T(8,128)(2,1)S(1)} collective-permute-done((bf16[144,1024]{1,0:T(8,128)(2,1)S(1)}, bf16[144,1024]{1,0:T(8,128)(2,1)S(1)}, u32[]{:S(2)}, u32[]{:S(2)}) %collective-permute-start.20) | collective-permute-done | bytes 294944 | tf_op jit(solution)/shard_map/ppermute | solution.py:245
  115.6 1.6 collective-permute-start.21
  117.3 0.5 collective-permute-start.22
  117.8 1.1 dynamic-slice_bitcast_fusion.6
  119.0 0.1 collective-permute-start.11
  119.1 2.0 %collective-permute-start.12 = (bf16[4,1,128,128]{3,2,1,0:T(8,128)(2,1)S(1)}, bf16[4,1,128,128]{3,2,1,0:T(8,128)(2,1)S(1)}, u32[]{:S(2)}, u32[]{:S(2)}) collective-permute-start(bf16[4,1,128,128]{3,2,1,0:T(8,128)(2,1)S(1)} %get-tuple-element.40), channel_id=1, source_target_pairs={{0,2},{1,3},{2,0},{3,1},{4,6},{5,7},{6,4},{7,5},{8,10},{9,11},{10,... | collective-permute-start | bytes 393224 | tf_op jit(solution)/shard_map/ppermute | solution.py:245
  121.1 2.3 %collective-permute-start.13 = (bf16[4,1,128,128]{3,2,1,0:T(8,128)(2,1)S(1)}, bf16[4,1,128,128]{3,2,1,0:T(8,128)(2,1)S(1)}, u32[]{:S(2)}, u32[]{:S(2)}) collective-permute-start(bf16[4,1,128,128]{3,2,1,0:T(8,128)(2,1)S(1)} %get-tuple-element.39), channel_id=1, source_target_pairs={{0,3},{1,2},{2,1},{3,0},{4,7},{5,6},{6,5},{7,4},{8,11},{9,10},{10,... | collective-permute-start | bytes 393224 | tf_op jit(solution)/shard_map/ppermute | solution.py:245
  123.4 0.8 collective-permute-done.21.refs_8_
  124.3 3.5 %project.1 = (f32[512,512]{1,0:T(8,128)S(1)}, f32[512,512]{1,0:T(8,128)S(1)}) custom-call(s32[3]{0:T(128)S(1)} %pad_add_fusion.2.where_ref, bf16[144,1024]{1,0:T(8,128)(2,1)S(1)} %broadcast_select_fusion.3.refs_0_, bf16[144,1024]{1,0:T(8,128)(2,1)S(1)} %collective-permute-done.14.refs_1_, bf16[144,1024]{1,0:T(8,128)(2,1)S(1)} %collective-permute-done.15.refs_2_, ...), custom_call_target="tpu_custom_call" | custom-call | flops 16000000000 | bytes 8388608 | tf_op jit(solution)/shard_map/project/pallas_call | solution.py:344
  127.9 7.7 %collective-permute-done.13.refs_3_ = bf16[4,1,128,128]{3,2,1,0:T(8,128)(2,1)S(1)} collective-permute-done((bf16[4,1,128,128]{3,2,1,0:T(8,128)(2,1)S(1)}, bf16[4,1,128,128]{3,2,1,0:T(8,128)(2,1)S(1)}, u32[]{:S(2)}, u32[]{:S(2)}) %collective-permute-start.13) | collective-permute-done | bytes 131104 | tf_op jit(solution)/shard_map/ppermute | solution.py:245
  135.6 0.1 join.3
  135.8 0.3 add_convert_fusion.k_ref.v_ref
  136.0 1.6 cross_attention.2
  137.6 0.8 copy-done
  138.4 8.0 %all-to-all-start.2 = ((bf16[16,128,128]{2,1,0:T(8,128)(2,1)}), bf16[16,128,128]{2,1,0:T(8,128)(2,1)S(1)}, u32[]{:S(2)}, u32[]{:S(2)}) async-start(bf16[16,128,128]{2,1,0:T(8,128)(2,1)} %bitcast.48), calls=%async_computation.2 | async-start | bytes 1048576 | tf_op jit(solution)/shard_map/all_to_all | solution.py:200
  146.5 5.7 %self_attention.3.self_ref = bf16[16,128,128]{2,1,0:T(8,128)(2,1)S(1)} custom-call(s32[1]{0:T(128)} %constant.38.clone.1.place_ref, bf16[16,4,128,128]{3,2,1,0:T(8,128)(2,1)S(1)} %bitcast.44, bf16[16,4,128,128]{3,2,1,0:T(8,128)(2,1)S(1)} %bitcast.45, bf16[16,4,128,128]{3,2,1,0:T(8,128)(2,1)S(1)} %bitcast.46), custom_call_target="tpu_custom_call" | custom-call | flops 8589934592 | bytes 2097152 | tf_op jit(solution)/shard_map/self_attention/pallas_call | solution.py:110
  152.2 1.6 cross_attention.3
  153.7 0.8 copy-done.1
  154.5 7.3 %all-to-all-done.2.refs_0_ = bf16[16,128,128]{2,1,0:T(8,128)(2,1)S(1)} async-done(((bf16[16,128,128]{2,1,0:T(8,128)(2,1)}), bf16[16,128,128]{2,1,0:T(8,128)(2,1)S(1)}, u32[]{:S(2)}, u32[]{:S(2)}) %all-to-all-start.2) | async-done | bytes 524320 | tf_op jit(solution)/shard_map/all_to_all | solution.py:200
  161.9 18.4 %all_to_all.20.refs_1_ = bf16[16,128,128]{2,1,0:T(8,128)(2,1)S(1)} all-to-all(bf16[16,128,128]{2,1,0:T(8,128)(2,1)} %copy-done.1), channel_id=1, replica_groups=mesh['dp'=2,'seq'=16] {'seq'}, dimensions={0} | all-to-all | bytes 1048576 | tf_op jit(solution)/shard_map/all_to_all | solution.py:200
  180.2 1.6 unpack.1
  (37 shorter events, 0.7 us)
Async XLA Ops:
  3.8 10.2 %collective-permute-start.1 = (bf16[512,4096]{1,0:T(8,128)(2,1)}, bf16[512,4096]{1,0:T(8,128)(2,1)}, u32[]{:S(2)}, u32[]{:S(2)}) collective-permute-start(bf16[512,4096]{1,0:T(8,128)(2,1)} %bitcast.87), channel_id=1, source_target_pairs={{0,16},{16,0},{1,17},{17,1},{2,18},{18,2},{3,19},{19,3},{4,20},{20... | collective-permute-start | bytes 12582920 | tf_op jit(solution)/shard_map/ppermute | solution.py:253
  4.3 54.9 %all-to-all-start = ((bf16[16,512,128]{2,1,0:T(8,128)(2,1)}), bf16[16,512,128]{2,1,0:T(8,128)(2,1)}, u32[]{:S(2)}, u32[]{:S(2)}) async-start(bf16[16,512,128]{2,1,0:T(8,128)(2,1)} %bitcast.86), calls=%async_computation | async-start | bytes 4194304 | tf_op jit(solution)/shard_map/all_to_all | solution.py:200
  11.6 1.1 collective-permute-start
  16.9 15.5 %collective-permute-start.4 = (bf16[2,144,1024]{2,1,0:T(8,128)(2,1)S(1)}, bf16[2,144,1024]{2,1,0:T(8,128)(2,1)S(1)}, u32[]{:S(2)}, u32[]{:S(2)}) collective-permute-start(bf16[2,144,1024]{2,1,0:T(8,128)(2,1)S(1)} %get-tuple-element.26), channel_id=1, source_target_pairs={{0,2},{1,3},{2,0},{3,1},{4,6},{5,7},{6,4},{7,5},{8,10},{9,11},{10,... | collective-permute-start | bytes 1769480 | tf_op jit(solution)/shard_map/ppermute | solution.py:245
  19.9 15.5 %collective-permute-start.2 = (bf16[2,144,1024]{2,1,0:T(8,128)(2,1)S(1)}, bf16[2,144,1024]{2,1,0:T(8,128)(2,1)S(1)}, u32[]{:S(2)}, u32[]{:S(2)}) collective-permute-start(bf16[2,144,1024]{2,1,0:T(8,128)(2,1)S(1)} %get-tuple-element.24), channel_id=1, source_target_pairs={{0,1},{1,0},{2,3},{3,2},{4,5},{5,4},{6,7},{7,6},{8,9},{9,8},{10,11... | collective-permute-start | bytes 1769480 | tf_op jit(solution)/shard_map/ppermute | solution.py:245
  32.6 8.8 %collective-permute-start.5 = (bf16[144,1024]{1,0:T(8,128)(2,1)S(1)}, bf16[144,1024]{1,0:T(8,128)(2,1)S(1)}, u32[]{:S(2)}, u32[]{:S(2)}) collective-permute-start(bf16[144,1024]{1,0:T(8,128)(2,1)S(1)} %dynamic-slice_bitcast_fusion.4), channel_id=1, source_target_pairs={{0,1},{1,0},{2,3},{3,2},{4,5},{5,4},{6,7},{7,6},{8,9},{9,8},{10,11... | collective-permute-start | bytes 884744 | tf_op jit(solution)/shard_map/ppermute | solution.py:245
  35.6 7.8 %collective-permute-start.3 = (bf16[144,1024]{1,0:T(8,128)(2,1)S(1)}, bf16[144,1024]{1,0:T(8,128)(2,1)S(1)}, u32[]{:S(2)}, u32[]{:S(2)}) collective-permute-start(bf16[144,1024]{1,0:T(8,128)(2,1)S(1)} %dynamic-slice_bitcast_fusion.5), channel_id=1, source_target_pairs={{0,2},{1,3},{2,0},{3,1},{4,6},{5,7},{6,4},{7,5},{8,10},{9,11},{10,... | collective-permute-start | bytes 884744 | tf_op jit(solution)/shard_map/ppermute | solution.py:245
  43.6 23.8 %collective-permute-start.6 = (bf16[144,2048]{1,0:T(8,128)(2,1)S(1)}, bf16[144,2048]{1,0:T(8,128)(2,1)S(1)}, u32[]{:S(2)}, u32[]{:S(2)}) collective-permute-start(bf16[144,2048]{1,0:T(8,128)(2,1)S(1)} %pad_maximum_fusion), channel_id=1, source_target_pairs={{0,4},{1,5},{2,6},{3,7},{4,0},{5,1},{6,2},{7,3},{8,12},{9,13},{10,... | collective-permute-start | bytes 1769480 | tf_op jit(solution)/shard_map/ppermute | solution.py:245
  60.8 12.1 %collective-permute-start.8 = (bf16[4,3,128,128]{3,2,1,0:T(8,128)(2,1)S(1)}, bf16[4,3,128,128]{3,2,1,0:T(8,128)(2,1)S(1)}, u32[]{:S(2)}, u32[]{:S(2)}) collective-permute-start(bf16[4,3,128,128]{3,2,1,0:T(8,128)(2,1)S(1)} %get-tuple-element.45), channel_id=1, source_target_pairs={{0,1},{1,0},{2,3},{3,2},{4,5},{5,4},{6,7},{7,6},{8,9},{9,8},{10,11... | collective-permute-start | bytes 1179656 | tf_op jit(solution)/shard_map/ppermute | solution.py:245
  62.3 18.5 %collective-permute-start.9 = (bf16[4,3,128,128]{3,2,1,0:T(8,128)(2,1)S(1)}, bf16[4,3,128,128]{3,2,1,0:T(8,128)(2,1)S(1)}, u32[]{:S(2)}, u32[]{:S(2)}) collective-permute-start(bf16[4,3,128,128]{3,2,1,0:T(8,128)(2,1)S(1)} %get-tuple-element.44), channel_id=1, source_target_pairs={{0,2},{1,3},{2,0},{3,1},{4,6},{5,7},{6,4},{7,5},{8,10},{9,11},{10,... | collective-permute-start | bytes 1179656 | tf_op jit(solution)/shard_map/ppermute | solution.py:245
  63.8 17.0 %collective-permute-start.10 = (bf16[4,3,128,128]{3,2,1,0:T(8,128)(2,1)S(1)}, bf16[4,3,128,128]{3,2,1,0:T(8,128)(2,1)S(1)}, u32[]{:S(2)}, u32[]{:S(2)}) collective-permute-start(bf16[4,3,128,128]{3,2,1,0:T(8,128)(2,1)S(1)} %get-tuple-element.43), channel_id=1, source_target_pairs={{0,3},{1,2},{2,1},{3,0},{4,7},{5,6},{6,5},{7,4},{8,11},{9,10},{10,... | collective-permute-start | bytes 1179656 | tf_op jit(solution)/shard_map/ppermute | solution.py:245
  67.6 14.6 %collective-permute-start.7 = (bf16[144,1024]{1,0:T(8,128)(2,1)S(1)}, bf16[144,1024]{1,0:T(8,128)(2,1)S(1)}, u32[]{:S(2)}, u32[]{:S(2)}) collective-permute-start(bf16[144,1024]{1,0:T(8,128)(2,1)S(1)} %slice_select_fusion), channel_id=1, source_target_pairs={{0,8},{1,9},{2,10},{3,11},{4,12},{5,13},{6,14},{7,15},{8,0},{9,1},... | collective-permute-start | bytes 884744 | tf_op jit(solution)/shard_map/ppermute | solution.py:245
  81.1 1.1 copy-start.3
  82.3 8.1 %collective-permute-start.18 = (bf16[144,1024]{1,0:T(8,128)(2,1)S(1)}, bf16[144,1024]{1,0:T(8,128)(2,1)S(1)}, u32[]{:S(2)}, u32[]{:S(2)}) collective-permute-start(bf16[144,1024]{1,0:T(8,128)(2,1)S(1)} %broadcast_select_fusion.3.refs_0_), channel_id=1, source_target_pairs={{0,4},{1,5},{2,6},{3,7},{4,0},{5,1},{6,2},{7,3},{8,12},{9,13},{10,... | collective-permute-start | bytes 884744 | tf_op jit(solution)/shard_map/ppermute | solution.py:245
  82.7 19.0 %collective-permute-start.14 = (bf16[144,1024]{1,0:T(8,128)(2,1)S(1)}, bf16[144,1024]{1,0:T(8,128)(2,1)S(1)}, u32[]{:S(2)}, u32[]{:S(2)}) collective-permute-start(bf16[144,1024]{1,0:T(8,128)(2,1)S(1)} %broadcast_select_fusion.3.refs_0_), channel_id=1, source_target_pairs={{0,1},{1,0},{2,3},{3,2},{4,5},{5,4},{6,7},{7,6},{8,9},{9,8},{10,11... | collective-permute-start | bytes 884744 | tf_op jit(solution)/shard_map/ppermute | solution.py:245
  84.2 16.8 %collective-permute-start.15 = (bf16[144,1024]{1,0:T(8,128)(2,1)S(1)}, bf16[144,1024]{1,0:T(8,128)(2,1)S(1)}, u32[]{:S(2)}, u32[]{:S(2)}) collective-permute-start(bf16[144,1024]{1,0:T(8,128)(2,1)S(1)} %broadcast_select_fusion.3.refs_0_), channel_id=1, source_target_pairs={{0,2},{1,3},{2,0},{3,1},{4,6},{5,7},{6,4},{7,5},{8,10},{9,11},{10,... | collective-permute-start | bytes 884744 | tf_op jit(solution)/shard_map/ppermute | solution.py:245
  84.5 53.9 %all-to-all-start.1 = ((bf16[16,512,128]{2,1,0:T(8,128)(2,1)}), bf16[16,512,128]{2,1,0:T(8,128)(2,1)S(1)}, u32[]{:S(2)}, u32[]{:S(2)}) async-start(bf16[16,512,128]{2,1,0:T(8,128)(2,1)} %bitcast.85), calls=%async_computation.1 | async-start | bytes 4194304 | tf_op jit(solution)/shard_map/all_to_all | solution.py:200
  90.5 26.8 %collective-permute-start.19 = (bf16[144,1024]{1,0:T(8,128)(2,1)S(1)}, bf16[144,1024]{1,0:T(8,128)(2,1)S(1)}, u32[]{:S(2)}, u32[]{:S(2)}) collective-permute-start(bf16[144,1024]{1,0:T(8,128)(2,1)S(1)} %collective-permute-done.18.refs_5_), channel_id=1, source_target_pairs={{0,1},{1,0},{2,3},{3,2},{4,5},{5,4},{6,7},{7,6},{8,9},{9,8},{10,11... | collective-permute-start | bytes 884744 | tf_op jit(solution)/shard_map/ppermute | solution.py:245
  92.4 23.2 %collective-permute-start.20 = (bf16[144,1024]{1,0:T(8,128)(2,1)S(1)}, bf16[144,1024]{1,0:T(8,128)(2,1)S(1)}, u32[]{:S(2)}, u32[]{:S(2)}) collective-permute-start(bf16[144,1024]{1,0:T(8,128)(2,1)S(1)} %collective-permute-done.18.refs_5_), channel_id=1, source_target_pairs={{0,2},{1,3},{2,0},{3,1},{4,6},{5,7},{6,4},{7,5},{8,10},{9,11},{10,... | collective-permute-start | bytes 884744 | tf_op jit(solution)/shard_map/ppermute | solution.py:245
  93.9 1.4 copy-start.4
  101.0 23.2 %copy-start.2 = (bf16[2048,256]{1,0:T(8,128)(2,1)S(1)}, bf16[2048,256]{1,0:T(8,128)(2,1)}, u32[]{:S(2)}) copy-start(bf16[2048,256]{1,0:T(8,128)(2,1)} %refs_10_.1) | copy-start | bytes 3145732
  101.0 18.0 %collective-permute-start.16 = (bf16[144,512]{1,0:T(8,128)(2,1)S(1)}, bf16[144,512]{1,0:T(8,128)(2,1)S(1)}, u32[]{:S(2)}, u32[]{:S(2)}) collective-permute-start(bf16[144,512]{1,0:T(8,128)(2,1)S(1)} %slice.35), channel_id=1, source_target_pairs={{0,1},{1,0},{2,3},{3,2},{4,5},{5,4},{6,7},{7,6},{8,9},{9,8},{10,11... | collective-permute-start | bytes 442376 | tf_op jit(solution)/shard_map/ppermute | solution.py:245
  101.7 19.4 %collective-permute-start.17 = (bf16[144,512]{1,0:T(8,128)(2,1)S(1)}, bf16[144,512]{1,0:T(8,128)(2,1)S(1)}, u32[]{:S(2)}, u32[]{:S(2)}) collective-permute-start(bf16[144,512]{1,0:T(8,128)(2,1)S(1)} %slice.36), channel_id=1, source_target_pairs={{0,2},{1,3},{2,0},{3,1},{4,6},{5,7},{6,4},{7,5},{8,10},{9,11},{10,... | collective-permute-start | bytes 442376 | tf_op jit(solution)/shard_map/ppermute | solution.py:245
  115.6 8.6 %collective-permute-start.21 = (bf16[144,512]{1,0:T(8,128)(2,1)S(1)}, bf16[144,512]{1,0:T(8,128)(2,1)S(1)}, u32[]{:S(2)}, u32[]{:S(2)}) collective-permute-start(bf16[144,512]{1,0:T(8,128)(2,1)S(1)} %slice.31), channel_id=1, source_target_pairs={{0,1},{1,0},{2,3},{3,2},{4,5},{5,4},{6,7},{7,6},{8,9},{9,8},{10,11... | collective-permute-start | bytes 442376 | tf_op jit(solution)/shard_map/ppermute | solution.py:245
  117.3 7.0 %collective-permute-start.22 = (bf16[144,512]{1,0:T(8,128)(2,1)S(1)}, bf16[144,512]{1,0:T(8,128)(2,1)S(1)}, u32[]{:S(2)}, u32[]{:S(2)}) collective-permute-start(bf16[144,512]{1,0:T(8,128)(2,1)S(1)} %slice.37), channel_id=1, source_target_pairs={{0,2},{1,3},{2,0},{3,1},{4,6},{5,7},{6,4},{7,5},{8,10},{9,11},{10,... | collective-permute-start | bytes 442376 | tf_op jit(solution)/shard_map/ppermute | solution.py:245
  119.0 8.9 %collective-permute-start.11 = (bf16[4,1,128,128]{3,2,1,0:T(8,128)(2,1)S(1)}, bf16[4,1,128,128]{3,2,1,0:T(8,128)(2,1)S(1)}, u32[]{:S(2)}, u32[]{:S(2)}) collective-permute-start(bf16[4,1,128,128]{3,2,1,0:T(8,128)(2,1)S(1)} %get-tuple-element.41), channel_id=1, source_target_pairs={{0,1},{1,0},{2,3},{3,2},{4,5},{5,4},{6,7},{7,6},{8,9},{9,8},{10,11... | collective-permute-start | bytes 393224 | tf_op jit(solution)/shard_map/ppermute | solution.py:245
  119.1 8.8 %collective-permute-start.12 = (bf16[4,1,128,128]{3,2,1,0:T(8,128)(2,1)S(1)}, bf16[4,1,128,128]{3,2,1,0:T(8,128)(2,1)S(1)}, u32[]{:S(2)}, u32[]{:S(2)}) collective-permute-start(bf16[4,1,128,128]{3,2,1,0:T(8,128)(2,1)S(1)} %get-tuple-element.40), channel_id=1, source_target_pairs={{0,2},{1,3},{2,0},{3,1},{4,6},{5,7},{6,4},{7,5},{8,10},{9,11},{10,... | collective-permute-start | bytes 393224 | tf_op jit(solution)/shard_map/ppermute | solution.py:245
  121.1 14.5 %collective-permute-start.13 = (bf16[4,1,128,128]{3,2,1,0:T(8,128)(2,1)S(1)}, bf16[4,1,128,128]{3,2,1,0:T(8,128)(2,1)S(1)}, u32[]{:S(2)}, u32[]{:S(2)}) collective-permute-start(bf16[4,1,128,128]{3,2,1,0:T(8,128)(2,1)S(1)} %get-tuple-element.39), channel_id=1, source_target_pairs={{0,3},{1,2},{2,1},{3,0},{4,7},{5,6},{6,5},{7,4},{8,11},{9,10},{10,... | collective-permute-start | bytes 393224 | tf_op jit(solution)/shard_map/ppermute | solution.py:245
  127.8 8.0 %collective-permute-start.23 = (f32[512,512]{1,0:T(8,128)S(1)}, f32[512,512]{1,0:T(8,128)S(1)}, u32[]{:S(2)}, u32[]{:S(2)}) collective-permute-start(f32[512,512]{1,0:T(8,128)S(1)} %get-tuple-element.33), channel_id=1, source_target_pairs={{0,16},{16,0},{1,17},{17,1},{2,18},{18,2},{3,19},{19,3},{4,20},{20... | collective-permute-start | bytes 3145736 | tf_op jit(solution)/shard_map/ppermute | solution.py:253
  137.6 0.8 copy-start
  138.4 23.4 %all-to-all-start.2 = ((bf16[16,128,128]{2,1,0:T(8,128)(2,1)}), bf16[16,128,128]{2,1,0:T(8,128)(2,1)S(1)}, u32[]{:S(2)}, u32[]{:S(2)}) async-start(bf16[16,128,128]{2,1,0:T(8,128)(2,1)} %bitcast.48), calls=%async_computation.2 | async-start | bytes 1048576 | tf_op jit(solution)/shard_map/all_to_all | solution.py:200
  153.7 0.8 copy-start.1

commit v8 on v7

--- a/solution.py
+++ b/solution.py
@@ -443,9 +443,7 @@
 
     part = heads // 2 * HEAD
     place = lax.axis_index("seq") & (QUAD - 1)
-    lines = pack(inputs, n, [(a, 0) for a in range(4)], part)
-    lines, embed = lax.optimization_barrier((lines, embed))
-    lines = spread_lines(lines)
+    lines = spread_lines(pack(inputs, n, [(a, 0) for a in range(4)], part))
     earlier = join(spread_planes(lines, place, 0, 3))
     cross_first = join(spread_planes(lines, place, 3, 1))
     rest = pack(inputs, n, [(a, 1) for a in range(4)], part)

time: 183 us -> 183 us (level)
  transfers between devices with their start and end apart: 27 -> 27, of which waited for: 13 -> 13; matrix products, arithmetic and copies ran while one was open for 3% -> 3% of each run, Pallas kernels for 14% -> 16%
where the time goes in v8:
time: 183 us; the launch traced here: 182 us
  waiting for transfers between devices  74 us (40%)
  starting transfers between devices  46.7 us (26%)
  Pallas kernels  30.4 us (17%)
  blocking collectives  18.4 us (10%)
  local copies, waits for them, and re-layouts  7.54 us (4%)
  between operations  3.56 us (2%)
    ppermute x21, waiting for transfers between devices, exchange(): return lax.ppermute(value, 'seq', [(i, i ^ apart) for i in range(n)])  56 us
    ppermute x21, starting transfers between devices, exchange(): return lax.ppermute(value, 'seq', [(i, i ^ apart) for i in range(n)])  26 us
    all_to_all x3, starting transfers between devices, spread(): lax.all_to_all(flat, 'seq', split_axis=0, concat_axis=0, tiled=True, axis...  19.9 us
    all_to_all x1, blocking collectives, spread(): lax.all_to_all(flat, 'seq', split_axis=0, concat_axis=0, tiled=True, axis...  18.4 us
    all_to_all x3, waiting for transfers between devices, spread(): lax.all_to_all(flat, 'seq', split_axis=0, concat_axis=0, tiled=True, axis...  17.2 us
    pallas_call x2, Pallas kernels, self_attention(): pl.pallas_call(body, grid_spec=pltpu.PrefetchScalarGridSpec(num_scalar_pr...  11.4 us
    pallas_call x2, Pallas kernels, pack(): pl.pallas_call(body, grid=(n // per,), in_specs=[block(j, g) for j in ran...  7.49 us
    unnamed x10, local copies, waits for them, and re-layouts  4.12 us
  transfers between devices with their start and end apart: 27, of which 13 were waited for; matrix products, arithmetic and copies ran while one was open for 3% of the time, Pallas kernels for 16%

profile of v8, /device:TPU:0, one launch (start us, length us, event | category | flops | bytes accessed | tf_op | source)
XLA Modules:
  0.0 181.9 jit_solution(6285218015314356090)
XLA Ops:
  0.0 0.5 collective-permute-start.1
  0.5 3.8 %pack.3 = bf16[16,4,128,128]{3,2,1,0:T(8,128)(2,1)} custom-call(bf16[128,4096]{1,0:T(8,128)(2,1)} %bitcast.53, bf16[128,4096]{1,0:T(8,128)(2,1)} %bitcast.61, bf16[128,4096]{1,0:T(8,128)(2,1)} %bitcast.69, bf16[128,4096]{1,0:T(8,128)(2,1)} %bitcast.77, bf16[128,4096]{1,0:T(8,128)(2,1)} %bitcast.54, bf16[128,4096]{1,0:T(8,128)(2,1)} %bitcast.62, ...), custom_call_target="tpu_custom_call" | custom-call | bytes 4194304 | tf_op jit(solution)/shard_map/pack/pallas_call | solution.py:38
  4.2 5.9 %all-to-all-start = ((bf16[16,512,128]{2,1,0:T(8,128)(2,1)}), bf16[16,512,128]{2,1,0:T(8,128)(2,1)}, u32[]{:S(2)}, u32[]{:S(2)}) async-start(bf16[16,512,128]{2,1,0:T(8,128)(2,1)} %bitcast.86), calls=%async_computation | async-start | bytes 4194304 | tf_op jit(solution)/shard_map/all_to_all | solution.py:200
  11.5 0.2 collective-permute-start
  11.7 0.9 collective-permute-done
  12.6 0.7 fusion.1
  13.9 2.9 %quarters.1 = (bf16[2,144,1024]{2,1,0:T(8,128)(2,1)S(1)}, bf16[2,144,1024]{2,1,0:T(8,128)(2,1)S(1)}, bf16[2,144,1024]{2,1,0:T(8,128)(2,1)S(1)}, bf16[2,144,1024]{2,1,0:T(8,128)(2,1)S(1)}) custom-call(s32[3]{0:T(128)S(1)} %pad_add_fusion.1.where_ref, bf16[512,4096]{1,0:T(8,128)(2,1)} %bitcast.88, bf16[512,4096]{1,0:T(8,128)(2,1)} %collective-permute-done.1.other_ref), custom_call_target="tpu_custom_call" | custom-call | bytes 4194304 | tf_op jit(solution)/shard_map/quarters/pallas_call | solution.py:287
  16.8 1.6 collective-permute-start.4
  19.8 1.6 collective-permute-start.2
  21.4 11.0 %collective-permute-done.4 = bf16[2,144,1024]{2,1,0:T(8,128)(2,1)S(1)} collective-permute-done((bf16[2,144,1024]{2,1,0:T(8,128)(2,1)S(1)}, bf16[2,144,1024]{2,1,0:T(8,128)(2,1)S(1)}, u32[]{:S(2)}, u32[]{:S(2)}) %collective-permute-start.4) | collective-permute-done | bytes 589856 | tf_op jit(solution)/shard_map/ppermute | solution.py:245
  32.4 0.1 broadcast_select_fusion
  32.5 1.6 collective-permute-start.5
  34.1 1.2 collective-permute-done.2
  35.3 0.1 broadcast_select_fusion.1
  35.5 0.4 collective-permute-start.3
  35.8 5.5 %collective-permute-done.5 = bf16[144,1024]{1,0:T(8,128)(2,1)S(1)} collective-permute-done((bf16[144,1024]{1,0:T(8,128)(2,1)S(1)}, bf16[144,1024]{1,0:T(8,128)(2,1)S(1)}, u32[]{:S(2)}, u32[]{:S(2)}) %collective-permute-start.5) | collective-permute-done | bytes 294944 | tf_op jit(solution)/shard_map/ppermute | solution.py:245
  41.4 0.1 bitcast_select_fusion
  41.5 1.9 %collective-permute-done.3 = bf16[144,1024]{1,0:T(8,128)(2,1)S(1)} collective-permute-done((bf16[144,1024]{1,0:T(8,128)(2,1)S(1)}, bf16[144,1024]{1,0:T(8,128)(2,1)S(1)}, u32[]{:S(2)}, u32[]{:S(2)}) %collective-permute-start.3) | collective-permute-done | bytes 294944 | tf_op jit(solution)/shard_map/ppermute | solution.py:245
  43.5 2.0 %collective-permute-start.6 = (bf16[144,2048]{1,0:T(8,128)(2,1)S(1)}, bf16[144,2048]{1,0:T(8,128)(2,1)S(1)}, u32[]{:S(2)}, u32[]{:S(2)}) collective-permute-start(bf16[144,2048]{1,0:T(8,128)(2,1)S(1)} %pad_maximum_fusion), channel_id=1, source_target_pairs={{0,4},{1,5},{2,6},{3,7},{4,0},{5,1},{6,2},{7,3},{8,12},{9,13},{10,... | collective-permute-start | bytes 1769480 | tf_op jit(solution)/shard_map/ppermute | solution.py:245
  45.6 3.7 %pack.2 = bf16[16,4,128,128]{3,2,1,0:T(8,128)(2,1)} custom-call(bf16[128,4096]{1,0:T(8,128)(2,1)} %bitcast.57, bf16[128,4096]{1,0:T(8,128)(2,1)} %bitcast.65, bf16[128,4096]{1,0:T(8,128)(2,1)} %bitcast.73, bf16[128,4096]{1,0:T(8,128)(2,1)} %bitcast.81, bf16[128,4096]{1,0:T(8,128)(2,1)} %bitcast.58, bf16[128,4096]{1,0:T(8,128)(2,1)} %bitcast.66, ...), custom_call_target="tpu_custom_call" | custom-call | bytes 4194304 | tf_op jit(solution)/shard_map/pack/pallas_call | solution.py:38
  49.4 9.8 %all-to-all-done = bf16[16,512,128]{2,1,0:T(8,128)(2,1)} async-done(((bf16[16,512,128]{2,1,0:T(8,128)(2,1)}), bf16[16,512,128]{2,1,0:T(8,128)(2,1)}, u32[]{:S(2)}, u32[]{:S(2)}) %all-to-all-start) | async-done | bytes 2097184 | tf_op jit(solution)/shard_map/all_to_all | solution.py:200
  59.2 1.5 dynamic-slice_bitcast_fusion
  60.7 1.6 collective-permute-start.8
  62.3 1.5 collective-permute-start.9
  63.8 0.5 collective-permute-start.10
  64.3 3.1 %collective-permute-done.6 = bf16[144,2048]{1,0:T(8,128)(2,1)S(1)} collective-permute-done((bf16[144,2048]{1,0:T(8,128)(2,1)S(1)}, bf16[144,2048]{1,0:T(8,128)(2,1)S(1)}, u32[]{:S(2)}, u32[]{:S(2)}) %collective-permute-start.6) | collective-permute-done | bytes 589856 | tf_op jit(solution)/shard_map/ppermute | solution.py:245
  67.4 0.2 broadcast_select_fusion.2
  67.6 2.4 %collective-permute-start.7 = (bf16[144,1024]{1,0:T(8,128)(2,1)S(1)}, bf16[144,1024]{1,0:T(8,128)(2,1)S(1)}, u32[]{:S(2)}, u32[]{:S(2)}) collective-permute-start(bf16[144,1024]{1,0:T(8,128)(2,1)S(1)} %slice_select_fusion), channel_id=1, source_target_pairs={{0,8},{1,9},{2,10},{3,11},{4,12},{5,13},{6,14},{7,15},{8,0},{9,1},... | collective-permute-start | bytes 884744 | tf_op jit(solution)/shard_map/ppermute | solution.py:245
  70.0 2.9 %collective-permute-done.8.refs_1_ = bf16[4,3,128,128]{3,2,1,0:T(8,128)(2,1)S(1)} collective-permute-done((bf16[4,3,128,128]{3,2,1,0:T(8,128)(2,1)S(1)}, bf16[4,3,128,128]{3,2,1,0:T(8,128)(2,1)S(1)}, u32[]{:S(2)}, u32[]{:S(2)}) %collective-permute-start.8) | collective-permute-done | bytes 393248 | tf_op jit(solution)/shard_map/ppermute | solution.py:245
  72.8 8.0 %collective-permute-done.9.refs_2_ = bf16[4,3,128,128]{3,2,1,0:T(8,128)(2,1)S(1)} collective-permute-done((bf16[4,3,128,128]{3,2,1,0:T(8,128)(2,1)S(1)}, bf16[4,3,128,128]{3,2,1,0:T(8,128)(2,1)S(1)}, u32[]{:S(2)}, u32[]{:S(2)}) %collective-permute-start.9) | collective-permute-done | bytes 393248 | tf_op jit(solution)/shard_map/ppermute | solution.py:245
  80.8 0.3 join.2
  81.1 1.1 copy-done.3
  82.2 0.1 broadcast_select_fusion.3.refs_0_
  82.3 0.5 collective-permute-start.18
  82.8 1.5 collective-permute-start.14
  84.3 0.2 collective-permute-start.15
  84.5 6.0 %all-to-all-start.1 = ((bf16[16,512,128]{2,1,0:T(8,128)(2,1)}), bf16[16,512,128]{2,1,0:T(8,128)(2,1)S(1)}, u32[]{:S(2)}, u32[]{:S(2)}) async-start(bf16[16,512,128]{2,1,0:T(8,128)(2,1)} %bitcast.85), calls=%async_computation.1 | async-start | bytes 4194304 | tf_op jit(solution)/shard_map/all_to_all | solution.py:200
  90.5 2.0 %collective-permute-start.19 = (bf16[144,1024]{1,0:T(8,128)(2,1)S(1)}, bf16[144,1024]{1,0:T(8,128)(2,1)S(1)}, u32[]{:S(2)}, u32[]{:S(2)}) collective-permute-start(bf16[144,1024]{1,0:T(8,128)(2,1)S(1)} %collective-permute-done.18.refs_5_), channel_id=1, source_target_pairs={{0,1},{1,0},{2,3},{3,2},{4,5},{5,4},{6,7},{7,6},{8,9},{9,8},{10,11... | collective-permute-start | bytes 884744 | tf_op jit(solution)/shard_map/ppermute | solution.py:245
  92.5 1.5 collective-permute-start.20
  94.0 1.4 copy-done.4
  95.4 5.7 %self_attention.2 = bf16[4,4,128,128]{3,2,1,0:T(8,128)(2,1)S(1)} custom-call(s32[1]{0:T(128)} %bitcast.3.place_ref, bf16[16,3,128,128]{3,2,1,0:T(8,128)(2,1)S(1)} %bitcast.49, bf16[16,3,128,128]{3,2,1,0:T(8,128)(2,1)S(1)} %bitcast.50, bf16[16,3,128,128]{3,2,1,0:T(8,128)(2,1)S(1)} %bitcast.51), custom_call_target="tpu_custom_call" | custom-call | flops 8589934592 | bytes 2097152 | tf_op jit(solution)/shard_map/self_attention/pallas_call | solution.py:110
  101.1 0.6 collective-permute-start.16
  101.8 0.2 collective-permute-start.17
  101.9 13.7 %collective-permute-done.20.refs_7_ = bf16[144,1024]{1,0:T(8,128)(2,1)S(1)} collective-permute-done((bf16[144,1024]{1,0:T(8,128)(2,1)S(1)}, bf16[144,1024]{1,0:T(8,128)(2,1)S(1)}, u32[]{:S(2)}, u32[]{:S(2)}) %collective-permute-start.20) | collective-permute-done | bytes 294944 | tf_op jit(solution)/shard_map/ppermute | solution.py:245
  115.7 1.6 collective-permute-start.21
  117.3 0.5 collective-permute-start.22
  117.9 1.1 dynamic-slice_bitcast_fusion.6
  119.0 0.1 collective-permute-start.11
  119.2 2.0 %collective-permute-start.12 = (bf16[4,1,128,128]{3,2,1,0:T(8,128)(2,1)S(1)}, bf16[4,1,128,128]{3,2,1,0:T(8,128)(2,1)S(1)}, u32[]{:S(2)}, u32[]{:S(2)}) collective-permute-start(bf16[4,1,128,128]{3,2,1,0:T(8,128)(2,1)S(1)} %get-tuple-element.36), channel_id=1, source_target_pairs={{0,2},{1,3},{2,0},{3,1},{4,6},{5,7},{6,4},{7,5},{8,10},{9,11},{10,... | collective-permute-start | bytes 393224 | tf_op jit(solution)/shard_map/ppermute | solution.py:245
  121.2 2.3 %collective-permute-start.13 = (bf16[4,1,128,128]{3,2,1,0:T(8,128)(2,1)S(1)}, bf16[4,1,128,128]{3,2,1,0:T(8,128)(2,1)S(1)}, u32[]{:S(2)}, u32[]{:S(2)}) collective-permute-start(bf16[4,1,128,128]{3,2,1,0:T(8,128)(2,1)S(1)} %get-tuple-element.35), channel_id=1, source_target_pairs={{0,3},{1,2},{2,1},{3,0},{4,7},{5,6},{6,5},{7,4},{8,11},{9,10},{10,... | collective-permute-start | bytes 393224 | tf_op jit(solution)/shard_map/ppermute | solution.py:245
  123.5 0.8 collective-permute-done.21.refs_8_
  124.3 3.5 %project.1 = (f32[512,512]{1,0:T(8,128)S(1)}, f32[512,512]{1,0:T(8,128)S(1)}) custom-call(s32[3]{0:T(128)S(1)} %pad_add_fusion.2.where_ref, bf16[144,1024]{1,0:T(8,128)(2,1)S(1)} %broadcast_select_fusion.3.refs_0_, bf16[144,1024]{1,0:T(8,128)(2,1)S(1)} %collective-permute-done.14.refs_1_, bf16[144,1024]{1,0:T(8,128)(2,1)S(1)} %collective-permute-done.15.refs_2_, ...), custom_call_target="tpu_custom_call" | custom-call | flops 16000000000 | bytes 8388608 | tf_op jit(solution)/shard_map/project/pallas_call | solution.py:344
  127.9 7.8 %collective-permute-done.13.refs_3_ = bf16[4,1,128,128]{3,2,1,0:T(8,128)(2,1)S(1)} collective-permute-done((bf16[4,1,128,128]{3,2,1,0:T(8,128)(2,1)S(1)}, bf16[4,1,128,128]{3,2,1,0:T(8,128)(2,1)S(1)}, u32[]{:S(2)}, u32[]{:S(2)}) %collective-permute-start.13) | collective-permute-done | bytes 131104 | tf_op jit(solution)/shard_map/ppermute | solution.py:245
  135.7 0.1 join.3
  135.9 0.3 add_convert_fusion.k_ref.v_ref
  136.1 1.6 cross_attention.2
  137.7 0.8 copy-done
  138.5 8.0 %all-to-all-start.2 = ((bf16[16,128,128]{2,1,0:T(8,128)(2,1)}), bf16[16,128,128]{2,1,0:T(8,128)(2,1)S(1)}, u32[]{:S(2)}, u32[]{:S(2)}) async-start(bf16[16,128,128]{2,1,0:T(8,128)(2,1)} %bitcast.48), calls=%async_computation.2 | async-start | bytes 1048576 | tf_op jit(solution)/shard_map/all_to_all | solution.py:200
  146.5 5.7 %self_attention.3.self_ref = bf16[16,128,128]{2,1,0:T(8,128)(2,1)S(1)} custom-call(s32[1]{0:T(128)} %constant.38.clone.1.place_ref, bf16[16,4,128,128]{3,2,1,0:T(8,128)(2,1)S(1)} %bitcast.44, bf16[16,4,128,128]{3,2,1,0:T(8,128)(2,1)S(1)} %bitcast.45, bf16[16,4,128,128]{3,2,1,0:T(8,128)(2,1)S(1)} %bitcast.46), custom_call_target="tpu_custom_call" | custom-call | flops 8589934592 | bytes 2097152 | tf_op jit(solution)/shard_map/self_attention/pallas_call | solution.py:110
  152.2 1.6 cross_attention.3
  153.8 0.8 copy-done.1
  154.5 7.3 %all-to-all-done.2.refs_0_ = bf16[16,128,128]{2,1,0:T(8,128)(2,1)S(1)} async-done(((bf16[16,128,128]{2,1,0:T(8,128)(2,1)}), bf16[16,128,128]{2,1,0:T(8,128)(2,1)S(1)}, u32[]{:S(2)}, u32[]{:S(2)}) %all-to-all-start.2) | async-done | bytes 524320 | tf_op jit(solution)/shard_map/all_to_all | solution.py:200
  161.9 18.4 %all_to_all.20.refs_1_ = bf16[16,128,128]{2,1,0:T(8,128)(2,1)S(1)} all-to-all(bf16[16,128,128]{2,1,0:T(8,128)(2,1)} %copy-done.1), channel_id=1, replica_groups=mesh['dp'=2,'seq'=16] {'seq'}, dimensions={0} | all-to-all | bytes 1048576 | tf_op jit(solution)/shard_map/all_to_all | solution.py:200
  180.3 1.6 unpack.1
  (37 shorter events, 0.7 us)
Async XLA Ops:
  0.0 13.9 %collective-permute-start.1 = (bf16[512,4096]{1,0:T(8,128)(2,1)}, bf16[512,4096]{1,0:T(8,128)(2,1)}, u32[]{:S(2)}, u32[]{:S(2)}) collective-permute-start(bf16[512,4096]{1,0:T(8,128)(2,1)} %bitcast.87), channel_id=1, source_target_pairs={{0,16},{16,0},{1,17},{17,1},{2,18},{18,2},{3,19},{19,3},{4,20},{20... | collective-permute-start | bytes 12582920 | tf_op jit(solution)/shard_map/ppermute | solution.py:253
  4.2 55.0 %all-to-all-start = ((bf16[16,512,128]{2,1,0:T(8,128)(2,1)}), bf16[16,512,128]{2,1,0:T(8,128)(2,1)}, u32[]{:S(2)}, u32[]{:S(2)}) async-start(bf16[16,512,128]{2,1,0:T(8,128)(2,1)} %bitcast.86), calls=%async_computation | async-start | bytes 4194304 | tf_op jit(solution)/shard_map/all_to_all | solution.py:200
  11.5 1.1 collective-permute-start
  16.8 15.5 %collective-permute-start.4 = (bf16[2,144,1024]{2,1,0:T(8,128)(2,1)S(1)}, bf16[2,144,1024]{2,1,0:T(8,128)(2,1)S(1)}, u32[]{:S(2)}, u32[]{:S(2)}) collective-permute-start(bf16[2,144,1024]{2,1,0:T(8,128)(2,1)S(1)} %get-tuple-element.23), channel_id=1, source_target_pairs={{0,2},{1,3},{2,0},{3,1},{4,6},{5,7},{6,4},{7,5},{8,10},{9,11},{10,... | collective-permute-start | bytes 1769480 | tf_op jit(solution)/shard_map/ppermute | solution.py:245
  19.8 15.5 %collective-permute-start.2 = (bf16[2,144,1024]{2,1,0:T(8,128)(2,1)S(1)}, bf16[2,144,1024]{2,1,0:T(8,128)(2,1)S(1)}, u32[]{:S(2)}, u32[]{:S(2)}) collective-permute-start(bf16[2,144,1024]{2,1,0:T(8,128)(2,1)S(1)} %get-tuple-element.21), channel_id=1, source_target_pairs={{0,1},{1,0},{2,3},{3,2},{4,5},{5,4},{6,7},{7,6},{8,9},{9,8},{10,11... | collective-permute-start | bytes 1769480 | tf_op jit(solution)/shard_map/ppermute | solution.py:245
  32.5 8.8 %collective-permute-start.5 = (bf16[144,1024]{1,0:T(8,128)(2,1)S(1)}, bf16[144,1024]{1,0:T(8,128)(2,1)S(1)}, u32[]{:S(2)}, u32[]{:S(2)}) collective-permute-start(bf16[144,1024]{1,0:T(8,128)(2,1)S(1)} %dynamic-slice_bitcast_fusion.4), channel_id=1, source_target_pairs={{0,1},{1,0},{2,3},{3,2},{4,5},{5,4},{6,7},{7,6},{8,9},{9,8},{10,11... | collective-permute-start | bytes 884744 | tf_op jit(solution)/shard_map/ppermute | solution.py:245
  35.5 7.9 %collective-permute-start.3 = (bf16[144,1024]{1,0:T(8,128)(2,1)S(1)}, bf16[144,1024]{1,0:T(8,128)(2,1)S(1)}, u32[]{:S(2)}, u32[]{:S(2)}) collective-permute-start(bf16[144,1024]{1,0:T(8,128)(2,1)S(1)} %dynamic-slice_bitcast_fusion.5), channel_id=1, source_target_pairs={{0,2},{1,3},{2,0},{3,1},{4,6},{5,7},{6,4},{7,5},{8,10},{9,11},{10,... | collective-permute-start | bytes 884744 | tf_op jit(solution)/shard_map/ppermute | solution.py:245
  43.5 23.8 %collective-permute-start.6 = (bf16[144,2048]{1,0:T(8,128)(2,1)S(1)}, bf16[144,2048]{1,0:T(8,128)(2,1)S(1)}, u32[]{:S(2)}, u32[]{:S(2)}) collective-permute-start(bf16[144,2048]{1,0:T(8,128)(2,1)S(1)} %pad_maximum_fusion), channel_id=1, source_target_pairs={{0,4},{1,5},{2,6},{3,7},{4,0},{5,1},{6,2},{7,3},{8,12},{9,13},{10,... | collective-permute-start | bytes 1769480 | tf_op jit(solution)/shard_map/ppermute | solution.py:245
  60.7 12.1 %collective-permute-start.8 = (bf16[4,3,128,128]{3,2,1,0:T(8,128)(2,1)S(1)}, bf16[4,3,128,128]{3,2,1,0:T(8,128)(2,1)S(1)}, u32[]{:S(2)}, u32[]{:S(2)}) collective-permute-start(bf16[4,3,128,128]{3,2,1,0:T(8,128)(2,1)S(1)} %get-tuple-element.41), channel_id=1, source_target_pairs={{0,1},{1,0},{2,3},{3,2},{4,5},{5,4},{6,7},{7,6},{8,9},{9,8},{10,11... | collective-permute-start | bytes 1179656 | tf_op jit(solution)/shard_map/ppermute | solution.py:245
  62.3 18.5 %collective-permute-start.9 = (bf16[4,3,128,128]{3,2,1,0:T(8,128)(2,1)S(1)}, bf16[4,3,128,128]{3,2,1,0:T(8,128)(2,1)S(1)}, u32[]{:S(2)}, u32[]{:S(2)}) collective-permute-start(bf16[4,3,128,128]{3,2,1,0:T(8,128)(2,1)S(1)} %get-tuple-element.40), channel_id=1, source_target_pairs={{0,2},{1,3},{2,0},{3,1},{4,6},{5,7},{6,4},{7,5},{8,10},{9,11},{10,... | collective-permute-start | bytes 1179656 | tf_op jit(solution)/shard_map/ppermute | solution.py:245
  63.8 17.0 %collective-permute-start.10 = (bf16[4,3,128,128]{3,2,1,0:T(8,128)(2,1)S(1)}, bf16[4,3,128,128]{3,2,1,0:T(8,128)(2,1)S(1)}, u32[]{:S(2)}, u32[]{:S(2)}) collective-permute-start(bf16[4,3,128,128]{3,2,1,0:T(8,128)(2,1)S(1)} %get-tuple-element.39), channel_id=1, source_target_pairs={{0,3},{1,2},{2,1},{3,0},{4,7},{5,6},{6,5},{7,4},{8,11},{9,10},{10,... | collective-permute-start | bytes 1179656 | tf_op jit(solution)/shard_map/ppermute | solution.py:245
  67.6 14.6 %collective-permute-start.7 = (bf16[144,1024]{1,0:T(8,128)(2,1)S(1)}, bf16[144,1024]{1,0:T(8,128)(2,1)S(1)}, u32[]{:S(2)}, u32[]{:S(2)}) collective-permute-start(bf16[144,1024]{1,0:T(8,128)(2,1)S(1)} %slice_select_fusion), channel_id=1, source_target_pairs={{0,8},{1,9},{2,10},{3,11},{4,12},{5,13},{6,14},{7,15},{8,0},{9,1},... | collective-permute-start | bytes 884744 | tf_op jit(solution)/shard_map/ppermute | solution.py:245
  81.1 1.1 copy-start.3
  82.3 8.2 %collective-permute-start.18 = (bf16[144,1024]{1,0:T(8,128)(2,1)S(1)}, bf16[144,1024]{1,0:T(8,128)(2,1)S(1)}, u32[]{:S(2)}, u32[]{:S(2)}) collective-permute-start(bf16[144,1024]{1,0:T(8,128)(2,1)S(1)} %broadcast_select_fusion.3.refs_0_), channel_id=1, source_target_pairs={{0,4},{1,5},{2,6},{3,7},{4,0},{5,1},{6,2},{7,3},{8,12},{9,13},{10,... | collective-permute-start | bytes 884744 | tf_op jit(solution)/shard_map/ppermute | solution.py:245
  82.8 19.0 %collective-permute-start.14 = (bf16[144,1024]{1,0:T(8,128)(2,1)S(1)}, bf16[144,1024]{1,0:T(8,128)(2,1)S(1)}, u32[]{:S(2)}, u32[]{:S(2)}) collective-permute-start(bf16[144,1024]{1,0:T(8,128)(2,1)S(1)} %broadcast_select_fusion.3.refs_0_), channel_id=1, source_target_pairs={{0,1},{1,0},{2,3},{3,2},{4,5},{5,4},{6,7},{7,6},{8,9},{9,8},{10,11... | collective-permute-start | bytes 884744 | tf_op jit(solution)/shard_map/ppermute | solution.py:245
  84.3 16.8 %collective-permute-start.15 = (bf16[144,1024]{1,0:T(8,128)(2,1)S(1)}, bf16[144,1024]{1,0:T(8,128)(2,1)S(1)}, u32[]{:S(2)}, u32[]{:S(2)}) collective-permute-start(bf16[144,1024]{1,0:T(8,128)(2,1)S(1)} %broadcast_select_fusion.3.refs_0_), channel_id=1, source_target_pairs={{0,2},{1,3},{2,0},{3,1},{4,6},{5,7},{6,4},{7,5},{8,10},{9,11},{10,... | collective-permute-start | bytes 884744 | tf_op jit(solution)/shard_map/ppermute | solution.py:245
  84.5 54.0 %all-to-all-start.1 = ((bf16[16,512,128]{2,1,0:T(8,128)(2,1)}), bf16[16,512,128]{2,1,0:T(8,128)(2,1)S(1)}, u32[]{:S(2)}, u32[]{:S(2)}) async-start(bf16[16,512,128]{2,1,0:T(8,128)(2,1)} %bitcast.85), calls=%async_computation.1 | async-start | bytes 4194304 | tf_op jit(solution)/shard_map/all_to_all | solution.py:200
  90.5 26.8 %collective-permute-start.19 = (bf16[144,1024]{1,0:T(8,128)(2,1)S(1)}, bf16[144,1024]{1,0:T(8,128)(2,1)S(1)}, u32[]{:S(2)}, u32[]{:S(2)}) collective-permute-start(bf16[144,1024]{1,0:T(8,128)(2,1)S(1)} %collective-permute-done.18.refs_5_), channel_id=1, source_target_pairs={{0,1},{1,0},{2,3},{3,2},{4,5},{5,4},{6,7},{7,6},{8,9},{9,8},{10,11... | collective-permute-start | bytes 884744 | tf_op jit(solution)/shard_map/ppermute | solution.py:245
  92.5 23.2 %collective-permute-start.20 = (bf16[144,1024]{1,0:T(8,128)(2,1)S(1)}, bf16[144,1024]{1,0:T(8,128)(2,1)S(1)}, u32[]{:S(2)}, u32[]{:S(2)}) collective-permute-start(bf16[144,1024]{1,0:T(8,128)(2,1)S(1)} %collective-permute-done.18.refs_5_), channel_id=1, source_target_pairs={{0,2},{1,3},{2,0},{3,1},{4,6},{5,7},{6,4},{7,5},{8,10},{9,11},{10,... | collective-permute-start | bytes 884744 | tf_op jit(solution)/shard_map/ppermute | solution.py:245
  94.0 1.4 copy-start.4
  101.1 23.2 %copy-start.2 = (bf16[2048,256]{1,0:T(8,128)(2,1)S(1)}, bf16[2048,256]{1,0:T(8,128)(2,1)}, u32[]{:S(2)}) copy-start(bf16[2048,256]{1,0:T(8,128)(2,1)} %refs_10_.1) | copy-start | bytes 3145732
  101.1 18.0 %collective-permute-start.16 = (bf16[144,512]{1,0:T(8,128)(2,1)S(1)}, bf16[144,512]{1,0:T(8,128)(2,1)S(1)}, u32[]{:S(2)}, u32[]{:S(2)}) collective-permute-start(bf16[144,512]{1,0:T(8,128)(2,1)S(1)} %slice.35), channel_id=1, source_target_pairs={{0,1},{1,0},{2,3},{3,2},{4,5},{5,4},{6,7},{7,6},{8,9},{9,8},{10,11... | collective-permute-start | bytes 442376 | tf_op jit(solution)/shard_map/ppermute | solution.py:245
  101.8 19.4 %collective-permute-start.17 = (bf16[144,512]{1,0:T(8,128)(2,1)S(1)}, bf16[144,512]{1,0:T(8,128)(2,1)S(1)}, u32[]{:S(2)}, u32[]{:S(2)}) collective-permute-start(bf16[144,512]{1,0:T(8,128)(2,1)S(1)} %slice.36), channel_id=1, source_target_pairs={{0,2},{1,3},{2,0},{3,1},{4,6},{5,7},{6,4},{7,5},{8,10},{9,11},{10,... | collective-permute-start | bytes 442376 | tf_op jit(solution)/shard_map/ppermute | solution.py:245
  115.7 8.6 %collective-permute-start.21 = (bf16[144,512]{1,0:T(8,128)(2,1)S(1)}, bf16[144,512]{1,0:T(8,128)(2,1)S(1)}, u32[]{:S(2)}, u32[]{:S(2)}) collective-permute-start(bf16[144,512]{1,0:T(8,128)(2,1)S(1)} %slice.31), channel_id=1, source_target_pairs={{0,1},{1,0},{2,3},{3,2},{4,5},{5,4},{6,7},{7,6},{8,9},{9,8},{10,11... | collective-permute-start | bytes 442376 | tf_op jit(solution)/shard_map/ppermute | solution.py:245
  117.3 7.0 %collective-permute-start.22 = (bf16[144,512]{1,0:T(8,128)(2,1)S(1)}, bf16[144,512]{1,0:T(8,128)(2,1)S(1)}, u32[]{:S(2)}, u32[]{:S(2)}) collective-permute-start(bf16[144,512]{1,0:T(8,128)(2,1)S(1)} %slice.37), channel_id=1, source_target_pairs={{0,2},{1,3},{2,0},{3,1},{4,6},{5,7},{6,4},{7,5},{8,10},{9,11},{10,... | collective-permute-start | bytes 442376 | tf_op jit(solution)/shard_map/ppermute | solution.py:245
  119.0 8.9 %collective-permute-start.11 = (bf16[4,1,128,128]{3,2,1,0:T(8,128)(2,1)S(1)}, bf16[4,1,128,128]{3,2,1,0:T(8,128)(2,1)S(1)}, u32[]{:S(2)}, u32[]{:S(2)}) collective-permute-start(bf16[4,1,128,128]{3,2,1,0:T(8,128)(2,1)S(1)} %get-tuple-element.37), channel_id=1, source_target_pairs={{0,1},{1,0},{2,3},{3,2},{4,5},{5,4},{6,7},{7,6},{8,9},{9,8},{10,11... | collective-permute-start | bytes 393224 | tf_op jit(solution)/shard_map/ppermute | solution.py:245
  119.2 8.7 %collective-permute-start.12 = (bf16[4,1,128,128]{3,2,1,0:T(8,128)(2,1)S(1)}, bf16[4,1,128,128]{3,2,1,0:T(8,128)(2,1)S(1)}, u32[]{:S(2)}, u32[]{:S(2)}) collective-permute-start(bf16[4,1,128,128]{3,2,1,0:T(8,128)(2,1)S(1)} %get-tuple-element.36), channel_id=1, source_target_pairs={{0,2},{1,3},{2,0},{3,1},{4,6},{5,7},{6,4},{7,5},{8,10},{9,11},{10,... | collective-permute-start | bytes 393224 | tf_op jit(solution)/shard_map/ppermute | solution.py:245
  121.2 14.5 %collective-permute-start.13 = (bf16[4,1,128,128]{3,2,1,0:T(8,128)(2,1)S(1)}, bf16[4,1,128,128]{3,2,1,0:T(8,128)(2,1)S(1)}, u32[]{:S(2)}, u32[]{:S(2)}) collective-permute-start(bf16[4,1,128,128]{3,2,1,0:T(8,128)(2,1)S(1)} %get-tuple-element.35), channel_id=1, source_target_pairs={{0,3},{1,2},{2,1},{3,0},{4,7},{5,6},{6,5},{7,4},{8,11},{9,10},{10,... | collective-permute-start | bytes 393224 | tf_op jit(solution)/shard_map/ppermute | solution.py:245
  127.8 8.0 %collective-permute-start.23 = (f32[512,512]{1,0:T(8,128)S(1)}, f32[512,512]{1,0:T(8,128)S(1)}, u32[]{:S(2)}, u32[]{:S(2)}) collective-permute-start(f32[512,512]{1,0:T(8,128)S(1)} %get-tuple-element.29), channel_id=1, source_target_pairs={{0,16},{16,0},{1,17},{17,1},{2,18},{18,2},{3,19},{19,3},{4,20},{20... | collective-permute-start | bytes 3145736 | tf_op jit(solution)/shard_map/ppermute | solution.py:253
  137.7 0.8 copy-start
  138.5 23.4 %all-to-all-start.2 = ((bf16[16,128,128]{2,1,0:T(8,128)(2,1)}), bf16[16,128,128]{2,1,0:T(8,128)(2,1)S(1)}, u32[]{:S(2)}, u32[]{:S(2)}) async-start(bf16[16,128,128]{2,1,0:T(8,128)(2,1)} %bitcast.48), calls=%async_computation.2 | async-start | bytes 1048576 | tf_op jit(solution)/shard_map/all_to_all | solution.py:200
  153.7 0.8 copy-start.1
